TPU v7x, 32 devices: a whole 2x2x4 slice. The times are simulated.
32 devices in a mesh: shard: 4 (over y, x), ctx: 4 (over z), tp: 2 (over core).
Axes of the slice: x: 2, y: 2, z: 4, core: 2. Of those that a mesh axis runs over, the one named last changes fastest.
Arguments:
- tokens: bfloat16 [8, 1056, 1536], P('shard', 'ctx'), may hold values from -6 to 6
- conditioning: bfloat16 [8, 130, 1536], P('shard')
- cotangent: bfloat16 [8, 1056, 1536], P('shard', 'ctx')
- piece_lengths: int32 [8, 4], P('shard'), may hold values from 192 to 257, as said below
- start_positions: int32 [8], P('shard'), may hold values from 0 to 2047
- cond_counts: int32 [8], P('shard'), may hold values from 65 to 130, as said below
- norm_gains: float32 [3, 1536], P(None, ('shard', 'ctx'))
- gains_moment: float32 [3, 1536], P(None, ('shard', 'ctx'))
- gains_square: float32 [3, 1536], P(None, ('shard', 'ctx'))
- qkv_weight: float32 [1536, 3, 1536], P(('shard', 'ctx'), None, 'tp')
- qkv_moment: float32 [1536, 3, 1536], P(('shard', 'ctx'), None, 'tp')
- qkv_square: float32 [1536, 3, 1536], P(('shard', 'ctx'), None, 'tp')
- output_weight: float32 [1536, 1536], P(('shard', 'ctx'), 'tp'), may hold values from -0.625 to 0.625
- output_moment: float32 [1536, 1536], P(('shard', 'ctx'), 'tp')
- output_square: float32 [1536, 1536], P(('shard', 'ctx'), 'tp')
- cross_query_weight: float32 [1536, 1536], P(('shard', 'ctx'), 'tp'), may hold values from -0.15625 to 0.15625
- cross_query_moment: float32 [1536, 1536], P(('shard', 'ctx'), 'tp')
- cross_query_square: float32 [1536, 1536], P(('shard', 'ctx'), 'tp')
- cross_pair_weight: float32 [1536, 2, 1536], P(('shard', 'ctx'), None, 'tp')
- cross_pair_moment: float32 [1536, 2, 1536], P(('shard', 'ctx'), None, 'tp')
- cross_pair_square: float32 [1536, 2, 1536], P(('shard', 'ctx'), None, 'tp')
- cross_out_weight: float32 [1536, 1536], P(('shard', 'ctx'), 'tp'), may hold values from -0.21875 to 0.21875
- cross_out_moment: float32 [1536, 1536], P(('shard', 'ctx'), 'tp')
- cross_out_square: float32 [1536, 1536], P(('shard', 'ctx'), 'tp')
- gate_up_weight: float32 [1536, 2, 6144], P(('shard', 'ctx'), None, 'tp')
- gate_up_moment: float32 [1536, 2, 6144], P(('shard', 'ctx'), None, 'tp')
- gate_up_square: float32 [1536, 2, 6144], P(('shard', 'ctx'), None, 'tp')
- down_weight: float32 [1536, 6144], P(('shard', 'ctx'), 'tp'), may hold values from -0.15625 to 0.15625
- down_moment: float32 [1536, 6144], P(('shard', 'ctx'), 'tp')
- down_square: float32 [1536, 6144], P(('shard', 'ctx'), 'tp')
Outputs:
- block_out: bfloat16 [8, 1056, 1536], P('shard', 'ctx')
- tokens_grad: float32 [8, 1056, 1536], P('shard', 'ctx')
- grad_norm: float32 [], replicated
- gains_moment_new: float32 [3, 1536], P(None, ('shard', 'ctx'))
- gains_square_new: float32 [3, 1536], P(None, ('shard', 'ctx'))
- gains_new: float32 [3, 1536], P(None, ('shard', 'ctx'))
- qkv_moment_new: float32 [1536, 3, 1536], P(('shard', 'ctx'), None, 'tp')
- qkv_square_new: float32 [1536, 3, 1536], P(('shard', 'ctx'), None, 'tp')
- qkv_new: float32 [1536, 3, 1536], P(('shard', 'ctx'), None, 'tp')
- output_moment_new: float32 [1536, 1536], P(('shard', 'ctx'), 'tp')
- output_square_new: float32 [1536, 1536], P(('shard', 'ctx'), 'tp')
- output_new: float32 [1536, 1536], P(('shard', 'ctx'), 'tp')
- cross_query_moment_new: float32 [1536, 1536], P(('shard', 'ctx'), 'tp')
- cross_query_square_new: float32 [1536, 1536], P(('shard', 'ctx'), 'tp')
- cross_query_new: float32 [1536, 1536], P(('shard', 'ctx'), 'tp')
- cross_pair_moment_new: float32 [1536, 2, 1536], P(('shard', 'ctx'), None, 'tp')
- cross_pair_square_new: float32 [1536, 2, 1536], P(('shard', 'ctx'), None, 'tp')
- cross_pair_new: float32 [1536, 2, 1536], P(('shard', 'ctx'), None, 'tp')
- cross_out_moment_new: float32 [1536, 1536], P(('shard', 'ctx'), 'tp')
- cross_out_square_new: float32 [1536, 1536], P(('shard', 'ctx'), 'tp')
- cross_out_new: float32 [1536, 1536], P(('shard', 'ctx'), 'tp')
- gate_up_moment_new: float32 [1536, 2, 6144], P(('shard', 'ctx'), None, 'tp')
- gate_up_square_new: float32 [1536, 2, 6144], P(('shard', 'ctx'), None, 'tp')
- gate_up_new: float32 [1536, 2, 6144], P(('shard', 'ctx'), None, 'tp')
- down_moment_new: float32 [1536, 6144], P(('shard', 'ctx'), 'tp')
- down_square_new: float32 [1536, 6144], P(('shard', 'ctx'), 'tp')
- down_new: float32 [1536, 6144], P(('shard', 'ctx'), 'tp')
Inputs may be any that keep to these rules, and one draw needn't show every extreme that they name: `piece_lengths`: in each latent one piece, drawn from the seed, holds 257 tokens and the others 256 - 256 // 4 to 256; in some latent all others hold 256. A latent attends to its first cond_counts conditioning tokens; some latent has all 130.
All inputs are finite; a program needn't handle non-finite values.
Results may differ from a plain program's by a relative error of at most 0.025.
Values may be sent and summed in bfloat16 or wider, within the bound.
No kernel may reach another device: no remote copies, remote signals or barrier semaphores. Data moves between devices by JAX's collectives and lax.ppermute only.
A program may use at most 320 MiB of HBM per device.

v0:
```python
import jax
import jax.numpy as jnp
from jax import lax
from jax.sharding import PartitionSpec as P

HD = 64
ROT = 32
STEP = 7


norm_eps = 1e-05
clip_norm = 1.0
beta_first = 0.9
beta_second = 0.999
learn_rate = 0.03
gain_rate = 0.75
weight_decay = 0.01
adam_eps = 1e-08
masked_score = -1e30


def frequencies(rotary):
    return 10000.0 ** (-jnp.arange(rotary // 2, dtype=jnp.float32) * 2.0 / rotary)


def rotate(heads, cosine, sine, rotary):
    half = rotary // 2
    first = heads[..., :half]
    second = heads[..., half:rotary]
    cosine = cosine[..., None, :]
    sine = sine[..., None, :]
    return jnp.concatenate(
        [first * cosine - second * sine, second * cosine + first * sine, heads[..., rotary:]],
        axis=-1,
    )


def layer_norm_parts(rows, gain):
    middle = jnp.mean(rows, axis=-1, keepdims=True)
    centred = rows - middle
    variance = jnp.mean(centred * centred, axis=-1, keepdims=True)
    inverse = lax.rsqrt(variance + norm_eps)
    plain = centred * inverse
    return (plain * gain, plain, inverse)


def norm_back(grad_out, plain, inverse, gain):
    scaled = grad_out * gain
    term_mean = jnp.mean(scaled, axis=-1, keepdims=True)
    term_along = jnp.mean(scaled * plain, axis=-1, keepdims=True)
    return (inverse * (scaled - term_mean - plain * term_along), jnp.sum(grad_out * plain, axis=0))


def contract_rows(left, right):
    return lax.dot_general(
        left, right, (((0,), (0,)), ((), ())), preferred_element_type=jnp.float32
    )


def times_transposed(left, right):
    return lax.dot_general(
        left, right, (((1,), (1,)), ((), ())), preferred_element_type=jnp.float32
    )


def tensor_total(partial_value):
    return lax.psum(partial_value.astype(jnp.bfloat16), "tp").astype(jnp.float32)


def input_total(partial_value):
    return lax.psum(partial_value.astype(jnp.bfloat16), "tp").astype(jnp.float32)


def adam_step(weight, moment, square, grad, scale, decay, rate):
    grad = grad * scale
    moment_new = beta_first * moment + (1.0 - beta_first) * grad
    square_new = beta_second * square + (1.0 - beta_second) * grad * grad
    moment_hat = moment_new / (1.0 - beta_first**STEP)
    square_hat = square_new / (1.0 - beta_second**STEP)
    weight_new = weight - rate * (moment_hat / (jnp.sqrt(square_hat) + adam_eps) + decay * weight)
    return (moment_new, square_new, weight_new)


def local(
    tokens,
    conditioning,
    cotangent,
    piece_lengths,
    start_positions,
    cond_counts,
    norm_gains,
    gains_moment,
    gains_square,
    qkv_weight,
    qkv_moment,
    qkv_square,
    output_weight,
    output_moment,
    output_square,
    cross_query_weight,
    cross_query_moment,
    cross_query_square,
    cross_pair_weight,
    cross_pair_moment,
    cross_pair_square,
    cross_out_weight,
    cross_out_moment,
    cross_out_square,
    gate_up_weight,
    gate_up_moment,
    gate_up_square,
    down_weight,
    down_moment,
    down_square,
):
    seqs, cap, width = tokens.shape
    rows = seqs * cap
    cond_len = conditioning.shape[1]
    pieces = piece_lengths.shape[1]
    scale = HD ** (-0.5)
    bf = jnp.bfloat16
    fl = jnp.float32
    ctx_index = lax.axis_index("ctx")
    offsets = jnp.cumsum(piece_lengths, axis=1) - piece_lengths
    own_length = lax.dynamic_slice_in_dim(piece_lengths, ctx_index, 1, 1)
    own_offset = lax.dynamic_slice_in_dim(offsets, ctx_index, 1, 1)
    slot = jnp.arange(cap, dtype=jnp.int32)
    positions = start_positions[:, None] + own_offset + slot[None, :]
    valid = (slot[None, :] < own_length).astype(fl).reshape(rows, 1)
    angles = positions.astype(fl).reshape(rows, 1) * frequencies(ROT)[None, :]
    cosine = jnp.cos(angles)
    sine = jnp.sin(angles)
    key_valid = (slot[None, None, :] < piece_lengths[:, :, None]).reshape(seqs, pieces * cap)
    sent_qkv = qkv_weight.astype(bf)
    sent_output = output_weight.astype(bf)
    sent_query = cross_query_weight.astype(bf)
    sent_pair = cross_pair_weight.astype(bf)
    sent_cross = cross_out_weight.astype(bf)
    sent_gate_up = gate_up_weight.astype(bf)
    sent_down = down_weight.astype(bf)
    sent_gains = jnp.transpose(norm_gains).astype(bf)
    (
        qkv_full,
        output_full,
        query_full,
        pair_full,
        cross_full,
        gate_up_full,
        down_full,
        gains_full,
    ) = (
        lax.all_gather(sent_qkv, ("shard", "ctx"), axis=0, tiled=True),
        lax.all_gather(sent_output, ("shard", "ctx"), axis=0, tiled=True),
        lax.all_gather(sent_query, ("shard", "ctx"), axis=0, tiled=True),
        lax.all_gather(sent_pair, ("shard", "ctx"), axis=0, tiled=True),
        lax.all_gather(sent_cross, ("shard", "ctx"), axis=0, tiled=True),
        lax.all_gather(sent_gate_up, ("shard", "ctx"), axis=0, tiled=True),
        lax.all_gather(sent_down, ("shard", "ctx"), axis=0, tiled=True),
        lax.all_gather(sent_gains, ("shard", "ctx"), axis=0, tiled=True),
    )
    gains = jnp.transpose(gains_full.astype(fl))
    local_width = qkv_full.shape[2]
    heads_local = local_width // HD
    x_rows = tokens.reshape(rows, width).astype(fl)
    normed1, plain1, inverse1 = layer_norm_parts(x_rows, gains[0])
    input1 = normed1.astype(bf)
    projected = jnp.dot(input1, qkv_full.reshape(width, -1), preferred_element_type=fl).reshape(
        rows, 3, heads_local, HD
    )
    queries = (
        rotate(projected[:, 0], cosine, sine, ROT).astype(bf).reshape(seqs, cap, heads_local, HD)
    )
    keys = rotate(projected[:, 1], cosine, sine, ROT).astype(bf).reshape(seqs, cap, heads_local, HD)
    values = projected[:, 2].astype(bf).reshape(seqs, cap, heads_local, HD)
    peak_run = jnp.full((seqs, heads_local, cap), masked_score, fl)
    piece_keys = lax.all_gather(keys[None], "ctx", axis=0, tiled=True)
    piece_values = lax.all_gather(values[None], "ctx", axis=0, tiled=True)
    mask = slot[None, None, :] < piece_lengths[:, :, None]
    scores = jnp.einsum("sqhd,nskhd->shqnk", queries, piece_keys, preferred_element_type=fl) * scale
    scores = jnp.where(mask[:, None, None], scores, masked_score)
    peak_new = jnp.maximum(peak_run, jnp.max(scores, axis=(3, 4)))
    weights = jnp.exp(scores - peak_new[..., None, None])
    total_new = jnp.sum(weights, axis=(3, 4))
    update = jnp.einsum(
        "shqnk,nskhd->sqhd", weights.astype(bf), piece_values, preferred_element_type=fl
    )
    mixed = update / jnp.transpose(total_new, (0, 2, 1))[..., None]
    peak_all = jnp.transpose(peak_new, (1, 0, 2))
    total_all = jnp.transpose(total_new, (1, 0, 2))
    mixed_low = mixed.reshape(rows, local_width).astype(bf)
    x_first = x_rows + tensor_total(times_transposed(mixed_low, output_full))
    normed2, plain2, inverse2 = layer_norm_parts(x_first, gains[1])
    input2 = normed2.astype(bf)
    cross_queries = (
        jnp.dot(input2, query_full, preferred_element_type=fl)
        .astype(bf)
        .reshape(seqs, cap, heads_local, HD)
    )
    cond_rows = conditioning.reshape(seqs * cond_len, width)
    pairs = jnp.dot(cond_rows, pair_full.reshape(width, -1), preferred_element_type=fl).reshape(
        seqs, cond_len, 2, heads_local, HD
    )
    cross_keys = pairs[:, :, 0].astype(bf)
    cross_values = pairs[:, :, 1].astype(bf)
    cond_valid = jnp.arange(cond_len, dtype=jnp.int32)[None, :] < cond_counts[:, None]
    cross_scores = (
        jnp.einsum("sqhd,skhd->shqk", cross_queries, cross_keys, preferred_element_type=fl) * scale
    )
    cross_scores = jnp.where(cond_valid[:, None, None, :], cross_scores, masked_score)
    cross_peak = jnp.max(cross_scores, axis=-1, keepdims=True)
    cross_exp = jnp.exp(cross_scores - cross_peak)
    cross_total = jnp.sum(cross_exp, axis=-1)
    cross_mixed = (
        jnp.einsum("shqk,skhd->sqhd", cross_exp.astype(bf), cross_values, preferred_element_type=fl)
        / jnp.transpose(cross_total, (0, 2, 1))[..., None]
    )
    cross_low = cross_mixed.reshape(rows, local_width).astype(bf)
    x_second = x_first + tensor_total(times_transposed(cross_low, cross_full))
    normed3, plain3, inverse3 = layer_norm_parts(x_second, gains[2])
    input3 = normed3.astype(bf)
    gated = jnp.dot(input3, gate_up_full.reshape(width, -1), preferred_element_type=fl).reshape(
        rows, 2, -1
    )
    gate = gated[:, 0]
    upward = gated[:, 1]
    activated = jax.nn.silu(gate)
    hidden = (activated * upward).astype(bf)
    result = x_second + tensor_total(times_transposed(hidden, down_full))
    block_out = result.reshape(seqs, cap, width).astype(bf)
    qkv_back, output_back, query_back, pair_back, cross_back, gate_up_back, down_back = (
        lax.all_gather(sent_qkv, ("shard", "ctx"), axis=0, tiled=True),
        lax.all_gather(sent_output, ("shard", "ctx"), axis=0, tiled=True),
        lax.all_gather(sent_query, ("shard", "ctx"), axis=0, tiled=True),
        lax.all_gather(sent_pair, ("shard", "ctx"), axis=0, tiled=True),
        lax.all_gather(sent_cross, ("shard", "ctx"), axis=0, tiled=True),
        lax.all_gather(sent_gate_up, ("shard", "ctx"), axis=0, tiled=True),
        lax.all_gather(sent_down, ("shard", "ctx"), axis=0, tiled=True),
    )
    grad_rows = cotangent.reshape(rows, width).astype(fl) * valid
    grad_low = grad_rows.astype(bf)
    grad_down = contract_rows(grad_low, hidden)
    grad_hidden = jnp.dot(grad_low, down_back, preferred_element_type=fl)
    sigmoid = jax.nn.sigmoid(gate)
    grad_gate = grad_hidden * upward * sigmoid * (1.0 + gate * (1.0 - sigmoid))
    grad_up = grad_hidden * activated
    grad_gated = jnp.stack([grad_gate, grad_up], axis=1).astype(bf).reshape(rows, -1)
    grad_gate_up = contract_rows(input3, grad_gated).reshape(width, 2, -1)
    back3, grad_gain3 = norm_back(
        input_total(times_transposed(grad_gated, gate_up_back.reshape(width, -1))),
        plain3,
        inverse3,
        gains[2],
    )
    grad_second = grad_rows + back3
    grad2_low = grad_second.astype(bf)
    grad_cross = contract_rows(grad2_low, cross_low)
    grad_cmixed = (
        jnp.dot(grad2_low, cross_back, preferred_element_type=fl)
        .astype(bf)
        .reshape(seqs, cap, heads_local, HD)
    )
    cross_delta = jnp.transpose(jnp.sum(grad_cmixed.astype(fl) * cross_mixed, axis=-1), (0, 2, 1))
    cross_probs = cross_exp / cross_total[..., None]
    cross_dprob = jnp.einsum(
        "sqhd,skhd->shqk", grad_cmixed, cross_values, preferred_element_type=fl
    )
    cross_dscore = (cross_probs * (cross_dprob - cross_delta[..., None])).astype(bf)
    grad_cq = (
        (jnp.einsum("shqk,skhd->sqhd", cross_dscore, cross_keys, preferred_element_type=fl) * scale)
        .astype(bf)
        .reshape(rows, local_width)
    )
    grad_ckeys = (
        jnp.einsum("shqk,sqhd->skhd", cross_dscore, cross_queries, preferred_element_type=fl)
        * scale
    )
    grad_cvalues = jnp.einsum(
        "shqk,sqhd->skhd", cross_probs.astype(bf), grad_cmixed, preferred_element_type=fl
    )
    grad_pairs_low = (
        jnp.stack([grad_ckeys, grad_cvalues], axis=2).astype(bf).reshape(seqs * cond_len, -1)
    )
    grad_pair = contract_rows(cond_rows, grad_pairs_low).reshape(width, 2, -1)
    grad_query = contract_rows(input2, grad_cq)
    back2, grad_gain2 = norm_back(
        input_total(times_transposed(grad_cq, query_back)), plain2, inverse2, gains[1]
    )
    grad_first = grad_second + back2
    grad1_low = grad_first.astype(bf)
    grad_output = contract_rows(grad1_low, mixed_low)
    grad_mixed = (
        jnp.dot(grad1_low, output_back, preferred_element_type=fl)
        .astype(bf)
        .reshape(seqs, cap, heads_local, HD)
    )
    delta = jnp.sum(grad_mixed.astype(fl) * mixed, axis=-1)
    back_keys, back_values = (
        lax.all_gather(keys[None], "ctx", axis=0, tiled=True),
        lax.all_gather(values[None], "ctx", axis=0, tiled=True),
    )
    keys_by_head = jnp.transpose(back_keys, (3, 1, 0, 2, 4)).reshape(
        heads_local, seqs, pieces * cap, HD
    )
    values_by_head = jnp.transpose(back_values, (3, 1, 0, 2, 4)).reshape(
        heads_local, seqs, pieces * cap, HD
    )

    def head_back(items):
        query_head, key_head, value_head, grad_head, peak_head, total_head, delta_head = items
        scores = jnp.einsum("sqd,skd->sqk", query_head, key_head, preferred_element_type=fl) * scale
        scores = jnp.where(key_valid[:, None, :], scores, masked_score)
        probs = jnp.exp(scores - peak_head[..., None]) / total_head[..., None]
        grad_prob = jnp.einsum("sqd,skd->sqk", grad_head, value_head, preferred_element_type=fl)
        grad_score = (probs * (grad_prob - delta_head[..., None])).astype(bf)
        grad_query_head = (
            jnp.einsum("sqk,skd->sqd", grad_score, key_head, preferred_element_type=fl) * scale
        )
        grad_key_head = (
            jnp.einsum("sqk,sqd->skd", grad_score, query_head, preferred_element_type=fl) * scale
        )
        grad_value_head = jnp.einsum(
            "sqk,sqd->skd", probs.astype(bf), grad_head, preferred_element_type=fl
        )
        return (grad_query_head, grad_key_head, grad_value_head)

    grad_q_heads, grad_k_heads, grad_v_heads = lax.map(
        head_back,
        (
            jnp.transpose(queries, (2, 0, 1, 3)),
            keys_by_head,
            values_by_head,
            jnp.transpose(grad_mixed, (2, 0, 1, 3)),
            peak_all,
            total_all,
            jnp.transpose(delta, (2, 0, 1)),
        ),
    )
    key_terms = jnp.stack([grad_k_heads, grad_v_heads], axis=0).reshape(
        2, heads_local, seqs, pieces, cap, HD
    )
    key_terms = jnp.transpose(key_terms, (3, 2, 4, 0, 1, 5))
    own_terms = lax.psum_scatter(
        key_terms.astype(jnp.bfloat16), "ctx", scatter_dimension=0, tiled=True
    ).astype(jnp.float32)[0]
    grad_queries = jnp.transpose(grad_q_heads, (1, 2, 0, 3)).reshape(rows, heads_local, HD)
    grad_keys_own = own_terms[:, :, 0].reshape(rows, heads_local, HD)
    grad_values_own = own_terms[:, :, 1].reshape(rows, heads_local, HD)
    grad_projected = (
        jnp.stack(
            [
                rotate(grad_queries, cosine, -sine, ROT),
                rotate(grad_keys_own, cosine, -sine, ROT),
                grad_values_own,
            ],
            axis=1,
        )
        .astype(bf)
        .reshape(rows, -1)
    )
    grad_qkv = contract_rows(input1, grad_projected).reshape(width, 3, -1)
    back1, grad_gain1 = norm_back(
        input_total(times_transposed(grad_projected, qkv_back.reshape(width, -1))),
        plain1,
        inverse1,
        gains[0],
    )
    tokens_grad = (grad_first + back1).reshape(seqs, cap, width)
    gains_grad_rows = jnp.stack([grad_gain1, grad_gain2, grad_gain3], axis=1)
    own_qkv, own_output, own_query, own_pair, own_cross, own_gate_up, own_down, own_gains = (
        lax.psum_scatter(grad_qkv, ("shard", "ctx"), scatter_dimension=0, tiled=True),
        lax.psum_scatter(grad_output, ("shard", "ctx"), scatter_dimension=0, tiled=True),
        lax.psum_scatter(grad_query, ("shard", "ctx"), scatter_dimension=0, tiled=True),
        lax.psum_scatter(grad_pair, ("shard", "ctx"), scatter_dimension=0, tiled=True),
        lax.psum_scatter(grad_cross, ("shard", "ctx"), scatter_dimension=0, tiled=True),
        lax.psum_scatter(grad_gate_up, ("shard", "ctx"), scatter_dimension=0, tiled=True),
        lax.psum_scatter(grad_down, ("shard", "ctx"), scatter_dimension=0, tiled=True),
        lax.psum_scatter(gains_grad_rows, ("shard", "ctx"), scatter_dimension=0, tiled=True),
    )
    own_gains = jnp.transpose(own_gains)
    squares = (
        jnp.sum(own_qkv * own_qkv)
        + jnp.sum(own_output * own_output)
        + jnp.sum(own_query * own_query)
    )
    squares = squares + jnp.sum(own_pair * own_pair) + jnp.sum(own_cross * own_cross)
    squares = squares + jnp.sum(own_gate_up * own_gate_up) + jnp.sum(own_down * own_down)
    squares = squares + jnp.sum(own_gains * own_gains) / float(lax.axis_size("tp"))
    total_square = lax.psum(squares, ("shard", "ctx", "tp"))
    grad_norm = jnp.sqrt(total_square)
    clip_scale = clip_norm / jnp.maximum(grad_norm, clip_norm)
    gains_m, gains_v, gains_w = adam_step(
        norm_gains, gains_moment, gains_square, own_gains, clip_scale, 0.0, gain_rate
    )
    qkv_m, qkv_v, qkv_w = adam_step(
        qkv_weight, qkv_moment, qkv_square, own_qkv, clip_scale, weight_decay, learn_rate
    )
    output_m, output_v, output_w = adam_step(
        output_weight,
        output_moment,
        output_square,
        own_output,
        clip_scale,
        weight_decay,
        learn_rate,
    )
    query_m, query_v, query_w = adam_step(
        cross_query_weight,
        cross_query_moment,
        cross_query_square,
        own_query,
        clip_scale,
        weight_decay,
        learn_rate,
    )
    pair_m, pair_v, pair_w = adam_step(
        cross_pair_weight,
        cross_pair_moment,
        cross_pair_square,
        own_pair,
        clip_scale,
        weight_decay,
        learn_rate,
    )
    cross_m, cross_v, cross_w = adam_step(
        cross_out_weight,
        cross_out_moment,
        cross_out_square,
        own_cross,
        clip_scale,
        weight_decay,
        learn_rate,
    )
    gate_m, gate_v, gate_w = adam_step(
        gate_up_weight,
        gate_up_moment,
        gate_up_square,
        own_gate_up,
        clip_scale,
        weight_decay,
        learn_rate,
    )
    down_m, down_v, down_w = adam_step(
        down_weight, down_moment, down_square, own_down, clip_scale, weight_decay, learn_rate
    )
    return (
        block_out,
        tokens_grad,
        grad_norm,
        gains_m,
        gains_v,
        gains_w,
        qkv_m,
        qkv_v,
        qkv_w,
        output_m,
        output_v,
        output_w,
        query_m,
        query_v,
        query_w,
        pair_m,
        pair_v,
        pair_w,
        cross_m,
        cross_v,
        cross_w,
        gate_m,
        gate_v,
        gate_w,
        down_m,
        down_v,
        down_w,
    )


def solution(mesh):
    in_specs = (
        P("shard", "ctx", None),
        P("shard", None, None),
        P("shard", "ctx", None),
        P("shard", None),
        P("shard"),
        P("shard"),
        P(None, ("shard", "ctx")),
        P(None, ("shard", "ctx")),
        P(None, ("shard", "ctx")),
        P(("shard", "ctx"), None, "tp"),
        P(("shard", "ctx"), None, "tp"),
        P(("shard", "ctx"), None, "tp"),
        P(("shard", "ctx"), "tp"),
        P(("shard", "ctx"), "tp"),
        P(("shard", "ctx"), "tp"),
        P(("shard", "ctx"), "tp"),
        P(("shard", "ctx"), "tp"),
        P(("shard", "ctx"), "tp"),
        P(("shard", "ctx"), None, "tp"),
        P(("shard", "ctx"), None, "tp"),
        P(("shard", "ctx"), None, "tp"),
        P(("shard", "ctx"), "tp"),
        P(("shard", "ctx"), "tp"),
        P(("shard", "ctx"), "tp"),
        P(("shard", "ctx"), None, "tp"),
        P(("shard", "ctx"), None, "tp"),
        P(("shard", "ctx"), None, "tp"),
        P(("shard", "ctx"), "tp"),
        P(("shard", "ctx"), "tp"),
        P(("shard", "ctx"), "tp"),
    )
    out_specs = (
        P("shard", "ctx", None),
        P("shard", "ctx", None),
        P(),
        P(None, ("shard", "ctx")),
        P(None, ("shard", "ctx")),
        P(None, ("shard", "ctx")),
        P(("shard", "ctx"), None, "tp"),
        P(("shard", "ctx"), None, "tp"),
        P(("shard", "ctx"), None, "tp"),
        P(("shard", "ctx"), "tp"),
        P(("shard", "ctx"), "tp"),
        P(("shard", "ctx"), "tp"),
        P(("shard", "ctx"), "tp"),
        P(("shard", "ctx"), "tp"),
        P(("shard", "ctx"), "tp"),
        P(("shard", "ctx"), None, "tp"),
        P(("shard", "ctx"), None, "tp"),
        P(("shard", "ctx"), None, "tp"),
        P(("shard", "ctx"), "tp"),
        P(("shard", "ctx"), "tp"),
        P(("shard", "ctx"), "tp"),
        P(("shard", "ctx"), None, "tp"),
        P(("shard", "ctx"), None, "tp"),
        P(("shard", "ctx"), None, "tp"),
        P(("shard", "ctx"), "tp"),
        P(("shard", "ctx"), "tp"),
        P(("shard", "ctx"), "tp"),
    )
    return jax.shard_map(local, mesh=mesh, in_specs=in_specs, out_specs=out_specs, check_vma=False)
```

profile of v0, /device:TPU:0, one launch (start us, length us, event | category | flops | bytes accessed | tf_op | source)
XLA Modules:
  0.0 3515.1 jit_solution(10194456415398989564)
XLA Ops:
  11.7 42.6 %all-gather = bf16[16,96,3]{1,2,0:T(4,128)(2,1)S(1)} all-gather(bf16[1,96,3]{1,2,0:T(4,128)(2,1)S(1)} %convert_bitcast_fusion), channel_id=1, replica_groups=mesh['shard'=4,'ctx'=4,'tp'=2] {'shard','ctx'}, dimensions={0}, use_global_device_ids=true | all-gather | bytes 9792 | tf_op jit(solution)/shard_map/all_gather | solution.py:159
  58.3 57.3 %all-gather.11.cloned.1.call-done = bf16[1536,3,768]{2,0,1:T(8,128)(2,1)} async-done(((bf16[96,3,768]{2,0,1:T(8,128)(2,1)}), bf16[1536,3,768]{2,0,1:T(8,128)(2,1)}) %all-gather.11.cloned.1.call-update) | async-done | bytes 7077904 | tf_op jit(solution)/shard_map/all_gather | solution.py:152
  153.7 76.1 %all-gather.15.cloned.1.call-done = bf16[4,2,264,12,64]{2,4,0,3,1:T(8,128)(2,1)} async-done(((bf16[1,2,264,12,64]{2,4,0,3,1:T(8,128)(2,1)}), bf16[4,2,264,12,64]{2,4,0,3,1:T(8,128)(2,1)}) %all-gather.15.cloned.1.call-update) | async-done | bytes 3244048 | tf_op jit(solution)/shard_map/all_gather | solution.py:176
  229.8 19.9 fusion.28
  267.9 51.9 %all-gather.13.cloned.1.call-done = bf16[4,2,264,12,64]{2,4,0,3,1:T(8,128)(2,1)} async-done(((bf16[1,2,264,12,64]{2,4,0,3,1:T(8,128)(2,1)}), bf16[4,2,264,12,64]{2,4,0,3,1:T(8,128)(2,1)}) %all-gather.13.cloned.1.call-update) | async-done | bytes 3244048 | tf_op jit(solution)/shard_map/all_gather | solution.py:177
  341.7 42.0 %all-gather.17.cloned.1.call-done = bf16[1536,768]{1,0:T(8,128)(2,1)} async-done(((bf16[96,768]{1,0:T(8,128)(2,1)}), bf16[1536,768]{1,0:T(8,128)(2,1)}) %all-gather.17.cloned.1.call-update) | async-done | bytes 2359312 | tf_op jit(solution)/shard_map/all_gather | solution.py:153
  390.0 76.2 %all-gather.19.cloned.1.call-done = bf16[1536,2,768]{2,1,0:T(2,128)(2,1)} async-done(((bf16[96,2,768]{2,1,0:T(2,128)(2,1)}), bf16[1536,2,768]{2,1,0:T(2,128)(2,1)}) %all-gather.19.cloned.1.call-update) | async-done | bytes 4718608 | tf_op jit(solution)/shard_map/all_gather | solution.py:155
  492.6 62.7 %all-gather.21.cloned.1.call-done = bf16[1536,768]{1,0:T(8,128)(2,1)} async-done(((bf16[96,768]{1,0:T(8,128)(2,1)}), bf16[1536,768]{1,0:T(8,128)(2,1)}) %all-gather.21.cloned.1.call-update) | async-done | bytes 2359312 | tf_op jit(solution)/shard_map/all_gather | solution.py:154
  574.9 45.2 %all-gather.23.cloned.1.call-done = bf16[1536,768]{1,0:T(8,128)(2,1)} async-done(((bf16[96,768]{1,0:T(8,128)(2,1)}), bf16[1536,768]{1,0:T(8,128)(2,1)}) %all-gather.23.cloned.1.call-update) | async-done | bytes 2359312 | tf_op jit(solution)/shard_map/all_gather | solution.py:156
  647.5 212.7 %all-gather.25.cloned.1.call-done = bf16[1536,2,3072]{2,0,1:T(8,128)(2,1)} async-done(((bf16[96,2,3072]{2,0,1:T(8,128)(2,1)}), bf16[1536,2,3072]{2,0,1:T(8,128)(2,1)}) %all-gather.25.cloned.1.call-update) | async-done | bytes 18874384 | tf_op jit(solution)/shard_map/all_gather | solution.py:157
  860.2 24.7 copy.259
  901.8 82.4 %all-gather.27.cloned.1.call-done = bf16[1536,3072]{1,0:T(8,128)(2,1)} async-done(((bf16[96,3072]{1,0:T(8,128)(2,1)}), bf16[1536,3072]{1,0:T(8,128)(2,1)}) %all-gather.27.cloned.1.call-update) | async-done | bytes 9437200 | tf_op jit(solution)/shard_map/all_gather | solution.py:158
  1113.6 137.0 %while.15 = (s32[]{:T(128)}, f32[12,2,264,64]{2,3,1,0:T(8,128)}, bf16[12,2,1056,64]{2,3,1,0:T(8,128)(2,1)}, bf16[12,2,1056,64]{2,3,1,0:T(8,128)(2,1)}, bf16[12,2...) while((s32[]{:T(128)}, f32[12,2,264,64]{2,3,1,0:T(8,128)}, ...), condition=%wide.region_23.24_spmd.clone, body=%wide.region_22.23_spmd.clone.sunk | while | flops 361475136 | bytes 12808553 | solution.py:326
  1311.7 140.8 %reduce-scatter.11.cloned.1.call-done = bf16[1,2,264,2,12,64]{2,5,4,3,1,0:T(8,128)(2,1)} async-done(((bf16[4,2,264,2,12,64]{2,5,4,3,1,0:T(8,128)(2,1)}), bf16[1,2,264,2,12,64]{2,5,4,3,1,0:T(8,128)(2,1)}) %reduce-scatter.11.cloned.1.call-update) | async-done | bytes 1622032 | tf_op jit(solution)/shard_map/reduce_scatter | solution.py:342
  1590.3 23.3 fusion.36
  1615.5 196.0 %all-reduce.17.cloned.1.call-done = f32[1536,2,768]{2,1,0:T(2,128)} async-done(((f32[1536,2,768]{2,1,0:T(2,128)}), f32[1536,2,768]{2,1,0:T(2,128)}) %all-reduce.17.cloned.1.call-update) | async-done | bytes 9437200
  1813.7 139.2 %reduce-scatter.17.cloned.1.call-done = f32[96,768]{1,0:T(8,128)} async-done(((f32[1536,768]{1,0:T(8,128)}), f32[96,768]{1,0:T(8,128)}) %reduce-scatter.17.cloned.1.call-update) | async-done | bytes 294928 | tf_op jit(solution)/shard_map/reduce_scatter | solution.py:372
  1954.6 140.7 %reduce-scatter.19.cloned.1.call-done = f32[96,768]{1,0:T(8,128)} async-done(((f32[1536,768]{1,0:T(8,128)}), f32[96,768]{1,0:T(8,128)}) %reduce-scatter.19.cloned.1.call-update) | async-done | bytes 294928 | tf_op jit(solution)/shard_map/reduce_scatter | solution.py:374
  2096.9 139.9 %reduce-scatter.15.cloned.1.call-done = f32[96,768]{1,0:T(8,128)} async-done(((f32[1536,768]{1,0:T(8,128)}), f32[96,768]{1,0:T(8,128)}) %reduce-scatter.15.cloned.1.call-update) | async-done | bytes 294928 | tf_op jit(solution)/shard_map/reduce_scatter | solution.py:371
  2244.1 119.7 %reduce-scatter.25.cloned.1.call-done = f32[96,3]{1,0:T(8,128)} async-done(((f32[1536,3]{1,0:T(8,128)}), f32[96,3]{1,0:T(8,128)}) %reduce-scatter.25.cloned.1.call-update) | async-done | bytes 1168
  2366.0 288.3 %reduce-scatter.23.cloned.1.call-done = f32[96,3072]{1,0:T(8,128)} async-done(((f32[1536,3072]{1,0:T(8,128)}), f32[96,3072]{1,0:T(8,128)}) %reduce-scatter.23.cloned.1.call-update) | async-done | bytes 1179664 | tf_op jit(solution)/shard_map/reduce_scatter | solution.py:376
  2656.5 224.2 %reduce-scatter.13.cloned.1.call-done = f32[96,3,768]{2,0,1:T(8,128)} async-done(((f32[1536,3,768]{2,0,1:T(8,128)}), f32[96,3,768]{2,0,1:T(8,128)}) %reduce-scatter.13.cloned.1.call-update) | async-done | bytes 884752 | tf_op jit(solution)/shard_map/reduce_scatter | solution.py:370
  2885.9 543.9 %reduce-scatter.21.cloned.1.call-done = f32[96,2,3072]{2,0,1:T(8,128)} async-done(((f32[1536,2,3072]{2,0,1:T(8,128)}), f32[96,2,3072]{2,0,1:T(8,128)}) %reduce-scatter.21.cloned.1.call-update) | async-done | bytes 2359312 | tf_op jit(solution)/shard_map/reduce_scatter | solution.py:375
  3437.0 39.5 %psum.55 = f32[]{:T(128)} all-reduce(f32[]{:T(128)S(6)} %add.292), channel_id=1, replica_groups=mesh['shard'=4,'ctx'=4,'tp'=2] {'shard','ctx','tp'}, use_global_device_ids=true, to_apply=%region_47.48 | all-reduce | flops 1 | bytes 8 | tf_op jit(solution)/shard_map/psum | solution.py:388
  (577 shorter events, 702.0 us)
Async XLA Ops:
  7.2 108.4 %all-gather.11.cloned.1.call-start = ((), (), s32[]{:S(2)}) async-start(), calls=%async_computation.8 | async-start | bytes 7520256 | tf_op jit(solution)/shard_map/all_gather | solution.py:152
  9.4 220.4 %all-gather.15.cloned.1.call-start = ((), (), s32[]{:S(2)}) async-start(), calls=%async_computation.10 | async-start | bytes 5898240 | tf_op jit(solution)/shard_map/all_gather | solution.py:176
  54.6 983.1 %copy-start.61 = (f32[1536]{0:T(1024)}, f32[1536]{0:T(1024)S(1)}, u32[]{:S(2)}) copy-start(f32[1536]{0:T(1024)S(1)} %get-tuple-element.325) | copy-start | bytes 18436
  142.1 177.7 %all-gather.13.cloned.1.call-start = ((), (), s32[]{:S(2)}) async-start(), calls=%async_computation.9 | async-start | bytes 5898240 | tf_op jit(solution)/shard_map/all_gather | solution.py:177
  149.1 234.6 %all-gather.17.cloned.1.call-start = ((), (), s32[]{:S(2)}) async-start(), calls=%async_computation.11 | async-start | bytes 2506752 | tf_op jit(solution)/shard_map/all_gather | solution.py:153
  149.9 316.3 %all-gather.19.cloned.1.call-start = ((), (), s32[]{:S(2)}) async-start(), calls=%async_computation.13 | async-start | bytes 5013504 | tf_op jit(solution)/shard_map/all_gather | solution.py:155
  152.0 336.1 %all-reduce.9.cloned.1.call-start = ((), (), s32[]{:S(2)}) async-start(), calls=%async_computation.12 | async-start | bytes 3244032 | tf_op jit(solution)/shard_map/psum | solution.py:67
  388.3 166.9 %all-gather.21.cloned.1.call-start = ((), (), s32[]{:S(2)}) async-start(), calls=%async_computation.14 | async-start | bytes 2506752 | tf_op jit(solution)/shard_map/all_gather | solution.py:154
  389.1 231.0 %all-gather.23.cloned.1.call-start = ((), (), s32[]{:S(2)}) async-start(), calls=%async_computation.15 | async-start | bytes 2506752 | tf_op jit(solution)/shard_map/all_gather | solution.py:156
  389.9 254.3 %all-reduce.11.cloned.1.call-start = ((), (), s32[]{:S(2)}) async-start(), calls=%async_computation.16 | async-start | bytes 3244032 | tf_op jit(solution)/shard_map/psum | solution.py:67
  624.7 235.4 %all-gather.25.cloned.1.call-start = ((), (), s32[]{:S(2)}) async-start(), calls=%async_computation.17 | async-start | bytes 20054016 | tf_op jit(solution)/shard_map/all_gather | solution.py:157
  628.3 355.9 %all-gather.27.cloned.1.call-start = ((), (), s32[]{:S(2)}) async-start(), calls=%async_computation.18 | async-start | bytes 10027008 | tf_op jit(solution)/shard_map/all_gather | solution.py:158
  629.3 404.9 %all-reduce.13.cloned.1.call-start = ((), (), s32[]{:S(2)}) async-start(), calls=%async_computation.19 | async-start | bytes 3244032 | tf_op jit(solution)/shard_map/psum | solution.py:71
  1015.3 81.8 %all-reduce.15.cloned.1.call-start = ((), (), s32[]{:S(2)}) async-start(), calls=%async_computation.20 | async-start | bytes 3244032 | tf_op jit(solution)/shard_map/psum | solution.py:71
  1062.4 390.1 %reduce-scatter.11.cloned.1.call-start = ((), (), s32[]{:S(2)}) async-start(), calls=%async_computation.21 | async-start | bytes 11796480 | tf_op jit(solution)/shard_map/reduce_scatter | solution.py:342
  1289.9 264.0 %all-reduce.19.cloned.1.call-start = ((), (), s32[]{:S(2)}) async-start(), calls=%async_computation.30 | async-start | bytes 6488064 | tf_op jit(solution)/shard_map/psum | solution.py:67
  1486.8 324.6 %all-reduce.17.cloned.1.call-start = ((), (), s32[]{:S(2)}) async-start(), calls=%async_computation.29 | async-start | bytes 18874368
  1529.5 423.4 %reduce-scatter.17.cloned.1.call-start = ((), (), s32[]{:S(2)}) async-start(), calls=%async_computation.24 | async-start | bytes 5013504 | tf_op jit(solution)/shard_map/reduce_scatter | solution.py:372
  1535.3 559.9 %reduce-scatter.19.cloned.1.call-start = ((), (), s32[]{:S(2)}) async-start(), calls=%async_computation.25 | async-start | bytes 5013504 | tf_op jit(solution)/shard_map/reduce_scatter | solution.py:374
  1543.7 693.1 %reduce-scatter.15.cloned.1.call-start = ((), (), s32[]{:S(2)}) async-start(), calls=%async_computation.23 | async-start | bytes 5013504 | tf_op jit(solution)/shard_map/reduce_scatter | solution.py:371
  1551.1 812.8 %reduce-scatter.25.cloned.1.call-start = ((), (), s32[]{:S(2)}) async-start(), calls=%async_computation.28 | async-start | bytes 835584
  1559.5 1094.8 %reduce-scatter.23.cloned.1.call-start = ((), (), s32[]{:S(2)}) async-start(), calls=%async_computation.27 | async-start | bytes 20054016 | tf_op jit(solution)/shard_map/reduce_scatter | solution.py:376
  1576.2 1304.5 %reduce-scatter.13.cloned.1.call-start = ((), (), s32[]{:S(2)}) async-start(), calls=%async_computation.22 | async-start | bytes 15040512 | tf_op jit(solution)/shard_map/reduce_scatter | solution.py:370
  1588.4 1841.4 %reduce-scatter.21.cloned.1.call-start = ((), (), s32[]{:S(2)}) async-start(), calls=%async_computation.26 | async-start | bytes 40108032 | tf_op jit(solution)/shard_map/reduce_scatter | solution.py:375
  (96 other events, 4000.7 us)
Sparse Core Ops, SparseCore 0:
  11.5 104.1 all-gather.10
  142.2 87.5 all-gather.14
  231.9 87.8 all-gather.12
  323.0 60.6 all-gather.16
  386.9 79.2 all-gather.18
  468.9 19.1 all-reduce.8
  491.8 63.4 all-gather.20
  559.0 61.0 all-gather.22
  624.8 19.2 all-reduce.10
  647.5 212.6 all-gather.24
  863.5 120.6 all-gather.26
  1015.4 18.6 all-reduce.12
  1062.5 21.6 all-reduce.14
  1290.0 162.4 reduce-scatter.10
  1486.9 24.2 all-reduce.18
  1529.6 281.7 all-reduce.16
  1816.4 136.4 reduce-scatter.16
  1958.8 136.4 reduce-scatter.18
  2100.4 136.3 reduce-scatter.14
  2242.6 121.2 reduce-scatter.24
  2370.6 283.6 reduce-scatter.22
  2661.0 219.5 reduce-scatter.12
  2886.7 543.0 reduce-scatter.20
where the time goes:
time: 3530 us; the launch traced here: 3520 us
  waiting for transfers between devices  2670 us (76%)
  matrix products  341 us (10%)
  local copies, waits for them, and re-layouts  265 us (8%)
  other arithmetic  127 us (4%)
  blocking collectives  82.1 us (2%)
    reduce_scatter x1, waiting for transfers between devices, local(): lax.psum_scatter(grad_gate_up, ('shard', 'ctx'), scatter_dimension=0, til...  544 us
    unnamed x25, waiting for transfers between devices  316 us
    reduce_scatter x1, waiting for transfers between devices, local(): lax.psum_scatter(grad_down, ('shard', 'ctx'), scatter_dimension=0, tiled=...  288 us
    reduce_scatter x1, waiting for transfers between devices, local(): lax.psum_scatter(grad_qkv, ('shard', 'ctx'), scatter_dimension=0, tiled=T...  224 us
    all_gather x1, waiting for transfers between devices, local(): lax.all_gather(sent_gate_up, ('shard', 'ctx'), axis=0, tiled=True)  213 us
    reduce_scatter x1, waiting for transfers between devices, local(): lax.psum_scatter(key_terms.astype(jnp.bfloat16), 'ctx', scatter_dimension...  141 us
    reduce_scatter x1, waiting for transfers between devices, local(): lax.psum_scatter(grad_cross, ('shard', 'ctx'), scatter_dimension=0, tiled...  141 us
    reduce_scatter x1, waiting for transfers between devices, local(): lax.psum_scatter(grad_output, ('shard', 'ctx'), scatter_dimension=0, tile...  140 us
  transfers between devices with their start and end apart: 23, of which 21 were waited for; matrix products, arithmetic and copies ran while one was open for 11% of the time, Pallas kernels for 0%

commit v1 on v0

v1 whole, which is shorter than its diff:
```python
import functools

import jax
import jax.numpy as jnp
from jax import lax
from jax.experimental import pallas as pl
from jax.experimental.pallas import tpu as pltpu
from jax.sharding import PartitionSpec as P

HD = 64
ROT = 32
STEP = 7
LANES = 128


norm_eps = 1e-05
clip_norm = 1.0
beta_first = 0.9
beta_second = 0.999
learn_rate = 0.03
gain_rate = 0.75
weight_decay = 0.01
adam_eps = 1e-08
masked_score = -1e30
bf = jnp.bfloat16
fl = jnp.float32
MIB = 1024 * 1024


def params(mib):
    return pltpu.CompilerParams(vmem_limit_bytes=mib * MIB)


def whole(shape):
    return pl.BlockSpec(shape, lambda *index: (0,) * len(shape))


def matmul_t(left, right):
    return lax.dot_general(
        left, right, (((1,), (1,)), ((), ())), preferred_element_type=jnp.float32
    )


def matmul(left, right):
    return jnp.dot(left, right, preferred_element_type=jnp.float32)


def contract_rows(left, right):
    return lax.dot_general(
        left, right, (((0,), (0,)), ((), ())), preferred_element_type=jnp.float32
    )


def flip(block):
    return block.astype(fl).T


def norm_parts(rows):
    middle = jnp.mean(rows, axis=-1, keepdims=True)
    centred = rows - middle
    variance = jnp.mean(centred * centred, axis=-1, keepdims=True)
    inverse = lax.rsqrt(variance + norm_eps)
    return (centred * inverse, inverse)


def norm_back(grad_out, plain, inverse, gain):
    scaled = grad_out * gain
    term_mean = jnp.mean(scaled, axis=-1, keepdims=True)
    term_along = jnp.mean(scaled * plain, axis=-1, keepdims=True)
    return (inverse * (scaled - term_mean - plain * term_along), jnp.sum(grad_out * plain, axis=0))


def turn(lanes, cosine, sine_up, sine_down):
    return (
        lanes * cosine
        + pltpu.roll(lanes, ROT // 2, 1) * sine_up
        + pltpu.roll(lanes, LANES - ROT // 2, 1) * sine_down
    )


def project_kernel(
    wide, scale, x_ref, gain_ref, w_ref, cos_ref, up_ref, down_ref, a_ref, qkv_ref
):
    plain, _ = norm_parts(x_ref[...].astype(fl))
    rows = (plain * gain_ref[...]).astype(bf)
    a_ref[...] = rows
    projected = matmul(rows, w_ref[...])
    cosine, up, down = cos_ref[...], up_ref[...], down_ref[...]
    for start in range(0, 2 * wide, LANES):
        turned = turn(projected[:, start : start + LANES], cosine, up, down)
        if start < wide:
            turned = turned * scale
        qkv_ref[:, start : start + LANES] = turned.astype(bf)
    qkv_ref[:, 2 * wide :] = projected[:, 2 * wide :].astype(bf)


def project(x, gain, weight, tables, scale, block):
    rows, width = x.shape
    wide = weight.shape[1] // 3
    cosine, up, down = tables
    by_rows = lambda lanes: pl.BlockSpec((block, lanes), lambda i: (i, 0))
    return pl.pallas_call(
        functools.partial(project_kernel, wide, scale),
        grid=(rows // block,),
        in_specs=[
            by_rows(width),
            whole((1, width)),
            whole(weight.shape),
            by_rows(LANES),
            by_rows(LANES),
            by_rows(LANES),
        ],
        out_specs=[by_rows(width), by_rows(3 * wide)],
        out_shape=[
            jax.ShapeDtypeStruct((rows, width), bf),
            jax.ShapeDtypeStruct((rows, 3 * wide), bf),
        ],
        compiler_params=params(48),
        cost_estimate=pl.CostEstimate(
            flops=2 * rows * width * 3 * wide,
            bytes_accessed=4 * rows * width + 2 * rows * 3 * wide,
            transcendentals=0,
        ),
        name="project",
    )(x, gain, weight, cosine, up, down)


def attend_kernel(heads, wide, block, qkv_ref, mask_ref, o_ref, lse_ref):
    mask = mask_ref[:, 0:1] > 0.5
    total = qkv_ref.shape[0]
    if heads * HD < wide:
        o_ref[:, heads * HD :] = jnp.zeros((total, wide - heads * HD), bf)
    for h in range(heads):
        low, high = h * HD, (h + 1) * HD
        keys = qkv_ref[:, wide + low : wide + high]
        values_t = flip(qkv_ref[:, 2 * wide + low : 2 * wide + high]).astype(bf)
        for b in range(total // block):
            queries = qkv_ref[b * block : (b + 1) * block, low:high]
            scores = jnp.where(mask, matmul_t(keys, queries), masked_score)
            peak = jnp.max(scores, axis=0, keepdims=True)
            weights = jnp.exp(scores - peak)
            sums = jnp.sum(weights, axis=0, keepdims=True)
            mixed = matmul(values_t, weights.astype(bf)) / sums
            o_ref[b * block : (b + 1) * block, low:high] = mixed.T.astype(bf)
            spot = h * (total // block) + b
            lse_ref[0, spot : spot + 1, :] = peak + jnp.log(sums)


def attend(qkv, mask, latents, heads, block):
    rows, lanes = qkv.shape
    wide = lanes // 3
    total = rows // latents
    spots = heads * (total // block)
    spots_up = -(-spots // 8) * 8
    return pl.pallas_call(
        functools.partial(attend_kernel, heads, wide, block),
        grid=(latents,),
        in_specs=[
            pl.BlockSpec((total, lanes), lambda i: (i, 0)),
            pl.BlockSpec((total, LANES), lambda i: (i, 0)),
        ],
        out_specs=[
            pl.BlockSpec((total, wide), lambda i: (i, 0)),
            pl.BlockSpec((1, spots_up, block), lambda i: (i, 0, 0)),
        ],
        out_shape=[
            jax.ShapeDtypeStruct((rows, wide), bf),
            jax.ShapeDtypeStruct((latents, spots_up, block), fl),
        ],
        compiler_params=params(48),
        cost_estimate=pl.CostEstimate(
            flops=latents * heads * total * total * 16 * HD,
            bytes_accessed=rows * 4 * wide * 2,
            transcendentals=latents * heads * total * total,
        ),
        name="attend",
    )(qkv, mask)


def attend_back_kernel(
    heads, wide, block, scale, qkv_ref, do_ref, o_ref, lse_ref, mask_ref, cos_ref, up_ref, down_ref,
    out_ref, work_ref,
):
    mask = mask_ref[:, 0:1] > 0.5
    total = qkv_ref.shape[0]
    ones = jnp.ones((8, HD), fl)
    if heads * HD < wide:
        for part in range(3):
            work_ref[:, part * wide + heads * HD : (part + 1) * wide] = jnp.zeros(
                (total, wide - heads * HD), fl
            )
    for h in range(heads):
        low, high = h * HD, (h + 1) * HD
        keys = qkv_ref[:, wide + low : wide + high]
        keys_t = flip(keys).astype(bf)
        values = qkv_ref[:, 2 * wide + low : 2 * wide + high]
        grad_keys = jnp.zeros((total, HD), fl)
        grad_values = jnp.zeros((total, HD), fl)
        for b in range(total // block):
            queries = qkv_ref[b * block : (b + 1) * block, low:high]
            grads = do_ref[b * block : (b + 1) * block, low:high]
            mixed = o_ref[b * block : (b + 1) * block, low:high]
            spot = h * (total // block) + b
            scores = jnp.where(mask, matmul_t(keys, queries), masked_score)
            probs = jnp.exp(scores - lse_ref[0, spot : spot + 1, :])
            delta = lax.dot_general(
                ones,
                grads.astype(fl) * mixed.astype(fl),
                (((1,), (1,)), ((), ())),
                precision=lax.Precision.HIGHEST,
                preferred_element_type=fl,
            )[0:1]
            grad_scores = (probs * (matmul_t(values, grads) - delta)).astype(bf)
            grad_values += matmul(probs.astype(bf), grads)
            grad_keys += matmul(grad_scores, queries)
            grad_queries = matmul(keys_t, grad_scores) * scale
            work_ref[b * block : (b + 1) * block, low:high] = grad_queries.T
        work_ref[:, wide + low : wide + high] = grad_keys
        work_ref[:, 2 * wide + low : 2 * wide + high] = grad_values
    cosine, up, down = cos_ref[...], -up_ref[...], -down_ref[...]
    for start in range(0, 2 * wide, LANES):
        out_ref[:, start : start + LANES] = turn(
            work_ref[:, start : start + LANES], cosine, up, down
        ).astype(bf)
    out_ref[:, 2 * wide :] = work_ref[:, 2 * wide :].astype(bf)


def attend_back(qkv, grads, mixed, lse, mask, tables, latents, heads, block, scale):
    rows, lanes = qkv.shape
    wide = lanes // 3
    total = rows // latents
    by_latent = lambda n: pl.BlockSpec((total, n), lambda i: (i, 0))
    return pl.pallas_call(
        functools.partial(attend_back_kernel, heads, wide, block, scale),
        grid=(latents,),
        in_specs=[
            by_latent(lanes),
            by_latent(wide),
            by_latent(wide),
            pl.BlockSpec((1,) + lse.shape[1:], lambda i: (i, 0, 0)),
            by_latent(LANES),
            by_latent(LANES),
            by_latent(LANES),
            by_latent(LANES),
        ],
        out_specs=by_latent(lanes),
        out_shape=jax.ShapeDtypeStruct((rows, lanes), bf),
        scratch_shapes=[pltpu.VMEM((total, lanes), fl)],
        compiler_params=params(56),
        cost_estimate=pl.CostEstimate(
            flops=latents * heads * total * total * 40 * HD,
            bytes_accessed=rows * 10 * wide * 2,
            transcendentals=latents * heads * total * total,
        ),
        name="attend_back",
    )(qkv, grads, mixed, lse, mask, *tables)


def cross_kernel(heads, scale, q_ref, kv_ref, mask_ref, o_ref, lse_ref):
    mask = mask_ref[0, :, 0:1] > 0.5
    wide = heads * HD
    for first in range(0, heads, 2):
        pair = []
        for h in (first, first + 1):
            low, high = h * HD, (h + 1) * HD
            keys = kv_ref[0, :, low:high]
            values_t = flip(kv_ref[0, :, wide + low : wide + high]).astype(bf)
            scores = jnp.where(mask, matmul_t(keys, q_ref[0, :, low:high]) * scale, masked_score)
            peak = jnp.max(scores, axis=0, keepdims=True)
            weights = jnp.exp(scores - peak)
            sums = jnp.sum(weights, axis=0, keepdims=True)
            pair.append(matmul(values_t, weights.astype(bf)) / sums)
            lse_ref[0, h : h + 1, :] = peak + jnp.log(sums)
        o_ref[0, :, first * HD : (first + 2) * HD] = (
            jnp.concatenate(pair, axis=0).T.astype(bf)
        )


def cross(queries, pairs, mask, scale):
    latents, rows, wide = queries.shape
    heads = wide // HD
    heads_up = -(-heads // 8) * 8
    one = lambda shape: pl.BlockSpec((1,) + shape, lambda i: (i, 0, 0))
    return pl.pallas_call(
        functools.partial(cross_kernel, heads, scale),
        grid=(latents,),
        in_specs=[one((rows, wide)), one(pairs.shape[1:]), one(mask.shape[1:])],
        out_specs=[one((rows, wide)), one((heads_up, rows))],
        out_shape=[
            jax.ShapeDtypeStruct((latents, rows, wide), bf),
            jax.ShapeDtypeStruct((latents, heads_up, rows), fl),
        ],
        compiler_params=params(32),
        cost_estimate=pl.CostEstimate(
            flops=latents * heads * rows * 256 * 16 * HD,
            bytes_accessed=8 * latents * rows * wide,
            transcendentals=latents * heads * rows * 144,
        ),
        name="cross",
    )(queries, pairs, mask)


def cross_back_kernel(
    heads, scale, q_ref, kv_ref, do_ref, o_ref, lse_ref, mask_ref, dq_ref, dkv_ref
):
    mask = mask_ref[0, :, 0:1] > 0.5
    wide = heads * HD
    ones = jnp.ones((8, HD), fl)
    for first in range(0, heads, 2):
        pair = []
        grad_keys = []
        grad_values = []
        for h in (first, first + 1):
            low, high = h * HD, (h + 1) * HD
            keys = kv_ref[0, :, low:high]
            keys_t = flip(keys).astype(bf)
            values = kv_ref[0, :, wide + low : wide + high]
            queries = q_ref[0, :, low:high]
            grads = do_ref[0, :, low:high]
            scores = jnp.where(mask, matmul_t(keys, queries) * scale, masked_score)
            probs = jnp.exp(scores - lse_ref[0, h : h + 1, :])
            delta = lax.dot_general(
                ones,
                grads.astype(fl) * o_ref[0, :, low:high].astype(fl),
                (((1,), (1,)), ((), ())),
                precision=lax.Precision.HIGHEST,
                preferred_element_type=fl,
            )[0:1]
            grad_scores = (probs * (matmul_t(values, grads) - delta)).astype(bf)
            grad_values.append(matmul(probs.astype(bf), grads))
            grad_keys.append(matmul(grad_scores, queries) * scale)
            pair.append(matmul(keys_t, grad_scores) * scale)
        low, high = first * HD, (first + 2) * HD
        dq_ref[0, :, low:high] = jnp.concatenate(pair, axis=0).T.astype(bf)
        dkv_ref[0, :, low:high] = jnp.concatenate(grad_keys, axis=1).astype(bf)
        dkv_ref[0, :, wide + low : wide + high] = jnp.concatenate(grad_values, axis=1).astype(bf)


def cross_back(queries, pairs, grads, mixed, lse, mask, scale):
    latents, rows, wide = queries.shape
    heads = wide // HD
    one = lambda shape: pl.BlockSpec((1,) + shape, lambda i: (i, 0, 0))
    return pl.pallas_call(
        functools.partial(cross_back_kernel, heads, scale),
        grid=(latents,),
        in_specs=[
            one((rows, wide)),
            one(pairs.shape[1:]),
            one((rows, wide)),
            one((rows, wide)),
            one(lse.shape[1:]),
            one(mask.shape[1:]),
        ],
        out_specs=[one((rows, wide)), one(pairs.shape[1:])],
        out_shape=[
            jax.ShapeDtypeStruct(queries.shape, bf),
            jax.ShapeDtypeStruct(pairs.shape, bf),
        ],
        compiler_params=params(32),
        cost_estimate=pl.CostEstimate(
            flops=latents * heads * rows * 256 * 40 * HD,
            bytes_accessed=12 * latents * rows * wide,
            transcendentals=latents * heads * rows * 144,
        ),
        name="cross_back",
    )(queries, pairs, grads, mixed, lse, mask)


def mlp_kernel(a_ref, dy_ref, w_ref, h_ref, dgu_ref, out_ref, da_ref):
    units = h_ref.shape[1]
    rows = a_ref[...]
    gate = matmul(rows, w_ref[:, :units])
    upward = matmul(rows, w_ref[:, units : 2 * units])
    sigmoid = jax.nn.sigmoid(gate)
    activated = gate * sigmoid
    hidden = (activated * upward).astype(bf)
    h_ref[...] = hidden
    grad_hidden = matmul(dy_ref[...], w_ref[:, 2 * units :])
    grad_gate = (grad_hidden * upward * sigmoid * (1.0 + gate * (1.0 - sigmoid))).astype(bf)
    grad_up = (grad_hidden * activated).astype(bf)
    dgu_ref[:, :units] = grad_gate
    dgu_ref[:, units:] = grad_up
    da_ref[...] = (
        matmul_t(grad_gate, w_ref[:, :units]) + matmul_t(grad_up, w_ref[:, units : 2 * units])
    ).astype(bf)
    out_ref[...] = matmul_t(hidden, w_ref[:, 2 * units :]).astype(bf)


def mlp(rows, grads, weight, block):
    count, width = rows.shape
    units = weight.shape[1] // 3
    by_rows = lambda lanes: pl.BlockSpec((block, lanes), lambda i: (i, 0))
    return pl.pallas_call(
        mlp_kernel,
        grid=(count // block,),
        in_specs=[by_rows(width), by_rows(width), whole(weight.shape)],
        out_specs=[by_rows(units), by_rows(2 * units), by_rows(width), by_rows(width)],
        out_shape=[
            jax.ShapeDtypeStruct((count, units), bf),
            jax.ShapeDtypeStruct((count, 2 * units), bf),
            jax.ShapeDtypeStruct((count, width), bf),
            jax.ShapeDtypeStruct((count, width), bf),
        ],
        compiler_params=params(56),
        cost_estimate=pl.CostEstimate(
            flops=12 * count * width * units,
            bytes_accessed=2 * count * (4 * width + 3 * units) + 6 * width * units,
            transcendentals=count * units,
        ),
        name="mlp",
    )(rows, grads, weight)


def swap(value):
    return lax.ppermute(value, "tp", [(0, 1), (1, 0)])


def ring_shift(value, by):
    size = lax.axis_size("ctx")
    return lax.ppermute(value, "ctx", [(i, (i - by) % size) for i in range(size)])


def cross_over(value, bits):
    size = lax.axis_size("shard")
    return lax.ppermute(value, "shard", [(i, i ^ bits) for i in range(size)])


def ring_gather(own):
    if lax.axis_size("ctx") != 4:
        return [own] + [ring_shift(own, r) for r in range(1, lax.axis_size("ctx"))]
    half = own.shape[-1] // 2
    after = ring_shift(own, 1)
    before = ring_shift(own, -1)
    far = jnp.concatenate(
        [ring_shift(after[:, :half], 1), ring_shift(before[:, half:], -1)], axis=-1
    )
    return [own, after, far, before]


def ring_scatter(parts):
    if lax.axis_size("ctx") != 4:
        total = parts[0].astype(fl)
        for r in range(1, len(parts)):
            total = total + ring_shift(parts[r], -r).astype(fl)
        return total
    half = parts[0].shape[-1] // 2
    by_after = ring_shift(parts[2][:, :half], -1)
    by_before = ring_shift(parts[2][:, half:], 1)
    to_after = jnp.concatenate([parts[1][:, :half] + by_after, parts[1][:, half:]], axis=-1)
    to_before = jnp.concatenate([parts[3][:, :half], parts[3][:, half:] + by_before], axis=-1)
    return (
        parts[0].astype(fl)
        + ring_shift(to_after, -1).astype(fl)
        + ring_shift(to_before, 1).astype(fl)
    )


def square_gather(own):
    size = lax.axis_size("shard")
    if size != 4:
        every = lax.all_gather(own, "shard", axis=0, tiled=False)
        return [every[i] for i in range(size)]
    half = own.shape[-1] // 2
    one = cross_over(own, 1)
    two = cross_over(own, 2)
    three = jnp.concatenate([cross_over(two[:, :half], 1), cross_over(one[:, half:], 2)], axis=-1)
    return [own, one, two, three]


def square_scatter(parts):
    size = lax.axis_size("shard")
    if size != 4:
        return lax.psum_scatter(
            jnp.concatenate(parts, axis=0), "shard", scatter_dimension=0, tiled=True
        ).astype(fl)
    half = parts[0].shape[-1] // 2
    by_one = cross_over(parts[3][:, :half], 1)
    by_two = cross_over(parts[3][:, half:], 2)
    to_two = jnp.concatenate([parts[2][:, :half] + by_one, parts[2][:, half:]], axis=-1)
    to_one = jnp.concatenate([parts[1][:, :half], parts[1][:, half:] + by_two], axis=-1)
    return (
        parts[0].astype(fl)
        + cross_over(to_one, 1).astype(fl)
        + cross_over(to_two, 2).astype(fl)
    )


def total_over_all(value):
    for axis in ("tp", "shard", "ctx"):
        size = lax.axis_size(axis)
        bit = 1
        while bit < size:
            value = value + lax.ppermute(value, axis, [(i, i ^ bit) for i in range(size)])
            bit *= 2
    return value


def adam_step(weight, moment, square, grad, scale, decay, rate):
    grad = grad * scale
    moment_new = beta_first * moment + (1.0 - beta_first) * grad
    square_new = beta_second * square + (1.0 - beta_second) * grad * grad
    moment_hat = moment_new / (1.0 - beta_first**STEP)
    square_hat = square_new / (1.0 - beta_second**STEP)
    weight_new = weight - rate * (moment_hat / (jnp.sqrt(square_hat) + adam_eps) + decay * weight)
    return (moment_new, square_new, weight_new)


def rotary_tables(positions):
    lane = jnp.arange(LANES, dtype=jnp.int32) % HD
    step = (lane % (ROT // 2)).astype(fl) * 2.0 / ROT
    frequency = jnp.where(lane < ROT, 10000.0 ** (-step), 0.0)
    angles = positions.astype(fl)[:, None] * frequency[None, :]
    sine = jnp.sin(angles)
    up = jnp.where((lane >= ROT // 2) & (lane < ROT), sine, 0.0)
    down = jnp.where(lane < ROT // 2, -sine, 0.0)
    return (jnp.cos(angles), up, down)


def local(
    tokens,
    conditioning,
    cotangent,
    piece_lengths,
    start_positions,
    cond_counts,
    norm_gains,
    gains_moment,
    gains_square,
    qkv_weight,
    qkv_moment,
    qkv_square,
    output_weight,
    output_moment,
    output_square,
    cross_query_weight,
    cross_query_moment,
    cross_query_square,
    cross_pair_weight,
    cross_pair_moment,
    cross_pair_square,
    cross_out_weight,
    cross_out_moment,
    cross_out_square,
    gate_up_weight,
    gate_up_moment,
    gate_up_square,
    down_weight,
    down_moment,
    down_square,
):
    seqs, cap, width = tokens.shape
    cond_len = conditioning.shape[1]
    pieces = piece_lengths.shape[1]
    scale = HD ** (-0.5)
    shards = lax.axis_size("shard")
    ctxs = lax.axis_size("ctx")
    ctx_index = lax.axis_index("ctx")
    tp_index = lax.axis_index("tp")
    owned = qkv_weight.shape[0]
    local_width = qkv_weight.shape[2]
    units_half = down_weight.shape[1]
    few = local_width // ctxs
    heads_few = few // HD
    wide = -(-few // LANES) * LANES
    units = units_half // shards

    latent_order = (tp_index + jnp.arange(seqs, dtype=jnp.int32)) % seqs
    piece_order = (ctx_index + jnp.arange(pieces, dtype=jnp.int32)) % pieces
    mine = lambda array: lax.dynamic_index_in_dim(array, latent_order[0], 0, keepdims=False)
    others = lambda array: lax.dynamic_index_in_dim(array, latent_order[1], 0, keepdims=False)

    def both(array):
        return jnp.stack([mine(array), others(array)])

    offsets = jnp.cumsum(piece_lengths, axis=1) - piece_lengths
    slot = jnp.arange(cap, dtype=jnp.int32)
    lengths_here = both(piece_lengths)[:, piece_order]
    offsets_here = both(offsets)[:, piece_order]
    starts_here = both(start_positions)
    positions = (starts_here[:, None, None] + offsets_here[:, :, None] + slot).reshape(-1)
    key_valid = (slot < lengths_here[:, :, None]).reshape(-1)
    key_mask = jnp.broadcast_to(key_valid.astype(fl)[:, None], (key_valid.shape[0], LANES))
    tables = rotary_tables(positions)
    own_valid = (slot < lengths_here[0, 0]).astype(fl)[:, None]

    tokens_mine = mine(tokens)
    tokens_other = others(tokens)
    token_blocks = ring_gather(tokens_mine)
    token_swapped = [tokens_other] + [swap(block) for block in token_blocks[1:]]
    tokens_all = jnp.concatenate(token_blocks + token_swapped, axis=0)
    dy_mine = mine(cotangent).astype(fl) * own_valid
    dy_low = dy_mine.astype(bf)
    dy_blocks = square_gather(dy_low)
    dy_all = jnp.concatenate([b for block in dy_blocks for b in (block, swap(block))], axis=0)

    kinds = jnp.concatenate(
        [
            qkv_weight.astype(bf),
            output_weight.astype(bf)[:, None],
            cross_pair_weight.astype(bf),
        ],
        axis=1,
    )
    n_kinds = kinds.shape[1]
    kinds = jnp.transpose(kinds.reshape(owned, n_kinds, ctxs, few), (2, 0, 1, 3)).reshape(
        ctxs, owned, n_kinds * few
    )
    gain_lanes = jnp.pad(jnp.transpose(norm_gains).astype(bf), ((0, 0), (0, LANES - 3)))
    sent_attn = jnp.concatenate(
        [kinds, jnp.broadcast_to(gain_lanes[None], (ctxs, owned, LANES))], axis=2
    )
    sent_attn = lax.all_to_all(sent_attn, "ctx", 0, 0, tiled=True)
    attn_full = lax.all_gather(
        sent_attn.reshape(ctxs * owned, -1), "shard", axis=0, tiled=True
    )
    weight_of = lambda kind: attn_full[:, kind * few : (kind + 1) * few]
    padded = lambda array: jnp.pad(array, ((0, 0), (0, wide - few)))
    qkv_wide = jnp.concatenate([padded(weight_of(kind)) for kind in range(3)], axis=1)
    output_wide = padded(weight_of(3))
    pair_full = attn_full[:, 4 * few : 6 * few]
    gains = jnp.transpose(attn_full[:, n_kinds * few : n_kinds * few + 3].astype(fl))

    cross_full = lax.all_gather(
        jnp.concatenate([cross_query_weight.astype(bf), cross_out_weight.astype(bf)], axis=1),
        ("shard", "ctx"),
        axis=0,
        tiled=True,
    )
    query_full = cross_full[:, :local_width]
    cross_out_full = cross_full[:, local_width:]

    sent_mlp = jnp.concatenate(
        [gate_up_weight.astype(bf), down_weight.astype(bf)[:, None]], axis=1
    )
    sent_mlp = jnp.transpose(sent_mlp.reshape(owned, 3, shards, units), (2, 0, 1, 3)).reshape(
        shards, owned, 3 * units
    )
    sent_mlp = lax.all_to_all(sent_mlp, "shard", 0, 0, tiled=True)
    mlp_full = lax.all_gather(sent_mlp, "ctx", axis=0, tiled=False)
    mlp_full = jnp.transpose(mlp_full, (1, 0, 2, 3)).reshape(width, 3 * units)

    total = pieces * cap
    block = total // 3
    input1, qkv = project(tokens_all, gains[0:1], qkv_wide, tables, scale, block)
    mixed_low, lse = attend(qkv, key_mask, seqs, heads_few, block)
    partial = matmul_t(mixed_low, output_wide).astype(bf).reshape(seqs, pieces, cap, width)
    from_other = swap(partial[1])
    mine_parts = [partial[0, r] + from_other[r] for r in range(pieces)]
    x_rows = tokens_mine.astype(fl)
    x_first = x_rows + ring_scatter(mine_parts)

    plain2, inverse2 = norm_parts(x_first)
    input2_mine = (plain2 * gains[1]).astype(bf)
    input2 = jnp.concatenate([input2_mine, swap(input2_mine)], axis=0)
    cross_queries = matmul(input2, query_full).astype(bf).reshape(seqs, cap, local_width)
    cond_up = -(-cond_len // 16) * 16
    cond_rows = jnp.pad(both(conditioning), ((0, 0), (0, cond_up - cond_len), (0, 0))).reshape(
        seqs * cond_up, width
    )
    own_pairs = matmul(cond_rows, pair_full).astype(bf)
    pairs = lax.all_gather(own_pairs, "ctx", axis=0, tiled=False)
    pairs = jnp.transpose(
        pairs.reshape(ctxs, seqs, cond_up, 2, few), (1, 2, 3, 0, 4)
    ).reshape(seqs, cond_up, 2 * local_width)
    cond_valid = jnp.arange(cond_up, dtype=jnp.int32)[None, :] < both(cond_counts)[:, None]
    cond_mask = jnp.broadcast_to(cond_valid.astype(fl)[:, :, None], (seqs, cond_up, LANES))
    cross_low, cross_lse = cross(cross_queries, pairs, cond_mask, scale)
    cross_low_rows = cross_low.reshape(seqs * cap, local_width)
    cross_partial = matmul_t(cross_low_rows, cross_out_full).astype(bf)
    x_second = x_first + (
        cross_partial[:cap].astype(fl) + swap(cross_partial[cap:]).astype(fl)
    )

    plain3, inverse3 = norm_parts(x_second)
    input3 = (plain3 * gains[2]).astype(bf)
    input3_all = jnp.concatenate(
        [b for block in square_gather(input3) for b in (block, swap(block))], axis=0
    )
    hidden, grad_gated, down_partial, back_partial = mlp(
        input3_all, dy_all, mlp_full, (shards * seqs * cap) // (6 * shards // 4)
    )

    def scatter_rows(partial_rows):
        parts = partial_rows.reshape(shards, seqs, cap, width)
        from_other = swap(parts[:, 1])
        return square_scatter([parts[r, 0] + from_other[r] for r in range(shards)])

    back3, grad_gain3 = norm_back(scatter_rows(back_partial), plain3, inverse3, gains[2])
    block_mine = (x_second + scatter_rows(down_partial)).astype(bf)
    block_other = swap(block_mine)

    def natural(first, second):
        straight = tp_index == 0
        return jnp.stack(
            [jnp.where(straight, first, second), jnp.where(straight, second, first)]
        )

    block_out = natural(block_mine, block_other)
    grad_gate_up = contract_rows(input3_all, grad_gated).astype(bf)
    grad_down = contract_rows(dy_all, hidden).astype(bf)
    grad_mlp = jnp.concatenate([grad_gate_up, grad_down], axis=1)
    grad_mlp = jnp.transpose(
        grad_mlp.reshape(shards, ctxs, owned, 3 * units), (1, 0, 2, 3)
    ).reshape(ctxs * shards * owned, 3 * units)
    own_mlp = lax.psum_scatter(grad_mlp, "ctx", scatter_dimension=0, tiled=True)
    own_mlp = lax.all_to_all(
        own_mlp.reshape(shards, owned, 3 * units), "shard", 0, 0, tiled=True
    )
    own_mlp = jnp.transpose(own_mlp.reshape(shards, owned, 3, units), (1, 2, 0, 3)).reshape(
        owned, 3, units_half
    )

    grad_second = dy_mine + back3
    grad2_mine = grad_second.astype(bf)
    grad2_low = jnp.concatenate([grad2_mine, swap(grad2_mine)], axis=0)
    grad_cross_out = contract_rows(grad2_low, cross_low_rows)
    grad_cmixed = matmul(grad2_low, cross_out_full).astype(bf).reshape(seqs, cap, local_width)
    grad_cq, grad_pairs = cross_back(
        cross_queries, pairs, grad_cmixed, cross_low, cross_lse, cond_mask, scale
    )
    grad_cq = grad_cq.reshape(seqs * cap, local_width)
    grad_query = contract_rows(input2, grad_cq)
    query_partial = matmul_t(grad_cq, query_full).astype(bf)
    back2, grad_gain2 = norm_back(
        query_partial[:cap].astype(fl) + swap(query_partial[cap:]).astype(fl),
        plain2,
        inverse2,
        gains[1],
    )
    own_cross = lax.psum_scatter(
        jnp.concatenate([grad_query.astype(bf), grad_cross_out.astype(bf)], axis=1),
        ("shard", "ctx"),
        scatter_dimension=0,
        tiled=True,
    ).astype(fl)
    grad_pairs = jnp.transpose(
        grad_pairs.reshape(seqs, cond_up, 2, ctxs, few), (3, 0, 1, 2, 4)
    ).reshape(ctxs * seqs * cond_up, 2 * few)
    own_pair_grads = lax.psum_scatter(grad_pairs, "ctx", scatter_dimension=0, tiled=True)
    grad_pair = contract_rows(cond_rows, own_pair_grads)

    grad_first = grad_second + back2
    grad1_mine = grad_first.astype(bf)
    grad1_blocks = ring_gather(grad1_mine)
    grad1_low = jnp.concatenate(
        grad1_blocks + [swap(block) for block in grad1_blocks], axis=0
    )
    grad_output = contract_rows(grad1_low, mixed_low)
    grad_mixed = matmul(grad1_low, output_wide).astype(bf)
    grad_projected = attend_back(
        qkv, grad_mixed, mixed_low, lse, key_mask, tables, seqs, heads_few, block, scale
    )
    first_partial = matmul_t(grad_projected, qkv_wide).astype(bf).reshape(
        seqs, pieces, cap, width
    )
    from_other = swap(first_partial[1])
    first_parts = [first_partial[0, r] + from_other[r] for r in range(pieces)]
    plain1, inverse1 = norm_parts(x_rows)
    back1, grad_gain1 = norm_back(ring_scatter(first_parts), plain1, inverse1, gains[0])
    tokens_grad_mine = grad_first + back1
    tokens_grad = natural(tokens_grad_mine, swap(tokens_grad_mine))
    grad_qkv = contract_rows(input1, grad_projected)

    gain_grads = jnp.pad(
        jnp.stack([grad_gain1, grad_gain2, grad_gain3], axis=1), ((0, 0), (0, LANES - 3))
    )
    grad_attn = jnp.concatenate(
        [grad_qkv[:, kind * wide : kind * wide + few].astype(bf) for kind in range(3)]
        + [grad_output[:, :few].astype(bf), grad_pair.astype(bf), gain_grads.astype(bf)],
        axis=1,
    )
    own_attn = lax.psum_scatter(grad_attn, "shard", scatter_dimension=0, tiled=True)
    own_attn = lax.all_to_all(own_attn.reshape(ctxs, owned, -1), "ctx", 0, 0, tiled=True)
    own_gains = jnp.sum(own_attn[:, :, n_kinds * few : n_kinds * few + 3].astype(fl), axis=0)
    own_gains = jnp.transpose(own_gains + swap(own_gains))
    own_kinds = jnp.transpose(
        own_attn[:, :, : n_kinds * few].reshape(ctxs, owned, n_kinds, few), (1, 2, 0, 3)
    ).reshape(owned, n_kinds, local_width).astype(fl)
    own_qkv = own_kinds[:, :3]
    own_output = own_kinds[:, 3]
    own_pair = own_kinds[:, 4:]
    own_query = own_cross[:, :local_width]
    own_cross_out = own_cross[:, local_width:]
    own_gate_up = own_mlp[:, :2].astype(fl)
    own_down = own_mlp[:, 2].astype(fl)

    squares = jnp.sum(own_kinds * own_kinds) + jnp.sum(own_cross * own_cross)
    squares = squares + jnp.sum(own_gate_up * own_gate_up) + jnp.sum(own_down * own_down)
    squares = squares + jnp.sum(own_gains * own_gains) / float(lax.axis_size("tp"))
    total_square = total_over_all(jnp.broadcast_to(squares, (8, LANES)))[0, 0]
    grad_norm = jnp.sqrt(total_square)
    clip_scale = clip_norm / jnp.maximum(grad_norm, clip_norm)

    def step(weight, moment, square, grad):
        return adam_step(weight, moment, square, grad, clip_scale, weight_decay, learn_rate)

    return (
        block_out,
        tokens_grad,
        grad_norm,
        *adam_step(
            norm_gains, gains_moment, gains_square, own_gains, clip_scale, 0.0, gain_rate
        ),
        *step(qkv_weight, qkv_moment, qkv_square, own_qkv),
        *step(output_weight, output_moment, output_square, own_output),
        *step(cross_query_weight, cross_query_moment, cross_query_square, own_query),
        *step(cross_pair_weight, cross_pair_moment, cross_pair_square, own_pair),
        *step(cross_out_weight, cross_out_moment, cross_out_square, own_cross_out),
        *step(gate_up_weight, gate_up_moment, gate_up_square, own_gate_up),
        *step(down_weight, down_moment, down_square, own_down),
    )


def solution(mesh):
    in_specs = (
        P("shard", "ctx", None),
        P("shard", None, None),
        P("shard", "ctx", None),
        P("shard", None),
        P("shard"),
        P("shard"),
        P(None, ("shard", "ctx")),
        P(None, ("shard", "ctx")),
        P(None, ("shard", "ctx")),
        P(("shard", "ctx"), None, "tp"),
        P(("shard", "ctx"), None, "tp"),
        P(("shard", "ctx"), None, "tp"),
        P(("shard", "ctx"), "tp"),
        P(("shard", "ctx"), "tp"),
        P(("shard", "ctx"), "tp"),
        P(("shard", "ctx"), "tp"),
        P(("shard", "ctx"), "tp"),
        P(("shard", "ctx"), "tp"),
        P(("shard", "ctx"), None, "tp"),
        P(("shard", "ctx"), None, "tp"),
        P(("shard", "ctx"), None, "tp"),
        P(("shard", "ctx"), "tp"),
        P(("shard", "ctx"), "tp"),
        P(("shard", "ctx"), "tp"),
        P(("shard", "ctx"), None, "tp"),
        P(("shard", "ctx"), None, "tp"),
        P(("shard", "ctx"), None, "tp"),
        P(("shard", "ctx"), "tp"),
        P(("shard", "ctx"), "tp"),
        P(("shard", "ctx"), "tp"),
    )
    out_specs = (
        P("shard", "ctx", None),
        P("shard", "ctx", None),
        P(),
        P(None, ("shard", "ctx")),
        P(None, ("shard", "ctx")),
        P(None, ("shard", "ctx")),
        P(("shard", "ctx"), None, "tp"),
        P(("shard", "ctx"), None, "tp"),
        P(("shard", "ctx"), None, "tp"),
        P(("shard", "ctx"), "tp"),
        P(("shard", "ctx"), "tp"),
        P(("shard", "ctx"), "tp"),
        P(("shard", "ctx"), "tp"),
        P(("shard", "ctx"), "tp"),
        P(("shard", "ctx"), "tp"),
        P(("shard", "ctx"), None, "tp"),
        P(("shard", "ctx"), None, "tp"),
        P(("shard", "ctx"), None, "tp"),
        P(("shard", "ctx"), "tp"),
        P(("shard", "ctx"), "tp"),
        P(("shard", "ctx"), "tp"),
        P(("shard", "ctx"), None, "tp"),
        P(("shard", "ctx"), None, "tp"),
        P(("shard", "ctx"), None, "tp"),
        P(("shard", "ctx"), "tp"),
        P(("shard", "ctx"), "tp"),
        P(("shard", "ctx"), "tp"),
    )
    return jax.shard_map(local, mesh=mesh, in_specs=in_specs, out_specs=out_specs, check_vma=False)
```

time: 3530 us -> 1160 us (0.33)
  waiting for transfers between devices: 2670 us -> 513 us
  matrix products: 341 us -> 72.1 us
  Pallas kernels: 0 us -> 114 us
  local copies, waits for them, and re-layouts: 265 us -> 170 us
  starting transfers between devices: 2.08 us -> 64 us
  other arithmetic: 127 us -> 89.6 us
    reduce_scatter x7 -> x4, waiting for transfers between devices: 1620 us -> 160 us  [the longest x1 142 us: local(): lax.psum_scatter(jnp.concatenate([grad_query.astype(bf), grad_cross_out.a...]
    all_gather x9 -> x3, waiting for transfers between devices: 706 us -> 0.02 us  [the longest x1 0.02 us: local(): lax.all_gather(jnp.concatenate([cross_query_weight.astype(bf), cross_out_...]
    ppermute x0 -> x63, waiting for transfers between devices: none -> 325 us  [the longest x16 243 us: ring_shift(): lax.ppermute(value, 'ctx', [(i, (i - by) % size) for i in range(size)])]
    unnamed x25 -> x7, waiting for transfers between devices: 316 us -> 0.12 us
    dot_general x81 -> x8, matrix products: 266 us -> 25.1 us  [the longest x4 12.6 us: matmul(): return jnp.dot(left, right, preferred_element_type=jnp.float32)]
    pallas_call x0 -> x6, Pallas kernels: none -> 114 us  [the longest x1 40.3 us: mlp(): pl.pallas_call(mlp_kernel, grid=(count // block,), in_specs=[by_rows(widt...]
    all_to_all x0 -> x2, blocking collectives: none -> 57.8 us  [the longest x1 30.7 us: local(): sent_attn = lax.all_to_all(sent_attn, 'ctx', 0, 0, tiled=True)]
    ppermute x0 -> x63, starting transfers between devices: none -> 55.3 us  [the longest x16 27.2 us: ring_shift(): lax.ppermute(value, 'ctx', [(i, (i - by) % size) for i in range(size)])]
  transfers between devices with their start and end apart: 23 -> 72, of which waited for: 21 -> 33; matrix products, arithmetic and copies ran while one was open for 11% -> 24% of each run, Pallas kernels for 0% -> 6%
where the time goes in v1:
time: 1160 us; the launch traced here: 1140 us
  waiting for transfers between devices  513 us (44%)
  local copies, waits for them, and re-layouts  170 us (15%)
  Pallas kernels  114 us (10%)
  blocking collectives  97.1 us (8%)
  other arithmetic  89.6 us (8%)
  matrix products  72.1 us (6%)
  starting transfers between devices  64 us (6%)
  between operations  25.2 us (2%)
    ppermute x16, waiting for transfers between devices, ring_shift(): lax.ppermute(value, 'ctx', [(i, (i - by) % size) for i in range(size)])  243 us
    reduce_scatter x1, waiting for transfers between devices, local(): lax.psum_scatter(jnp.concatenate([grad_query.astype(bf), grad_cross_out.a...  142 us
    unnamed x244, local copies, waits for them, and re-layouts  77.1 us
    ppermute x16, waiting for transfers between devices, cross_over(): return lax.ppermute(value, 'shard', [(i, i ^ bits) for i in range(size)])  74.9 us
    dot_general x7, matrix products, contract_rows(): lax.dot_general(left, right, (((0,), (0,)), ((), ())), preferred_element_...  46.9 us
    pallas_call x1, Pallas kernels, mlp(): pl.pallas_call(mlp_kernel, grid=(count // block,), in_specs=[by_rows(widt...  40.3 us
    all_gather x1, blocking collectives, local(): pairs = lax.all_gather(own_pairs, 'ctx', axis=0, tiled=False)  39.3 us
    all_to_all x1, blocking collectives, local(): sent_attn = lax.all_to_all(sent_attn, 'ctx', 0, 0, tiled=True)  30.7 us
  transfers between devices with their start and end apart: 72, of which 33 were waited for; matrix products, arithmetic and copies ran while one was open for 24% of the time, Pallas kernels for 6%

profile of v1, /device:TPU:0, one launch (start us, length us, event | category | flops | bytes accessed | tf_op | source)
XLA Modules:
  0.0 1144.6 jit_solution(6381324637227743917)
XLA Ops:
  13.8 30.7 %all_to_all.20 = bf16[4,96,1280]{2,1,0:T(8,128)(2,1)} all-to-all(bf16[4,96,1280]{2,1,0:T(8,128)(2,1)S(1)} %copy.375), channel_id=1, replica_groups=mesh['shard'=4,'ctx'=4,'tp'=2] {'ctx'}, dimensions={0} | all-to-all | bytes 1966080 | tf_op jit(solution)/shard_map/all_to_all | solution.py:612
  74.1 12.6 %collective-permute-done = bf16[264,1536]{1,0:T(8,128)(2,1)} collective-permute-done((bf16[264,1536]{1,0:T(8,128)(2,1)}, bf16[264,1536]{1,0:T(8,128)(2,1)}, u32[]{:S(2)}, u32[]{:S(2)}) %collective-permute-start) | collective-permute-done | bytes 811040 | tf_op jit(solution)/shard_map/ppermute | solution.py:420
  122.2 13.3 %project.1 = (bf16[2112,1536]{1,0:T(8,128)(2,1)}, bf16[2112,768]{1,0:T(8,128)(2,1)}) custom-call(bf16[2112,1536]{1,0:T(8,128)(2,1)} %constant_dynamic-update-slice_fusion.x_ref, f32[1,1536]{1,0:T(1,128)S(1)} %copy.379.gain_ref, bf16[1536,768]{1,0:T(8,128)(2,1)S(1)} %fusion.9.w_ref, f32[2112,128]{1,0:T(8,128)S(1)} %get-tuple-element.321.cos_ref, ...), custom_call_target="tpu_custom_call" | custom-call | flops 4982833152 | bytes 16220160 | tf_op jit(solution)/shard_map/project/pallas_call | solution.py:102
  138.2 15.4 %attend.1 = (bf16[2112,256]{1,0:T(8,128)(2,1)S(1)}, f32[2,16,352]{2,1,0:T(8,128)S(1)}) custom-call(bf16[2112,768]{1,0:T(8,128)(2,1)S(1)} %copy-done.8, f32[2112,128]{1,0:T(8,128)S(1)} %broadcast_in_dim.29.mask_ref), custom_call_target="tpu_custom_call" | custom-call | flops 6851395584 | bytes 4325376 | tf_op jit(solution)/shard_map/attend/pallas_call | solution.py:155
  168.7 27.1 %all_to_all.21 = bf16[4,96,2304]{2,1,0:T(8,128)(2,1)} all-to-all(bf16[4,96,2304]{2,1,0:T(8,128)(2,1)} %reshape.377), channel_id=1, replica_groups=mesh['shard'=4,'ctx'=4,'tp'=2] {'shard'}, dimensions={0} | all-to-all | bytes 3538944 | tf_op jit(solution)/shard_map/all_to_all | solution.py:638
  202.6 23.9 %collective-permute-done.10 = bf16[264,768]{1,0:T(8,128)(2,1)S(1)} collective-permute-done((bf16[264,768]{1,0:T(8,128)(2,1)S(1)}, bf16[264,768]{1,0:T(8,128)(2,1)S(1)}, u32[]{:S(2)}, u32[]{:S(2)}) %collective-permute-start.10) | collective-permute-done | bytes 405536 | tf_op jit(solution)/shard_map/ppermute | solution.py:420
  247.2 53.8 %collective-permute-done.11 = bf16[264,1536]{1,0:T(8,128)(2,1)S(1)} collective-permute-done((bf16[264,1536]{1,0:T(8,128)(2,1)S(1)}, bf16[264,1536]{1,0:T(8,128)(2,1)S(1)}, u32[]{:S(2)}, u32[]{:S(2)}) %collective-permute-start.11) | collective-permute-done | bytes 811040 | tf_op jit(solution)/shard_map/ppermute | solution.py:420
  308.4 39.3 %all-gather = bf16[1152,384]{1,0:T(8,128)(2,1)S(1)} all-gather(bf16[288,384]{1,0:T(8,128)(2,1)S(1)} %convolution_convert_fusion.11), channel_id=2, replica_groups=mesh['shard'=4,'ctx'=4,'tp'=2] {'ctx'}, dimensions={0}, use_global_device_ids=true | all-gather | bytes 1105920 | tf_op jit(solution)/shard_map/all_gather | solution.py:661
  387.4 13.1 %collective-permute-done.15 = bf16[264,1536]{1,0:T(8,128)(2,1)S(1)} collective-permute-done((bf16[264,1536]{1,0:T(8,128)(2,1)}, bf16[264,1536]{1,0:T(8,128)(2,1)S(1)}, u32[]{:S(2)}, u32[]{:S(2)}) %collective-permute-start.15) | collective-permute-done | bytes 811040 | tf_op jit(solution)/shard_map/ppermute | solution.py:425
  429.5 40.3 %mlp.1 = (bf16[2112,768]{1,0:T(8,128)(2,1)}, bf16[2112,1536]{1,0:T(8,128)(2,1)}, bf16[2112,1536]{1,0:T(8,128)(2,1)}, bf16[2112,1536]{1,0:T(8,128)(2,1)}) custom-call(bf16[2112,1536]{1,0:T(8,128)(2,1)} %constant_dynamic-update-slice_fusion.7.a_ref, bf16[2112,1536]{1,0:T(8,128)(2,1)} %constant_dynamic-update-slice_fusion.15.dy_ref, bf16[1536,2304]{1,0:T(8,128)(2,1)} %bitcast.287), custom_call_target="tpu_custom_call" | custom-call | flops 29896998912 | bytes 42762240 | tf_op jit(solution)/shard_map/mlp/pallas_call | solution.py:393
  491.8 12.2 %collective-permute-done.37 = bf16[264,768]{1,0:T(8,128)(2,1)S(1)} collective-permute-done((bf16[264,768]{1,0:T(8,128)(2,1)S(1)}, bf16[264,768]{1,0:T(8,128)(2,1)S(1)}, u32[]{:S(2)}, u32[]{:S(2)}) %collective-permute-start.37) | collective-permute-done | bytes 405536 | tf_op jit(solution)/shard_map/ppermute | solution.py:425
  507.6 13.8 %collective-permute-done.40 = bf16[264,1536]{1,0:T(8,128)(2,1)S(1)} collective-permute-done((bf16[264,1536]{1,0:T(8,128)(2,1)S(1)}, bf16[264,1536]{1,0:T(8,128)(2,1)S(1)}, u32[]{:S(2)}, u32[]{:S(2)}) %collective-permute-start.40) | collective-permute-done | bytes 811040 | tf_op jit(solution)/shard_map/ppermute | solution.py:425
  526.6 11.5 %collective-permute-done.34 = bf16[264,1536]{1,0:T(8,128)(2,1)S(1)} collective-permute-done((bf16[264,1536]{1,0:T(8,128)(2,1)S(1)}, bf16[264,1536]{1,0:T(8,128)(2,1)S(1)}, u32[]{:S(2)}, u32[]{:S(2)}) %collective-permute-start.34) | collective-permute-done | bytes 811040 | tf_op jit(solution)/shard_map/ppermute | solution.py:425
  542.9 16.6 %convolution_convert_fusion.2 = bf16[1536,1536]{0,1:T(8,128)(2,1)} fusion(bf16[2112,1536]{1,0:T(8,128)(2,1)} %constant_dynamic-update-slice_fusion.7.a_ref, bf16[2112,1536]{1,0:T(8,128)(2,1)} %get-tuple-element.49), kind=kOutput, calls=%fused_computation.4 | convolution fusion | flops 9968025600 | bytes 17694720 | tf_op jit(solution)/shard_map/dot_general | solution.py:49
  634.7 15.5 %collective-permute-done.43 = bf16[264,1536]{1,0:T(8,128)(2,1)S(1)} collective-permute-done((bf16[264,1536]{1,0:T(8,128)(2,1)}, bf16[264,1536]{1,0:T(8,128)(2,1)S(1)}, u32[]{:S(2)}, u32[]{:S(2)}) %collective-permute-start.43) | collective-permute-done | bytes 811040 | tf_op jit(solution)/shard_map/ppermute | solution.py:420
  660.7 23.6 %collective-permute-done.44 = bf16[264,768]{1,0:T(8,128)(2,1)S(1)} collective-permute-done((bf16[264,768]{1,0:T(8,128)(2,1)S(1)}, bf16[264,768]{1,0:T(8,128)(2,1)S(1)}, u32[]{:S(2)}, u32[]{:S(2)}) %collective-permute-start.44) | collective-permute-done | bytes 405536 | tf_op jit(solution)/shard_map/ppermute | solution.py:420
  696.6 28.9 %attend_back.1 = bf16[2112,768]{1,0:T(8,128)(2,1)} custom-call(bf16[2112,768]{1,0:T(8,128)(2,1)} %get-tuple-element.39.qkv_ref, bf16[2112,256]{1,0:T(8,128)(2,1)} %convolution_convert_fusion.3.do_ref, bf16[2112,256]{1,0:T(8,128)(2,1)} %copy-done, f32[2,16,352]{2,1,0:T(8,128)} %copy-done.11, f32[2112,128]{1,0:T(8,128)} %copy-done.5, f32[2112,128]{1,0:T(8,128)} %copy-done.4, ...), custom_call_target="tpu_custom_call" | custom-call | flops 17128488960 | bytes 10813440 | tf_op jit(solution)/shard_map/attend_back/pallas_call | solution.py:233
  734.3 10.4 convolution_convert_fusion.7
  752.3 36.6 %collective-permute-done.54 = bf16[264,768]{1,0:T(8,128)(2,1)S(1)} collective-permute-done((bf16[264,768]{1,0:T(8,128)(2,1)S(1)}, bf16[264,768]{1,0:T(8,128)(2,1)S(1)}, u32[]{:S(2)}, u32[]{:S(2)}) %collective-permute-start.54) | collective-permute-done | bytes 405536 | tf_op jit(solution)/shard_map/ppermute | solution.py:420
  797.5 19.9 %collective-permute-done.55 = bf16[264,1536]{1,0:T(8,128)(2,1)S(1)} collective-permute-done((bf16[264,1536]{1,0:T(8,128)(2,1)}, bf16[264,1536]{1,0:T(8,128)(2,1)S(1)}, u32[]{:S(2)}, u32[]{:S(2)}) %collective-permute-start.55) | collective-permute-done | bytes 811040 | tf_op jit(solution)/shard_map/ppermute | solution.py:420
  817.4 17.8 %collective-permute-done.53 = bf16[264,1536]{1,0:T(8,128)(2,1)S(1)} collective-permute-done((bf16[264,1536]{1,0:T(8,128)(2,1)}, bf16[264,1536]{1,0:T(8,128)(2,1)S(1)}, u32[]{:S(2)}, u32[]{:S(2)}) %collective-permute-start.53) | collective-permute-done | bytes 811040 | tf_op jit(solution)/shard_map/ppermute | solution.py:420
  865.4 27.3 %all-to-all-done.3 = bf16[4,96,2304]{2,1,0:T(8,128)(2,1)S(1)} async-done(((bf16[4,96,2304]{2,1,0:T(8,128)(2,1)}), bf16[4,96,2304]{2,1,0:T(8,128)(2,1)S(1)}, u32[]{:S(2)}, u32[]{:S(2)}) %all-to-all-start.3) | async-done | bytes 1769504 | tf_op jit(solution)/shard_map/all_to_all | solution.py:706
  892.8 18.7 %reduce-scatter.13.cloned.1.call-done = bf16[384,1280]{1,0:T(8,128)(2,1)} async-done(((bf16[1536,1280]{1,0:T(8,128)(2,1)}), bf16[384,1280]{1,0:T(8,128)(2,1)}) %reduce-scatter.13.cloned.1.call-update) | async-done | bytes 983056 | tf_op jit(solution)/shard_map/reduce_scatter | solution.py:772
  920.2 141.6 %reduce-scatter.15.cloned.1.call-done = bf16[96,1536]{1,0:T(8,128)(2,1)} async-done(((bf16[1536,1536]{1,0:T(8,128)(2,1)}), bf16[96,1536]{1,0:T(8,128)(2,1)}) %reduce-scatter.15.cloned.1.call-update) | async-done | bytes 294928 | tf_op jit(solution)/shard_map/reduce_scatter | solution.py:730
  (578 shorter events, 455.5 us)
Async XLA Ops:
  7.2 105.2 %all-gather.6.cloned.1.call-start = ((), (), s32[]{:S(2)}) async-start(), calls=%async_computation.8 | async-start | bytes 4915200 | tf_op jit(solution)/shard_map/all_gather | solution.py:613
  44.5 306.6 %all-gather.8.cloned.1.call-start = ((), (), s32[]{:S(2)}) async-start(), calls=%async_computation.9 | async-start | bytes 5013504 | tf_op jit(solution)/shard_map/all_gather | solution.py:623
  50.2 36.4 %collective-permute-start = (bf16[264,1536]{1,0:T(8,128)(2,1)}, bf16[264,1536]{1,0:T(8,128)(2,1)}, u32[]{:S(2)}, u32[]{:S(2)}) collective-permute-start(bf16[264,1536]{1,0:T(8,128)(2,1)} %get-tuple-element.253), channel_id=1, source_target_pairs={{0,6},{2,0},{4,2},{6,4},{1,7},{3,1},{5,3},{7,5},{8,14},{10,8},{12,... | collective-permute-start | bytes 2433032 | tf_op jit(solution)/shard_map/ppermute | solution.py:420
  54.5 347.0 %all-gather.10.cloned.1.call-start = ((), (), s32[]{:S(2)}) async-start(), calls=%async_computation.12 | async-start | bytes 8847360 | tf_op jit(solution)/shard_map/all_gather | solution.py:639
  159.2 36.7 %collective-permute-start.7 = (bf16[4,264,1536]{2,1,0:T(8,128)(2,1)}, bf16[4,264,1536]{2,1,0:T(8,128)(2,1)}, u32[]{:S(2)}, u32[]{:S(2)}) collective-permute-start(bf16[4,264,1536]{2,1,0:T(8,128)(2,1)} %bitcast.15), channel_id=1, source_target_pairs={{0,1},{1,0},{2,3},{3,2},{4,5},{5,4},{6,7},{7,6},{8,9},{9,8},{10,11... | collective-permute-start | bytes 9732104 | tf_op jit(solution)/shard_map/ppermute | solution.py:415
  195.8 598.8 %reduce-scatter.9.cloned.1.call-start = ((), (), s32[]{:S(2)}) async-start(), calls=%async_computation.10 | async-start | bytes 1105920 | tf_op jit(solution)/shard_map/reduce_scatter | solution.py:739
  226.6 74.4 %collective-permute-start.11 = (bf16[264,1536]{1,0:T(8,128)(2,1)S(1)}, bf16[264,1536]{1,0:T(8,128)(2,1)S(1)}, u32[]{:S(2)}, u32[]{:S(2)}) collective-permute-start(bf16[264,1536]{1,0:T(8,128)(2,1)S(1)} %pad_maximum_fusion.14), channel_id=1, source_target_pairs={{0,6},{2,0},{4,2},{6,4},{1,7},{3,1},{5,3},{7,5},{8,14},{10,8},{12,... | collective-permute-start | bytes 2433032 | tf_op jit(solution)/shard_map/ppermute | solution.py:420
  234.2 67.6 %collective-permute-start.9 = (bf16[264,1536]{1,0:T(8,128)(2,1)S(1)}, bf16[264,1536]{1,0:T(8,128)(2,1)S(1)}, u32[]{:S(2)}, u32[]{:S(2)}) collective-permute-start(bf16[264,1536]{1,0:T(8,128)(2,1)S(1)} %pad_maximum_fusion.13), channel_id=1, source_target_pairs={{0,2},{2,4},{4,6},{6,0},{1,3},{3,5},{5,7},{7,1},{8,10},{10,12},{12... | collective-permute-start | bytes 2433032 | tf_op jit(solution)/shard_map/ppermute | solution.py:420
  242.1 120.7 %collective-permute-start.25 = (bf16[264,1536]{1,0:T(8,128)(2,1)}, bf16[264,1536]{1,0:T(8,128)(2,1)}, u32[]{:S(2)}, u32[]{:S(2)}) collective-permute-start(bf16[264,1536]{1,0:T(8,128)(2,1)} %get-tuple-element.261), channel_id=1, source_target_pairs={{0,16},{8,24},{16,0},{24,8},{1,17},{9,25},{17,1},{25,9},{2,18},{10... | collective-permute-start | bytes 2433032 | tf_op jit(solution)/shard_map/ppermute | solution.py:425
  243.8 121.0 %collective-permute-start.23 = (bf16[264,1536]{1,0:T(8,128)(2,1)}, bf16[264,1536]{1,0:T(8,128)(2,1)}, u32[]{:S(2)}, u32[]{:S(2)}) collective-permute-start(bf16[264,1536]{1,0:T(8,128)(2,1)} %get-tuple-element.261), channel_id=1, source_target_pairs={{0,8},{8,0},{16,24},{24,16},{1,9},{9,1},{17,25},{25,17},{2,10},{10... | collective-permute-start | bytes 2433032 | tf_op jit(solution)/shard_map/ppermute | solution.py:425
  245.3 121.3 %collective-permute-start.22 = (bf16[264,1536]{1,0:T(8,128)(2,1)}, bf16[264,1536]{1,0:T(8,128)(2,1)}, u32[]{:S(2)}, u32[]{:S(2)}) collective-permute-start(bf16[264,1536]{1,0:T(8,128)(2,1)} %get-tuple-element.261), channel_id=1, source_target_pairs={{0,1},{1,0},{2,3},{3,2},{4,5},{5,4},{6,7},{7,6},{8,9},{9,8},{10,11... | collective-permute-start | bytes 2433032 | tf_op jit(solution)/shard_map/ppermute | solution.py:415
  305.6 45.6 %collective-permute-start.12 = (bf16[264,1536]{1,0:T(8,128)(2,1)S(1)}, bf16[264,1536]{1,0:T(8,128)(2,1)}, u32[]{:S(2)}, u32[]{:S(2)}) collective-permute-start(bf16[264,1536]{1,0:T(8,128)(2,1)S(1)} %multiply_convert_fusion.1), channel_id=1, source_target_pairs={{0,1},{1,0},{2,3},{3,2},{4,5},{5,4},{6,7},{7,6},{8,9},{9,8},{10,11... | collective-permute-start | bytes 2433032 | tf_op jit(solution)/shard_map/ppermute | solution.py:415
  593.0 268.7 %reduce-scatter.11.cloned.1.call-start = ((), (), s32[]{:S(2)}) async-start(), calls=%async_computation.11 | async-start | bytes 8847360 | tf_op jit(solution)/shard_map/reduce_scatter | solution.py:705
  597.6 37.0 %collective-permute-start.45 = (bf16[264,1536]{1,0:T(8,128)(2,1)}, bf16[264,1536]{1,0:T(8,128)(2,1)S(1)}, u32[]{:S(2)}, u32[]{:S(2)}) collective-permute-start(bf16[264,1536]{1,0:T(8,128)(2,1)} %get-tuple-element.255), channel_id=1, source_target_pairs={{0,2},{2,4},{4,6},{6,0},{1,3},{3,5},{5,7},{7,1},{8,10},{10,12},{12... | collective-permute-start | bytes 2433032 | tf_op jit(solution)/shard_map/ppermute | solution.py:420
  600.2 50.0 %collective-permute-start.43 = (bf16[264,1536]{1,0:T(8,128)(2,1)}, bf16[264,1536]{1,0:T(8,128)(2,1)S(1)}, u32[]{:S(2)}, u32[]{:S(2)}) collective-permute-start(bf16[264,1536]{1,0:T(8,128)(2,1)} %get-tuple-element.255), channel_id=1, source_target_pairs={{0,6},{2,0},{4,2},{6,4},{1,7},{3,1},{5,3},{7,5},{8,14},{10,8},{12,... | collective-permute-start | bytes 2433032 | tf_op jit(solution)/shard_map/ppermute | solution.py:420
  624.4 287.1 %reduce-scatter.13.cloned.1.call-start = ((), (), s32[]{:S(2)}) async-start(), calls=%async_computation.13 | async-start | bytes 4915200 | tf_op jit(solution)/shard_map/reduce_scatter | solution.py:772
  652.7 37.3 %collective-permute-start.50 = (bf16[264,1536]{1,0:T(8,128)(2,1)S(1)}, bf16[264,1536]{1,0:T(8,128)(2,1)S(1)}, u32[]{:S(2)}, u32[]{:S(2)}) collective-permute-start(bf16[264,1536]{1,0:T(8,128)(2,1)S(1)} %collective-permute-done.45), channel_id=1, source_target_pairs={{0,1},{1,0},{2,3},{3,2},{4,5},{5,4},{6,7},{7,6},{8,9},{9,8},{10,11... | collective-permute-start | bytes 2433032 | tf_op jit(solution)/shard_map/ppermute | solution.py:415
  749.4 39.5 %collective-permute-start.54 = (bf16[264,768]{1,0:T(8,128)(2,1)S(1)}, bf16[264,768]{1,0:T(8,128)(2,1)S(1)}, u32[]{:S(2)}, u32[]{:S(2)}) collective-permute-start(bf16[264,768]{1,0:T(8,128)(2,1)S(1)} %get-tuple-element.291), channel_id=1, source_target_pairs={{0,6},{2,0},{4,2},{6,4},{1,7},{3,1},{5,3},{7,5},{8,14},{10,8},{12,... | collective-permute-start | bytes 1216520 | tf_op jit(solution)/shard_map/ppermute | solution.py:420
  750.3 39.6 %collective-permute-start.52 = (bf16[264,768]{1,0:T(8,128)(2,1)S(1)}, bf16[264,768]{1,0:T(8,128)(2,1)S(1)}, u32[]{:S(2)}, u32[]{:S(2)}) collective-permute-start(bf16[264,768]{1,0:T(8,128)(2,1)S(1)} %get-tuple-element.290), channel_id=1, source_target_pairs={{0,2},{2,4},{4,6},{6,0},{1,3},{3,5},{5,7},{7,1},{8,10},{10,12},{12... | collective-permute-start | bytes 1216520 | tf_op jit(solution)/shard_map/ppermute | solution.py:420
  790.9 44.2 %collective-permute-start.53 = (bf16[264,1536]{1,0:T(8,128)(2,1)}, bf16[264,1536]{1,0:T(8,128)(2,1)S(1)}, u32[]{:S(2)}, u32[]{:S(2)}) collective-permute-start(bf16[264,1536]{1,0:T(8,128)(2,1)} %pad_maximum_fusion.22), channel_id=1, source_target_pairs={{0,2},{2,4},{4,6},{6,0},{1,3},{3,5},{5,7},{7,1},{8,10},{10,12},{12... | collective-permute-start | bytes 2433032 | tf_op jit(solution)/shard_map/ppermute | solution.py:420
  845.8 216.0 %reduce-scatter.15.cloned.1.call-start = ((), (), s32[]{:S(2)}) async-start(), calls=%async_computation.14 | async-start | bytes 5013504 | tf_op jit(solution)/shard_map/reduce_scatter | solution.py:730
  865.3 215.6 %collective-permute-start.35 = (bf16[264,1536]{1,0:T(8,128)(2,1)}, bf16[264,1536]{1,0:T(8,128)(2,1)}, u32[]{:S(2)}, u32[]{:S(2)}) collective-permute-start(bf16[264,1536]{1,0:T(8,128)(2,1)} %get-tuple-element.285), channel_id=1, source_target_pairs={{0,1},{1,0},{2,3},{3,2},{4,5},{5,4},{6,7},{7,6},{8,9},{9,8},{10,11... | collective-permute-start | bytes 2433032 | tf_op jit(solution)/shard_map/ppermute | solution.py:415
  911.5 163.8 %all-to-all-start.2 = ((bf16[4,96,1280]{2,1,0:T(8,128)(2,1)}), bf16[4,96,1280]{2,1,0:T(8,128)(2,1)S(1)}, u32[]{:S(2)}, u32[]{:S(2)}) async-start(bf16[4,96,1280]{2,1,0:T(8,128)(2,1)} %bitcast.304), calls=%async_computation.3 | async-start | bytes 1966080 | tf_op jit(solution)/shard_map/all_to_all | solution.py:773
  920.2 167.2 %collective-permute-start.56 = (f32[264,1536]{1,0:T(8,128)}, f32[264,1536]{1,0:T(8,128)}, u32[]{:S(2)}, u32[]{:S(2)}) collective-permute-start(f32[264,1536]{1,0:T(8,128)} %fusion.26), channel_id=1, source_target_pairs={{0,1},{1,0},{2,3},{3,2},{4,5},{5,4},{6,7},{7,6},{8,9},{9,8},{10,11... | collective-permute-start | bytes 4866056 | tf_op jit(solution)/shard_map/ppermute | solution.py:415
  (148 other events, 2066.8 us)
Sparse Core Ops, SparseCore 0:
  44.7 49.6 all-gather.5
  97.7 80.4 all-gather.7
  196.0 185.4 all-gather.9
  593.1 47.0 reduce-scatter.8
  642.4 162.7 reduce-scatter.10
  845.9 65.5 reduce-scatter.12
  916.7 145.1 reduce-scatter.14

commit v2 on v1

--- a/solution.py
+++ b/solution.py
@@ -11,6 +11,7 @@
 ROT = 32
 STEP = 7
 LANES = 128
+MOST_BLOCKS = 8
 
 
 norm_eps = 1e-05
@@ -78,58 +79,76 @@
     )
 
 
-def project_kernel(
-    wide, scale, x_ref, gain_ref, w_ref, cos_ref, up_ref, down_ref, a_ref, qkv_ref
-):
-    plain, _ = norm_parts(x_ref[...].astype(fl))
+def pick(step, refs, held):
+    for k, ref in enumerate(refs):
+
+        @pl.when(step == k)
+        def _(ref=ref):
+            held[...] = ref[...]
+
+
+def one_buffer(shape):
+    return pl.BlockSpec(
+        shape, lambda *index: (0,) * len(shape), pipeline_mode=pl.Buffered(buffer_count=1)
+    )
+
+
+def stacked(shape):
+    return pl.BlockSpec((1,) + shape, lambda i: (i, 0, 0))
+
+
+def project_kernel(count, few, scale, *refs):
+    x_refs = refs[:count]
+    gain_ref, w_ref, cos_ref, up_ref, down_ref, a_ref, qkv_ref, held = refs[count:]
+    pick(pl.program_id(0), x_refs, held)
+    plain, _ = norm_parts(held[...].astype(fl))
     rows = (plain * gain_ref[...]).astype(bf)
-    a_ref[...] = rows
-    projected = matmul(rows, w_ref[...])
-    cosine, up, down = cos_ref[...], up_ref[...], down_ref[...]
-    for start in range(0, 2 * wide, LANES):
+    a_ref[0] = rows
+    projected = matmul(rows, w_ref[:, : 3 * few])
+    cosine, up, down = cos_ref[0], up_ref[0], down_ref[0]
+    lane = lax.broadcasted_iota(jnp.int32, cosine.shape, 1)
+    for start in range(0, 2 * few, LANES):
         turned = turn(projected[:, start : start + LANES], cosine, up, down)
-        if start < wide:
-            turned = turned * scale
-        qkv_ref[:, start : start + LANES] = turned.astype(bf)
-    qkv_ref[:, 2 * wide :] = projected[:, 2 * wide :].astype(bf)
-
-
-def project(x, gain, weight, tables, scale, block):
-    rows, width = x.shape
-    wide = weight.shape[1] // 3
-    cosine, up, down = tables
-    by_rows = lambda lanes: pl.BlockSpec((block, lanes), lambda i: (i, 0))
+        if start < few:
+            turned = jnp.where(lane < few - start, turned * scale, turned)
+        qkv_ref[0, :, start : start + LANES] = turned.astype(bf)
+    qkv_ref[0, :, 2 * few :] = projected[:, 2 * few :].astype(bf)
+
+
+def project(blocks, gain, weight, tables, scale, few):
+    count = len(blocks)
+    rows, width = blocks[0].shape
+    used = -(-3 * few // LANES) * LANES
     return pl.pallas_call(
-        functools.partial(project_kernel, wide, scale),
-        grid=(rows // block,),
-        in_specs=[
-            by_rows(width),
+        functools.partial(project_kernel, count, few, scale),
+        grid=(count,),
+        in_specs=[one_buffer((rows, width))] * count
+        + [
             whole((1, width)),
-            whole(weight.shape),
-            by_rows(LANES),
-            by_rows(LANES),
-            by_rows(LANES),
-        ],
-        out_specs=[by_rows(width), by_rows(3 * wide)],
+            one_buffer((width, used)),
+            stacked((rows, LANES)),
+            stacked((rows, LANES)),
+            stacked((rows, LANES)),
+        ],
+        out_specs=[stacked((rows, width)), stacked((rows, 3 * few))],
         out_shape=[
-            jax.ShapeDtypeStruct((rows, width), bf),
-            jax.ShapeDtypeStruct((rows, 3 * wide), bf),
-        ],
+            jax.ShapeDtypeStruct((count, rows, width), bf),
+            jax.ShapeDtypeStruct((count, rows, 3 * few), bf),
+        ],
+        scratch_shapes=[pltpu.VMEM((rows, width), bf)],
         compiler_params=params(48),
         cost_estimate=pl.CostEstimate(
-            flops=2 * rows * width * 3 * wide,
-            bytes_accessed=4 * rows * width + 2 * rows * 3 * wide,
+            flops=2 * count * rows * width * 4 * few,
+            bytes_accessed=count * rows * (4 * width + 6 * few),
             transcendentals=0,
         ),
         name="project",
-    )(x, gain, weight, cosine, up, down)
+    )(*blocks, gain, weight, *(table.reshape(count, rows, LANES) for table in tables))
 
 
 def attend_kernel(heads, wide, block, qkv_ref, mask_ref, o_ref, lse_ref):
     mask = mask_ref[:, 0:1] > 0.5
     total = qkv_ref.shape[0]
-    if heads * HD < wide:
-        o_ref[:, heads * HD :] = jnp.zeros((total, wide - heads * HD), bf)
     for h in range(heads):
         low, high = h * HD, (h + 1) * HD
         keys = qkv_ref[:, wide + low : wide + high]
@@ -184,11 +203,6 @@
     mask = mask_ref[:, 0:1] > 0.5
     total = qkv_ref.shape[0]
     ones = jnp.ones((8, HD), fl)
-    if heads * HD < wide:
-        for part in range(3):
-            work_ref[:, part * wide + heads * HD : (part + 1) * wide] = jnp.zeros(
-                (total, wide - heads * HD), fl
-            )
     for h in range(heads):
         low, high = h * HD, (h + 1) * HD
         keys = qkv_ref[:, wide + low : wide + high]
@@ -366,49 +380,168 @@
     )(queries, pairs, grads, mixed, lse, mask)
 
 
-def mlp_kernel(a_ref, dy_ref, w_ref, h_ref, dgu_ref, out_ref, da_ref):
-    units = h_ref.shape[1]
-    rows = a_ref[...]
-    gate = matmul(rows, w_ref[:, :units])
-    upward = matmul(rows, w_ref[:, units : 2 * units])
+def mix_back_kernel(count, *refs):
+    g_refs = refs[:count]
+    w_ref, o_ref, do_ref, grad_ref, held, total = refs[count:]
+    step = pl.program_id(0)
+    few = o_ref.shape[2]
+
+    @pl.when(step == 0)
+    def _():
+        total[...] = jnp.zeros_like(total)
+
+    pick(step, g_refs, held)
+    rows = held[...]
+    do_ref[0] = matmul(rows, w_ref[:, :few]).astype(bf)
+    total[...] += matmul(flip(o_ref[0]).astype(bf), rows)
+
+    @pl.when(step == count - 1)
+    def _():
+        grad_ref[...] = total[...].T.astype(bf)
+
+
+def mix_back(blocks, weight, mixed):
+    count = len(blocks)
+    rows, width = blocks[0].shape
+    few = mixed.shape[2]
+    return pl.pallas_call(
+        functools.partial(mix_back_kernel, count),
+        grid=(count,),
+        in_specs=[one_buffer((rows, width))] * count
+        + [one_buffer(weight.shape), stacked((rows, few))],
+        out_specs=[stacked((rows, few)), whole((width, few))],
+        out_shape=[
+            jax.ShapeDtypeStruct((count, rows, few), bf),
+            jax.ShapeDtypeStruct((width, few), bf),
+        ],
+        scratch_shapes=[pltpu.VMEM((rows, width), bf), pltpu.VMEM((few, width), fl)],
+        compiler_params=params(48),
+        cost_estimate=pl.CostEstimate(
+            flops=4 * count * rows * width * 256,
+            bytes_accessed=2 * count * rows * (width + 2 * few) + 8 * width * few,
+            transcendentals=0,
+        ),
+        name="mix_back",
+    )(*blocks, weight, mixed)
+
+
+def mlp_kernel(count, given, *refs):
+    a_refs, dy_refs = refs[:given], refs[given : 2 * given]
+    (
+        gate_ref,
+        up_ref,
+        down_ref,
+        a_ref,
+        dy_ref,
+        h_ref,
+        dgu_ref,
+        out_other,
+        out_own,
+        da_other,
+        da_own,
+        weight,
+        a_held,
+        dy_held,
+    ) = refs[2 * given :]
+    step = pl.program_id(0)
+    ctxs, shards, owned, units = gate_ref.shape
+
+    @pl.when(step == 0)
+    def _():
+        for s in range(shards):
+            for c in range(ctxs):
+                row = (s * ctxs + c) * owned
+                for k, kind in enumerate((gate_ref, up_ref, down_ref)):
+                    weight[row : row + owned, k * units : (k + 1) * units] = kind[c, s]
+
+    if given == count:
+        pick(step, a_refs, a_held)
+        pick(step, dy_refs, dy_held)
+    else:
+        a_held[...] = a_refs[0][0]
+        dy_held[...] = dy_refs[0][0]
+    rows = a_held[...]
+    grads = dy_held[...]
+    a_ref[0] = rows
+    dy_ref[0] = grads
+    gate = matmul(rows, weight[:, :units])
+    upward = matmul(rows, weight[:, units : 2 * units])
     sigmoid = jax.nn.sigmoid(gate)
     activated = gate * sigmoid
     hidden = (activated * upward).astype(bf)
-    h_ref[...] = hidden
-    grad_hidden = matmul(dy_ref[...], w_ref[:, 2 * units :])
+    h_ref[0] = hidden
+    grad_hidden = matmul(grads, weight[:, 2 * units :])
     grad_gate = (grad_hidden * upward * sigmoid * (1.0 + gate * (1.0 - sigmoid))).astype(bf)
     grad_up = (grad_hidden * activated).astype(bf)
-    dgu_ref[:, :units] = grad_gate
-    dgu_ref[:, units:] = grad_up
-    da_ref[...] = (
-        matmul_t(grad_gate, w_ref[:, :units]) + matmul_t(grad_up, w_ref[:, units : 2 * units])
+    dgu_ref[0, :, :units] = grad_gate
+    dgu_ref[0, :, units:] = grad_up
+    da = (
+        matmul_t(grad_gate, weight[:, :units]) + matmul_t(grad_up, weight[:, units : 2 * units])
     ).astype(bf)
-    out_ref[...] = matmul_t(hidden, w_ref[:, 2 * units :]).astype(bf)
-
-
-def mlp(rows, grads, weight, block):
-    count, width = rows.shape
-    units = weight.shape[1] // 3
-    by_rows = lambda lanes: pl.BlockSpec((block, lanes), lambda i: (i, 0))
+    out = matmul_t(hidden, weight[:, 2 * units :]).astype(bf)
+
+    @pl.when(step < count // 2)
+    def _():
+        da_other[0] = da
+        out_other[0] = out
+
+    @pl.when(step >= count // 2)
+    def _():
+        da_own[0] = da
+        out_own[0] = out
+
+
+def mlp(blocks, grads, weights):
+    count = len(blocks)
+    half = count // 2
+    rows, width = blocks[0].shape
+    units = weights[0].shape[3]
+    if count <= MOST_BLOCKS:
+        feeds = one_buffer((rows, width))
+    else:
+        feeds = stacked((rows, width))
+        blocks, grads = [jnp.stack(blocks)], [jnp.stack(grads)]
+    given = len(blocks)
+    first = pl.BlockSpec((1, rows, width), lambda i: (jnp.minimum(i, half - 1), 0, 0))
+    second = pl.BlockSpec((1, rows, width), lambda i: (jnp.maximum(i - half, 0), 0, 0))
     return pl.pallas_call(
-        mlp_kernel,
-        grid=(count // block,),
-        in_specs=[by_rows(width), by_rows(width), whole(weight.shape)],
-        out_specs=[by_rows(units), by_rows(2 * units), by_rows(width), by_rows(width)],
+        functools.partial(mlp_kernel, count, given),
+        grid=(count,),
+        in_specs=[feeds] * (2 * given) + [one_buffer(weights[0].shape)] * 3,
+        out_specs=[
+            stacked((rows, width)),
+            stacked((rows, width)),
+            stacked((rows, units)),
+            stacked((rows, 2 * units)),
+            first,
+            second,
+            first,
+            second,
+        ],
         out_shape=[
-            jax.ShapeDtypeStruct((count, units), bf),
-            jax.ShapeDtypeStruct((count, 2 * units), bf),
-            jax.ShapeDtypeStruct((count, width), bf),
-            jax.ShapeDtypeStruct((count, width), bf),
-        ],
-        compiler_params=params(56),
+            jax.ShapeDtypeStruct((count, rows, width), bf),
+            jax.ShapeDtypeStruct((count, rows, width), bf),
+            jax.ShapeDtypeStruct((count, rows, units), bf),
+            jax.ShapeDtypeStruct((count, rows, 2 * units), bf),
+        ]
+        + [jax.ShapeDtypeStruct((half, rows, width), bf)] * 4,
+        scratch_shapes=[
+            pltpu.VMEM((width, 3 * units), bf),
+            pltpu.VMEM((rows, width), bf),
+            pltpu.VMEM((rows, width), bf),
+        ],
+        compiler_params=params(60),
         cost_estimate=pl.CostEstimate(
-            flops=12 * count * width * units,
-            bytes_accessed=2 * count * (4 * width + 3 * units) + 6 * width * units,
-            transcendentals=count * units,
+            flops=12 * count * rows * width * units,
+            bytes_accessed=2 * count * rows * (6 * width + 3 * units) + 6 * width * units,
+            transcendentals=count * rows * units,
         ),
         name="mlp",
-    )(rows, grads, weight)
+    )(*blocks, *grads, *weights)
+
+
+def after(value, *others):
+    return lax.optimization_barrier((value,) + others)[0]
 
 
 def swap(value):
@@ -425,64 +558,94 @@
     return lax.ppermute(value, "shard", [(i, i ^ bits) for i in range(size)])
 
 
-def ring_gather(own):
-    if lax.axis_size("ctx") != 4:
-        return [own] + [ring_shift(own, r) for r in range(1, lax.axis_size("ctx"))]
+def ring_gather(own, first=(), second=()):
+    size = lax.axis_size("ctx")
+    if size != 4:
+        return [own] + [after(ring_shift(own, r), *second) for r in range(1, size)]
     half = own.shape[-1] // 2
-    after = ring_shift(own, 1)
-    before = ring_shift(own, -1)
+    following = after(ring_shift(own, 1), *first)
+    before = after(ring_shift(own, -1), *first)
     far = jnp.concatenate(
-        [ring_shift(after[:, :half], 1), ring_shift(before[:, half:], -1)], axis=-1
-    )
-    return [own, after, far, before]
-
-
-def ring_scatter(parts):
+        [
+            after(ring_shift(following[:, :half], 1), *second),
+            after(ring_shift(before[:, half:], -1), *second),
+        ],
+        axis=-1,
+    )
+    return [own, following, far, before]
+
+
+def ring_scatter(parts, first=(), second=()):
     if lax.axis_size("ctx") != 4:
         total = parts[0].astype(fl)
         for r in range(1, len(parts)):
-            total = total + ring_shift(parts[r], -r).astype(fl)
+            total = total + after(ring_shift(parts[r], -r), *second).astype(fl)
         return total
     half = parts[0].shape[-1] // 2
-    by_after = ring_shift(parts[2][:, :half], -1)
-    by_before = ring_shift(parts[2][:, half:], 1)
+    by_after = after(ring_shift(parts[2][:, :half], -1), *first)
+    by_before = after(ring_shift(parts[2][:, half:], 1), *first)
     to_after = jnp.concatenate([parts[1][:, :half] + by_after, parts[1][:, half:]], axis=-1)
     to_before = jnp.concatenate([parts[3][:, :half], parts[3][:, half:] + by_before], axis=-1)
-    return (
-        parts[0].astype(fl)
-        + ring_shift(to_after, -1).astype(fl)
-        + ring_shift(to_before, 1).astype(fl)
-    )
-
-
-def square_gather(own):
+    from_before = after(ring_shift(to_after, -1), *second)
+    from_after = after(ring_shift(to_before, 1), *second)
+    return parts[0].astype(fl) + from_before.astype(fl) + from_after.astype(fl)
+
+
+def ring_exchange(parts):
+    return [parts[0]] + [ring_shift(part, -r) for r, part in enumerate(parts[1:], 1)]
+
+
+def square_exchange(parts):
+    return [parts[0]] + [cross_over(part, r) for r, part in enumerate(parts[1:], 1)]
+
+
+def at(array, index):
+    return lax.dynamic_index_in_dim(array, index, 0, keepdims=False)
+
+
+def rows_at(array, index, count):
+    return lax.dynamic_slice_in_dim(array, index * count, count, 0)
+
+
+def place(blocks, indices):
+    out = jnp.zeros((len(blocks),) + blocks[0].shape, blocks[0].dtype)
+    for block, index in zip(blocks, indices):
+        out = lax.dynamic_update_index_in_dim(out, block, index, 0)
+    return out
+
+
+def square_gather(own, first=(), second=()):
     size = lax.axis_size("shard")
     if size != 4:
-        every = lax.all_gather(own, "shard", axis=0, tiled=False)
-        return [every[i] for i in range(size)]
+        return [own] + [after(cross_over(own, r), *second) for r in range(1, size)]
     half = own.shape[-1] // 2
-    one = cross_over(own, 1)
-    two = cross_over(own, 2)
-    three = jnp.concatenate([cross_over(two[:, :half], 1), cross_over(one[:, half:], 2)], axis=-1)
+    one = after(cross_over(own, 1), *first)
+    two = after(cross_over(own, 2), *first)
+    three = jnp.concatenate(
+        [
+            after(cross_over(two[:, :half], 1), *second),
+            after(cross_over(one[:, half:], 2), *second),
+        ],
+        axis=-1,
+    )
     return [own, one, two, three]
 
 
-def square_scatter(parts):
+def square_scatter(parts, first=(), second=()):
     size = lax.axis_size("shard")
     if size != 4:
-        return lax.psum_scatter(
-            jnp.concatenate(parts, axis=0), "shard", scatter_dimension=0, tiled=True
-        ).astype(fl)
+        total = parts[0].astype(fl)
+        for r in range(1, size):
+            total = total + after(cross_over(parts[r], r), *second).astype(fl)
+        return total
     half = parts[0].shape[-1] // 2
-    by_one = cross_over(parts[3][:, :half], 1)
-    by_two = cross_over(parts[3][:, half:], 2)
+    by_one = after(cross_over(parts[3][:, :half], 1), *first)
+    by_two = after(cross_over(parts[3][:, half:], 2), *first)
     to_two = jnp.concatenate([parts[2][:, :half] + by_one, parts[2][:, half:]], axis=-1)
     to_one = jnp.concatenate([parts[1][:, :half], parts[1][:, half:] + by_two], axis=-1)
-    return (
-        parts[0].astype(fl)
-        + cross_over(to_one, 1).astype(fl)
-        + cross_over(to_two, 2).astype(fl)
-    )
+    from_one = after(cross_over(to_one, 1), *second)
+    from_two = after(cross_over(to_two, 2), *second)
+    return parts[0].astype(fl) + from_one.astype(fl) + from_two.astype(fl)
 
 
 def total_over_all(value):
@@ -554,6 +717,7 @@
     scale = HD ** (-0.5)
     shards = lax.axis_size("shard")
     ctxs = lax.axis_size("ctx")
+    shard_index = lax.axis_index("shard")
     ctx_index = lax.axis_index("ctx")
     tp_index = lax.axis_index("tp")
     owned = qkv_weight.shape[0]
@@ -561,7 +725,6 @@
     units_half = down_weight.shape[1]
     few = local_width // ctxs
     heads_few = few // HD
-    wide = -(-few // LANES) * LANES
     units = units_half // shards
 
     latent_order = (tp_index + jnp.arange(seqs, dtype=jnp.int32)) % seqs
@@ -580,18 +743,13 @@
     positions = (starts_here[:, None, None] + offsets_here[:, :, None] + slot).reshape(-1)
     key_valid = (slot < lengths_here[:, :, None]).reshape(-1)
     key_mask = jnp.broadcast_to(key_valid.astype(fl)[:, None], (key_valid.shape[0], LANES))
-    tables = rotary_tables(positions)
+    tables = lax.optimization_barrier(rotary_tables(positions))
     own_valid = (slot < lengths_here[0, 0]).astype(fl)[:, None]
 
     tokens_mine = mine(tokens)
     tokens_other = others(tokens)
-    token_blocks = ring_gather(tokens_mine)
-    token_swapped = [tokens_other] + [swap(block) for block in token_blocks[1:]]
-    tokens_all = jnp.concatenate(token_blocks + token_swapped, axis=0)
     dy_mine = mine(cotangent).astype(fl) * own_valid
     dy_low = dy_mine.astype(bf)
-    dy_blocks = square_gather(dy_low)
-    dy_all = jnp.concatenate([b for block in dy_blocks for b in (block, swap(block))], axis=0)
 
     kinds = jnp.concatenate(
         [
@@ -609,59 +767,79 @@
     sent_attn = jnp.concatenate(
         [kinds, jnp.broadcast_to(gain_lanes[None], (ctxs, owned, LANES))], axis=2
     )
-    sent_attn = lax.all_to_all(sent_attn, "ctx", 0, 0, tiled=True)
-    attn_full = lax.all_gather(
-        sent_attn.reshape(ctxs * owned, -1), "shard", axis=0, tiled=True
-    )
-    weight_of = lambda kind: attn_full[:, kind * few : (kind + 1) * few]
-    padded = lambda array: jnp.pad(array, ((0, 0), (0, wide - few)))
-    qkv_wide = jnp.concatenate([padded(weight_of(kind)) for kind in range(3)], axis=1)
-    output_wide = padded(weight_of(3))
+    sent_attn = after(sent_attn, tokens_mine)
+    ctx_after = [(ctx_index + r) % ctxs for r in range(ctxs)]
+    ctx_before = [(ctx_index - r) % ctxs for r in range(ctxs)]
+    shard_near = [shard_index ^ r for r in range(shards)]
+    attn_rows = place(
+        ring_exchange([at(sent_attn, index) for index in ctx_after]), ctx_before
+    ).reshape(ctxs * owned, -1)
+    attn_full = lax.all_gather(attn_rows, "shard", axis=0, tiled=True)
     pair_full = attn_full[:, 4 * few : 6 * few]
+    output_full = attn_full[:, 3 * few : 4 * few]
     gains = jnp.transpose(attn_full[:, n_kinds * few : n_kinds * few + 3].astype(fl))
 
-    cross_full = lax.all_gather(
-        jnp.concatenate([cross_query_weight.astype(bf), cross_out_weight.astype(bf)], axis=1),
-        ("shard", "ctx"),
-        axis=0,
-        tiled=True,
-    )
+    sent_mlp = jnp.concatenate(
+        [gate_up_weight.astype(bf), down_weight.astype(bf)[:, None]], axis=1
+    )
+    sent_mlp = jnp.transpose(sent_mlp.reshape(owned, 3, shards, units), (2, 0, 1, 3)).reshape(
+        shards, owned, 3 * units
+    )
+    sent_mlp = place(
+        square_exchange([at(sent_mlp, index) for index in shard_near]), shard_near
+    )
+    token_blocks = ring_gather(tokens_mine)
+    sent_mlp = after(sent_mlp, token_blocks[2], attn_rows)
+    over_ctx = lambda array: lax.all_gather(array, "ctx", axis=0, tiled=False)
+    gate_full = over_ctx(sent_mlp[:, :, :units])
+    up_full = over_ctx(sent_mlp[:, :, units : 2 * units])
+
+    token_swapped = [tokens_other] + [swap(block) for block in token_blocks[1:]]
+    token_last = after(token_swapped[-1], sent_mlp)
+
+    total = pieces * cap
+    block = total // 3
+    sent_cross = jnp.concatenate(
+        [cross_query_weight.astype(bf), cross_out_weight.astype(bf)], axis=1
+    )
+    sent_cross = after(sent_cross, token_blocks[2])
+    input1, qkv = project(
+        token_blocks + token_swapped[:-1] + [token_last], gains[0:1], attn_full, tables, scale, few
+    )
+    qkv = qkv.reshape(seqs * total, 3 * few)
+    cond_up = -(-cond_len // 16) * 16
+    cond_rows = jnp.pad(both(conditioning), ((0, 0), (0, cond_up - cond_len), (0, 0))).reshape(
+        seqs * cond_up, width
+    )
+    own_pairs = after(matmul(cond_rows, pair_full).astype(bf), qkv)
+    mixed_low, lse = attend(qkv, key_mask, seqs, heads_few, block)
+    cross_blocks = ring_gather(sent_cross, (qkv,), (mixed_low,))
+    partial = matmul_t(mixed_low, output_full).astype(bf).reshape(seqs, pieces, cap, width)
+    from_other = swap(partial[1])
+    mine_parts = [partial[0, r] + from_other[r] for r in range(pieces)]
+    pairs = place(
+        [own_pairs]
+        + [after(ring_shift(own_pairs, r), mine_parts[0]) for r in range(1, ctxs)],
+        ctx_after,
+    )
+    pairs = jnp.transpose(
+        pairs.reshape(ctxs, seqs, cond_up, 2, few), (1, 2, 3, 0, 4)
+    ).reshape(seqs, cond_up, 2 * local_width)
+    cross_rows = place(cross_blocks, ctx_after).reshape(ctxs * owned, -1)
+    cross_full = place(square_gather(cross_rows, (mine_parts[0],)), shard_near).reshape(width, -1)
     query_full = cross_full[:, :local_width]
     cross_out_full = cross_full[:, local_width:]
-
-    sent_mlp = jnp.concatenate(
-        [gate_up_weight.astype(bf), down_weight.astype(bf)[:, None]], axis=1
-    )
-    sent_mlp = jnp.transpose(sent_mlp.reshape(owned, 3, shards, units), (2, 0, 1, 3)).reshape(
-        shards, owned, 3 * units
-    )
-    sent_mlp = lax.all_to_all(sent_mlp, "shard", 0, 0, tiled=True)
-    mlp_full = lax.all_gather(sent_mlp, "ctx", axis=0, tiled=False)
-    mlp_full = jnp.transpose(mlp_full, (1, 0, 2, 3)).reshape(width, 3 * units)
-
-    total = pieces * cap
-    block = total // 3
-    input1, qkv = project(tokens_all, gains[0:1], qkv_wide, tables, scale, block)
-    mixed_low, lse = attend(qkv, key_mask, seqs, heads_few, block)
-    partial = matmul_t(mixed_low, output_wide).astype(bf).reshape(seqs, pieces, cap, width)
-    from_other = swap(partial[1])
-    mine_parts = [partial[0, r] + from_other[r] for r in range(pieces)]
     x_rows = tokens_mine.astype(fl)
-    x_first = x_rows + ring_scatter(mine_parts)
+    x_first = x_rows + ring_scatter(mine_parts, (), (pairs, cross_full))
+    dy_low = after(dy_low, cross_full)
+    dy_blocks = square_gather(dy_low, (x_first,), (x_first,))
+    dy_swapped = [swap(block_of) for block_of in dy_blocks]
+    down_full = over_ctx(after(sent_mlp[:, :, 2 * units :], x_first))
 
     plain2, inverse2 = norm_parts(x_first)
     input2_mine = (plain2 * gains[1]).astype(bf)
     input2 = jnp.concatenate([input2_mine, swap(input2_mine)], axis=0)
     cross_queries = matmul(input2, query_full).astype(bf).reshape(seqs, cap, local_width)
-    cond_up = -(-cond_len // 16) * 16
-    cond_rows = jnp.pad(both(conditioning), ((0, 0), (0, cond_up - cond_len), (0, 0))).reshape(
-        seqs * cond_up, width
-    )
-    own_pairs = matmul(cond_rows, pair_full).astype(bf)
-    pairs = lax.all_gather(own_pairs, "ctx", axis=0, tiled=False)
-    pairs = jnp.transpose(
-        pairs.reshape(ctxs, seqs, cond_up, 2, few), (1, 2, 3, 0, 4)
-    ).reshape(seqs, cond_up, 2 * local_width)
     cond_valid = jnp.arange(cond_up, dtype=jnp.int32)[None, :] < both(cond_counts)[:, None]
     cond_mask = jnp.broadcast_to(cond_valid.astype(fl)[:, :, None], (seqs, cond_up, LANES))
     cross_low, cross_lse = cross(cross_queries, pairs, cond_mask, scale)
@@ -673,21 +851,34 @@
 
     plain3, inverse3 = norm_parts(x_second)
     input3 = (plain3 * gains[2]).astype(bf)
-    input3_all = jnp.concatenate(
-        [b for block in square_gather(input3) for b in (block, swap(block))], axis=0
-    )
-    hidden, grad_gated, down_partial, back_partial = mlp(
-        input3_all, dy_all, mlp_full, (shards * seqs * cap) // (6 * shards // 4)
-    )
-
-    def scatter_rows(partial_rows):
-        parts = partial_rows.reshape(shards, seqs, cap, width)
-        from_other = swap(parts[:, 1])
-        return square_scatter([parts[r, 0] + from_other[r] for r in range(shards)])
-
-    back3, grad_gain3 = norm_back(scatter_rows(back_partial), plain3, inverse3, gains[2])
-    block_mine = (x_second + scatter_rows(down_partial)).astype(bf)
-    block_other = swap(block_mine)
+    input3_blocks = square_gather(input3)
+    (
+        input3_all,
+        dy_all,
+        hidden,
+        grad_gated,
+        down_other,
+        down_own,
+        back_other,
+        back_own,
+    ) = mlp(
+        [swap(block_of) for block_of in input3_blocks] + input3_blocks,
+        dy_swapped + dy_blocks,
+        (gate_full, up_full, down_full),
+    )
+    merged = lambda array: array.reshape(-1, array.shape[-1])
+    grad_down = contract_rows(merged(dy_all), merged(hidden)).astype(bf)
+    grad_gate = contract_rows(merged(input3_all), merged(grad_gated)[:, :units]).astype(bf)
+    grad_up = contract_rows(merged(input3_all), merged(grad_gated)[:, units:]).astype(bf)
+
+    def add_cores(own, other):
+        from_other = swap(other)
+        return [own[r] + from_other[r] for r in range(own.shape[0])]
+
+    back_sum = square_scatter(
+        add_cores(back_own, back_other), (grad_down,), (grad_gate, grad_up)
+    )
+    back3, grad_gain3 = norm_back(back_sum, plain3, inverse3, gains[2])
 
     def natural(first, second):
         straight = tp_index == 0
@@ -695,20 +886,14 @@
             [jnp.where(straight, first, second), jnp.where(straight, second, first)]
         )
 
-    block_out = natural(block_mine, block_other)
-    grad_gate_up = contract_rows(input3_all, grad_gated).astype(bf)
-    grad_down = contract_rows(dy_all, hidden).astype(bf)
-    grad_mlp = jnp.concatenate([grad_gate_up, grad_down], axis=1)
-    grad_mlp = jnp.transpose(
-        grad_mlp.reshape(shards, ctxs, owned, 3 * units), (1, 0, 2, 3)
-    ).reshape(ctxs * shards * owned, 3 * units)
-    own_mlp = lax.psum_scatter(grad_mlp, "ctx", scatter_dimension=0, tiled=True)
-    own_mlp = lax.all_to_all(
-        own_mlp.reshape(shards, owned, 3 * units), "shard", 0, 0, tiled=True
-    )
-    own_mlp = jnp.transpose(own_mlp.reshape(shards, owned, 3, units), (1, 2, 0, 3)).reshape(
-        owned, 3, units_half
-    )
+    def sum_over_ctx(array):
+        by_owner = jnp.transpose(
+            array.reshape(shards, ctxs, owned, array.shape[1]), (1, 0, 2, 3)
+        ).reshape(ctxs * shards * owned, -1)
+        return lax.psum_scatter(by_owner, "ctx", scatter_dimension=0, tiled=True)
+
+    sum_down = sum_over_ctx(grad_down)
+    sum_gate = sum_over_ctx(grad_gate)
 
     grad_second = dy_mine + back3
     grad2_mine = grad_second.astype(bf)
@@ -727,68 +912,98 @@
         inverse2,
         gains[1],
     )
-    own_cross = lax.psum_scatter(
-        jnp.concatenate([grad_query.astype(bf), grad_cross_out.astype(bf)], axis=1),
-        ("shard", "ctx"),
-        scatter_dimension=0,
-        tiled=True,
-    ).astype(fl)
+    grad_cross = jnp.concatenate([grad_query.astype(bf), grad_cross_out.astype(bf)], axis=1)
     grad_pairs = jnp.transpose(
         grad_pairs.reshape(seqs, cond_up, 2, ctxs, few), (3, 0, 1, 2, 4)
-    ).reshape(ctxs * seqs * cond_up, 2 * few)
-    own_pair_grads = lax.psum_scatter(grad_pairs, "ctx", scatter_dimension=0, tiled=True)
-    grad_pair = contract_rows(cond_rows, own_pair_grads)
+    ).reshape(ctxs, seqs * cond_up, 2 * few)
 
     grad_first = grad_second + back2
     grad1_mine = grad_first.astype(bf)
     grad1_blocks = ring_gather(grad1_mine)
-    grad1_low = jnp.concatenate(
-        grad1_blocks + [swap(block) for block in grad1_blocks], axis=0
-    )
-    grad_output = contract_rows(grad1_low, mixed_low)
-    grad_mixed = matmul(grad1_low, output_wide).astype(bf)
+    grad_cross = after(grad_cross, grad1_mine)
+    cross_sum = square_scatter(
+        [rows_at(grad_cross, index, ctxs * owned) for index in shard_near]
+    ).astype(bf)
+    grad_mixed, grad_output = mix_back(
+        grad1_blocks + [swap(block_of) for block_of in grad1_blocks],
+        output_full,
+        mixed_low.reshape(seqs * pieces, cap, few),
+    )
+    sum_up = sum_over_ctx(after(grad_up, grad1_blocks[2]))
     grad_projected = attend_back(
-        qkv, grad_mixed, mixed_low, lse, key_mask, tables, seqs, heads_few, block, scale
-    )
-    first_partial = matmul_t(grad_projected, qkv_wide).astype(bf).reshape(
+        qkv,
+        grad_mixed.reshape(seqs * total, few),
+        mixed_low,
+        lse,
+        key_mask,
+        tables,
+        seqs,
+        heads_few,
+        block,
+        scale,
+    )
+    first_partial = matmul_t(grad_projected, attn_full[:, : 3 * few]).astype(bf).reshape(
         seqs, pieces, cap, width
     )
-    from_other = swap(first_partial[1])
-    first_parts = [first_partial[0, r] + from_other[r] for r in range(pieces)]
+    first_parts = add_cores(first_partial[0], first_partial[1])
+    grad_qkv = contract_rows(merged(input1), grad_projected).astype(bf)
+    grad_pairs = after(grad_pairs, grad_mixed)
+    own_pair_grads = ring_scatter(
+        [at(grad_pairs, index) for index in ctx_after], (grad_projected,), (first_parts[0],)
+    ).astype(bf)
+    grad_pair = contract_rows(cond_rows, own_pair_grads).astype(bf)
+    down_own, down_other = after(down_own, grad_mixed), after(down_other, grad_mixed)
+    down_parts = add_cores(down_own, after(down_other, grad_mixed))
+    down_sum = square_scatter(down_parts, (first_parts[0],), (grad_qkv,))
+    grad_attn = jnp.concatenate([grad_qkv, grad_output, grad_pair], axis=1)
+    attn_sum = square_scatter(
+        [rows_at(grad_attn, index, ctxs * owned) for index in shard_near]
+    ).astype(bf)
+    back1_sum = ring_scatter(first_parts, (grad_qkv,), (cross_sum, attn_sum, down_sum))
+    block_mine = (x_second + down_sum).astype(bf)
+    block_out = natural(block_mine, swap(block_mine))
     plain1, inverse1 = norm_parts(x_rows)
-    back1, grad_gain1 = norm_back(ring_scatter(first_parts), plain1, inverse1, gains[0])
+    back1, grad_gain1 = norm_back(back1_sum, plain1, inverse1, gains[0])
     tokens_grad_mine = grad_first + back1
     tokens_grad = natural(tokens_grad_mine, swap(tokens_grad_mine))
-    grad_qkv = contract_rows(input1, grad_projected)
-
-    gain_grads = jnp.pad(
-        jnp.stack([grad_gain1, grad_gain2, grad_gain3], axis=1), ((0, 0), (0, LANES - 3))
-    )
-    grad_attn = jnp.concatenate(
-        [grad_qkv[:, kind * wide : kind * wide + few].astype(bf) for kind in range(3)]
-        + [grad_output[:, :few].astype(bf), grad_pair.astype(bf), gain_grads.astype(bf)],
-        axis=1,
-    )
-    own_attn = lax.psum_scatter(grad_attn, "shard", scatter_dimension=0, tiled=True)
-    own_attn = lax.all_to_all(own_attn.reshape(ctxs, owned, -1), "ctx", 0, 0, tiled=True)
-    own_gains = jnp.sum(own_attn[:, :, n_kinds * few : n_kinds * few + 3].astype(fl), axis=0)
-    own_gains = jnp.transpose(own_gains + swap(own_gains))
+
+    own_cross = ring_scatter([rows_at(cross_sum, index, owned) for index in ctx_after])
+    own_kinds = place(
+        ring_exchange([rows_at(attn_sum, index, owned) for index in ctx_after]), ctx_before
+    )
     own_kinds = jnp.transpose(
-        own_attn[:, :, : n_kinds * few].reshape(ctxs, owned, n_kinds, few), (1, 2, 0, 3)
+        own_kinds.reshape(ctxs, owned, n_kinds, few), (1, 2, 0, 3)
     ).reshape(owned, n_kinds, local_width).astype(fl)
     own_qkv = own_kinds[:, :3]
     own_output = own_kinds[:, 3]
     own_pair = own_kinds[:, 4:]
     own_query = own_cross[:, :local_width]
     own_cross_out = own_cross[:, local_width:]
+    own_mlp = jnp.concatenate([sum_gate, sum_up, sum_down], axis=1)
+    own_mlp = place(
+        square_exchange([rows_at(own_mlp, index, owned) for index in shard_near]), shard_near
+    )
+    own_mlp = jnp.transpose(own_mlp.reshape(shards, owned, 3, units), (1, 2, 0, 3)).reshape(
+        owned, 3, units_half
+    )
     own_gate_up = own_mlp[:, :2].astype(fl)
     own_down = own_mlp[:, 2].astype(fl)
 
     squares = jnp.sum(own_kinds * own_kinds) + jnp.sum(own_cross * own_cross)
     squares = squares + jnp.sum(own_gate_up * own_gate_up) + jnp.sum(own_down * own_down)
-    squares = squares + jnp.sum(own_gains * own_gains) / float(lax.axis_size("tp"))
-    total_square = total_over_all(jnp.broadcast_to(squares, (8, LANES)))[0, 0]
-    grad_norm = jnp.sqrt(total_square)
+    totals = total_over_all(
+        jnp.concatenate(
+            [
+                jnp.stack([grad_gain1, grad_gain2, grad_gain3]),
+                jnp.broadcast_to(squares, (5, width)),
+            ]
+        )
+    )
+    gain_grads = totals[:3]
+    own_gains = lax.dynamic_slice_in_dim(
+        gain_grads, (shard_index * ctxs + ctx_index) * owned, owned, 1
+    )
+    grad_norm = jnp.sqrt(totals[3, 0] + jnp.sum(gain_grads * gain_grads))
     clip_scale = clip_norm / jnp.maximum(grad_norm, clip_norm)
 
     def step(weight, moment, square, grad):

time: 1160 us -> 1010 us (0.87)
  waiting for transfers between devices: 513 us -> 362 us
  starting transfers between devices: 64 us -> 169 us
  blocking collectives: 97.1 us -> 0 us
  local copies, waits for them, and re-layouts: 170 us -> 142 us
  Pallas kernels: 114 us -> 134 us
  other arithmetic: 89.6 us -> 105 us
    reduce_scatter x4 -> x3, waiting for transfers between devices: 160 us -> 0.02 us  [sum_over_ctx(): return lax.psum_scatter(by_owner, 'ctx', scatter_dimension=0, tiled=True)]
    ppermute x16 -> x34, waiting for transfers between devices: 74.9 us -> 159 us  [cross_over(): return lax.ppermute(value, 'shard', [(i, i ^ bits) for i in range(size)])]
    ppermute x16 -> x37, starting transfers between devices: 27.2 us -> 110 us  [ring_shift(): lax.ppermute(value, 'ctx', [(i, (i - by) % size) for i in range(size)])]
    all_to_all x2 -> x0, blocking collectives: 57.8 us -> none  [the longest x1 30.7 us: local(): sent_attn = lax.all_to_all(sent_attn, 'ctx', 0, 0, tiled=True)]
    ppermute x16 -> x37, waiting for transfers between devices: 243 us -> 187 us  [ring_shift(): lax.ppermute(value, 'ctx', [(i, (i - by) % size) for i in range(size)])]
    all_gather x1 -> x0, blocking collectives: 39.3 us -> none  [local(): pairs = lax.all_gather(own_pairs, 'ctx', axis=0, tiled=False)]
    unnamed x244 -> x208, local copies, waits for them, and re-layouts: 77.1 us -> 39.4 us
    all_to_all x2 -> x0, waiting for transfers between devices: 27.3 us -> none  [the longest x1 27.3 us: local(): lax.all_to_all(own_mlp.reshape(shards, owned, 3 * units), 'shard', 0, 0,...]
  transfers between devices with their start and end apart: 72 -> 108, of which waited for: 33 -> 52; matrix products, arithmetic and copies ran while one was open for 24% -> 28% of each run, Pallas kernels for 6% -> 8%
where the time goes in v2:
time: 1010 us
  waiting for transfers between devices  362 us (36%)
  starting transfers between devices  169 us (17%)
  local copies, waits for them, and re-layouts  142 us (14%)
  Pallas kernels  134 us (13%)
  other arithmetic  105 us (10%)
  matrix products  66.9 us (7%)
  between operations  25.6 us (3%)
    ppermute x37, waiting for transfers between devices, ring_shift(): lax.ppermute(value, 'ctx', [(i, (i - by) % size) for i in range(size)])  187 us
    ppermute x34, waiting for transfers between devices, cross_over(): return lax.ppermute(value, 'shard', [(i, i ^ bits) for i in range(size)])  159 us
    ppermute x37, starting transfers between devices, ring_shift(): lax.ppermute(value, 'ctx', [(i, (i - by) % size) for i in range(size)])  110 us
    pallas_call x1, Pallas kernels, mlp(): pl.pallas_call(functools.partial(mlp_kernel, count, given), grid=(count,)...  50.6 us
    ppermute x34, starting transfers between devices, cross_over(): return lax.ppermute(value, 'shard', [(i, i ^ bits) for i in range(size)])  40.9 us
    dot_general x7, matrix products, contract_rows(): lax.dot_general(left, right, (((0,), (0,)), ((), ())), preferred_element_...  40.6 us
    unnamed x208, local copies, waits for them, and re-layouts  39.4 us
    pallas_call x1, Pallas kernels, attend_back(): pl.pallas_call(functools.partial(attend_back_kernel, heads, wide, block,...  28 us
  transfers between devices with their start and end apart: 108, of which 52 were waited for; matrix products, arithmetic and copies ran while one was open for 28% of the time, Pallas kernels for 8%

profile of v2, /device:TPU:0, one launch (start us, length us, event | category | flops | bytes accessed | tf_op | source)
XLA Modules:
  0.0 1005.1 jit_solution(11785195286475641576)
XLA Ops:
  29.2 9.7 collective-permute-done.11
  121.5 14.7 %project.1 = (bf16[8,264,1536]{2,1,0:T(8,128)(2,1)}, bf16[8,264,576]{2,1,0:T(8,128)(2,1)}) custom-call(bf16[264,1536]{1,0:T(8,128)(2,1)S(1)} %get-tuple-element.331.refs_0_, bf16[264,1536]{1,0:T(8,128)(2,1)S(1)} %collective-permute-done.refs_1_, bf16[264,1536]{1,0:T(8,128)(2,1)S(1)} %pad_maximum_fusion.16.refs_2_, ...), custom_call_target="tpu_custom_call" | custom-call | flops 4982833152 | bytes 15409152 | tf_op jit(solution)/shard_map/project/pallas_call | solution.py:122
  138.3 15.6 %attend.1 = (bf16[2112,192]{1,0:T(8,128)(2,1)S(1)}, f32[2,16,352]{2,1,0:T(8,128)S(1)}) custom-call(bf16[2112,576]{1,0:T(8,128)(2,1)S(1)} %bitcast.278, f32[2112,128]{1,0:T(8,128)S(1)} %broadcast_in_dim.176.mask_ref), custom_call_target="tpu_custom_call" | custom-call | flops 6851395584 | bytes 3244032 | tf_op jit(solution)/shard_map/attend/pallas_call | solution.py:174
  181.0 13.5 %collective-permute-start.22 = (bf16[96,768]{1,0:T(8,128)(2,1)S(1)}, bf16[96,768]{1,0:T(8,128)(2,1)S(1)}, u32[]{:S(2)}, u32[]{:S(2)}) collective-permute-start(bf16[96,768]{1,0:T(8,128)(2,1)S(1)} %slice.417), channel_id=1, source_target_pairs={{0,2},{2,4},{4,6},{6,0},{1,3},{3,5},{5,7},{7,1},{8,10},{10,12},{12... | collective-permute-start | bytes 442376 | tf_op jit(solution)/shard_map/ppermute | solution.py:553
  195.5 14.2 %collective-permute-done.20 = bf16[96,768]{1,0:T(8,128)(2,1)S(1)} collective-permute-done((bf16[96,768]{1,0:T(8,128)(2,1)S(1)}, bf16[96,768]{1,0:T(8,128)(2,1)S(1)}, u32[]{:S(2)}, u32[]{:S(2)}) %collective-permute-start.20) | collective-permute-done | bytes 147488 | tf_op jit(solution)/shard_map/ppermute | solution.py:553
  234.2 18.4 %collective-permute-start.14 = (bf16[264,768]{1,0:T(8,128)(2,1)S(1)}, bf16[264,768]{1,0:T(8,128)(2,1)S(1)}, u32[]{:S(2)}, u32[]{:S(2)}) collective-permute-start(bf16[264,768]{1,0:T(8,128)(2,1)S(1)} %get-tuple-element.416), channel_id=1, source_target_pairs={{0,2},{2,4},{4,6},{6,0},{1,3},{3,5},{5,7},{7,1},{8,10},{10,12},{12... | collective-permute-start | bytes 1216520 | tf_op jit(solution)/shard_map/ppermute | solution.py:553
  263.5 11.4 %collective-permute-start.15 = (bf16[264,1536]{1,0:T(8,128)(2,1)}, bf16[264,1536]{1,0:T(8,128)(2,1)}, u32[]{:S(2)}, u32[]{:S(2)}) collective-permute-start(bf16[264,1536]{1,0:T(8,128)(2,1)} %pad_maximum_fusion.17), channel_id=1, source_target_pairs={{0,2},{2,4},{4,6},{6,0},{1,3},{3,5},{5,7},{7,1},{8,10},{10,12},{12... | collective-permute-start | bytes 2433032 | tf_op jit(solution)/shard_map/ppermute | solution.py:553
  286.6 9.8 collective-permute-done.15
  296.4 15.9 %collective-permute-done.28 = bf16[264,1536]{1,0:T(8,128)(2,1)} collective-permute-done((bf16[264,1536]{1,0:T(8,128)(2,1)}, bf16[264,1536]{1,0:T(8,128)(2,1)}, u32[]{:S(2)}, u32[]{:S(2)}) %collective-permute-start.28) | collective-permute-done | bytes 811040 | tf_op jit(solution)/shard_map/ppermute | solution.py:553
  340.8 13.1 %collective-permute-done.40.refs_13_ = bf16[264,1536]{1,0:T(8,128)(2,1)} collective-permute-done((bf16[264,1536]{1,0:T(8,128)(2,1)S(1)}, bf16[264,1536]{1,0:T(8,128)(2,1)}, u32[]{:S(2)}, u32[]{:S(2)}) %collective-permute-start.40) | collective-permute-done | bytes 811040 | tf_op jit(solution)/shard_map/ppermute | solution.py:558
  357.3 14.0 %collective-permute-done.34.refs_6_ = bf16[264,1536]{1,0:T(8,128)(2,1)} collective-permute-done((bf16[264,1536]{1,0:T(8,128)(2,1)}, bf16[264,1536]{1,0:T(8,128)(2,1)}, u32[]{:S(2)}, u32[]{:S(2)}) %collective-permute-start.34) | collective-permute-done | bytes 811040 | tf_op jit(solution)/shard_map/ppermute | solution.py:558
  399.4 50.6 %mlp.1 = (bf16[8,264,1536]{2,1,0:T(8,128)(2,1)}, bf16[8,264,1536]{2,1,0:T(8,128)(2,1)}, bf16[8,264,768]{2,1,0:T(8,128)(2,1)}, bf16[8,264,1536]{2,1,0:T(8,128)(2,...) custom-call(bf16[264,1536]{1,0:T(8,128)(2,1)} %collective-permute-do, ...), custom_call_target="tpu_custom_call" | custom-call | flops 29896998912 | bytes 55738368 | tf_op jit(solution)/shard_map/mlp/pallas_call | solution.py:507
  450.5 10.0 bitcast_convert_fusion
  473.2 9.5 collective-permute-done.50
  509.9 9.3 cross_back.1
  530.3 35.8 %collective-permute-done.54.refs_1_ = bf16[264,1536]{1,0:T(8,128)(2,1)S(1)} collective-permute-done((bf16[264,1536]{1,0:T(8,128)(2,1)S(1)}, bf16[264,1536]{1,0:T(8,128)(2,1)S(1)}, u32[]{:S(2)}, u32[]{:S(2)}) %collective-permute-start.54) | collective-permute-done | bytes 811040 | tf_op jit(solution)/shard_map/ppermute | solution.py:553
  570.2 17.1 %collective-permute-done.56.refs_3_ = bf16[264,1536]{1,0:T(8,128)(2,1)S(1)} collective-permute-done((bf16[264,1536]{1,0:T(8,128)(2,1)S(1)}, bf16[264,1536]{1,0:T(8,128)(2,1)S(1)}, u32[]{:S(2)}, u32[]{:S(2)}) %collective-permute-start.56) | collective-permute-done | bytes 811040 | tf_op jit(solution)/shard_map/ppermute | solution.py:553
  618.4 13.9 %collective-permute-done.73 = bf16[384,768]{1,0:T(8,128)(2,1)S(1)} collective-permute-done((bf16[384,768]{1,0:T(8,128)(2,1)}, bf16[384,768]{1,0:T(8,128)(2,1)S(1)}, u32[]{:S(2)}, u32[]{:S(2)}) %collective-permute-start.73) | collective-permute-done | bytes 589856 | tf_op jit(solution)/shard_map/ppermute | solution.py:558
  640.5 11.2 %collective-permute-done.71 = bf16[384,768]{1,0:T(8,128)(2,1)} collective-permute-done((bf16[384,768]{1,0:T(8,128)(2,1)}, bf16[384,768]{1,0:T(8,128)(2,1)}, u32[]{:S(2)}, u32[]{:S(2)}) %collective-permute-start.71) | collective-permute-done | bytes 589856 | tf_op jit(solution)/shard_map/ppermute | solution.py:558
  676.6 10.0 mix_back.1
  687.1 28.0 %attend_back.1 = bf16[2112,576]{1,0:T(8,128)(2,1)} custom-call(bf16[2112,576]{1,0:T(8,128)(2,1)} %bitcast.277, bf16[2112,192]{1,0:T(8,128)(2,1)} %bitcast.320, bf16[2112,192]{1,0:T(8,128)(2,1)} %copy-done.2, f32[2,16,352]{2,1,0:T(8,128)} %copy-done.12, f32[2112,128]{1,0:T(8,128)} %copy-done.3, f32[2112,128]{1,0:T(8,128)} %get-tuple-element.95.cos_ref, ...), custom_call_target="tpu_custom_call" | custom-call | flops 17128488960 | bytes 8110080 | tf_op jit(solution)/shard_map/attend_back/pallas_call | solution.py:247
  814.8 17.3 %collective-permute-done.79 = bf16[384,576]{0,1:T(8,128)(2,1)} collective-permute-done((bf16[384,576]{0,1:T(8,128)(2,1)}, bf16[384,576]{0,1:T(8,128)(2,1)}, u32[]{:S(2)}, u32[]{:S(2)}) %collective-permute-start.79) | collective-permute-done | bytes 442400 | tf_op jit(solution)/shard_map/ppermute | solution.py:558
  842.7 14.5 %collective-permute-done.94 = bf16[96,2304]{1,0:T(8,128)(2,1)S(1)} collective-permute-done((bf16[96,2304]{1,0:T(8,128)(2,1)S(1)}, bf16[96,2304]{1,0:T(8,128)(2,1)S(1)}, u32[]{:S(2)}, u32[]{:S(2)}) %collective-permute-start.94) | collective-permute-done | bytes 442400 | tf_op jit(solution)/shard_map/ppermute | solution.py:558
  908.4 9.8 collective-permute-done.87
  (670 shorter events, 592.3 us)
Async XLA Ops:
  7.2 109.8 %all-gather.8.cloned.1.call-start = ((), (), s32[]{:S(2)}) async-start(), calls=%async_computation.3 | async-start | bytes 4915200 | tf_op jit(solution)/shard_map/all_gather | solution.py:777
  39.9 355.4 %all-gather.10.cloned.1.call-start = ((), (), s32[]{:S(2)}) async-start(), calls=%async_computation.7 | async-start | bytes 2949120 | tf_op jit(solution)/shard_map/all_gather | solution.py:793
  39.9 51.2 %collective-permute-start = (bf16[264,1536]{1,0:T(8,128)(2,1)S(1)}, bf16[264,1536]{1,0:T(8,128)(2,1)S(1)}, u32[]{:S(2)}, u32[]{:S(2)}) collective-permute-start(bf16[264,1536]{1,0:T(8,128)(2,1)S(1)} %get-tuple-element.331.refs_0_), channel_id=1, source_target_pairs={{0,6},{2,0},{4,2},{6,4},{1,7},{3,1},{5,3},{7,5},{8,14},{10,8},{12,... | collective-permute-start | bytes 2433032 | tf_op jit(solution)/shard_map/ppermute | solution.py:553
  46.8 43.2 %collective-permute-start.2 = (bf16[264,1536]{1,0:T(8,128)(2,1)S(1)}, bf16[264,1536]{1,0:T(8,128)(2,1)}, u32[]{:S(2)}, u32[]{:S(2)}) collective-permute-start(bf16[264,1536]{1,0:T(8,128)(2,1)S(1)} %get-tuple-element.331.refs_0_), channel_id=1, source_target_pairs={{0,2},{2,4},{4,6},{6,0},{1,3},{3,5},{5,7},{7,1},{8,10},{10,12},{12... | collective-permute-start | bytes 2433032 | tf_op jit(solution)/shard_map/ppermute | solution.py:553
  116.7 278.6 %all-gather.12.cloned.1.call-start = ((), (), s32[]{:S(2)}) async-start(), calls=%async_computation.8 | async-start | bytes 2949120 | tf_op jit(solution)/shard_map/all_gather | solution.py:793
  161.3 58.4 %collective-permute-start.13 = (bf16[4,264,1536]{2,1,0:T(8,128)(2,1)}, bf16[4,264,1536]{2,1,0:T(8,128)(2,1)}, u32[]{:S(2)}, u32[]{:S(2)}) collective-permute-start(bf16[4,264,1536]{2,1,0:T(8,128)(2,1)} %bitcast.32), channel_id=1, source_target_pairs={{0,1},{1,0},{2,3},{3,2},{4,5},{5,4},{6,7},{7,6},{8,9},{9,8},{10,11... | collective-permute-start | bytes 9732104 | tf_op jit(solution)/shard_map/ppermute | solution.py:548
  166.0 232.2 %all-gather.14.cloned.1.call-start = ((), (), s32[]{:S(2)}) async-start(), calls=%async_computation.9 | async-start | bytes 2949120 | tf_op jit(solution)/shard_map/all_gather | solution.py:793
  168.0 86.4 %collective-permute-start.18 = (bf16[288,384]{1,0:T(8,128)(2,1)S(1)}, bf16[288,384]{1,0:T(8,128)(2,1)S(1)}, u32[]{:S(2)}, u32[]{:S(2)}) collective-permute-start(bf16[288,384]{1,0:T(8,128)(2,1)S(1)} %convolution_convert_fusion.10), channel_id=1, source_target_pairs={{0,2},{2,4},{4,6},{6,0},{1,3},{3,5},{5,7},{7,1},{8,10},{10,12},{12... | collective-permute-start | bytes 663560 | tf_op jit(solution)/shard_map/ppermute | solution.py:553
  169.8 86.2 %collective-permute-start.17 = (bf16[288,384]{1,0:T(8,128)(2,1)S(1)}, bf16[288,384]{1,0:T(8,128)(2,1)S(1)}, u32[]{:S(2)}, u32[]{:S(2)}) collective-permute-start(bf16[288,384]{1,0:T(8,128)(2,1)S(1)} %convolution_convert_fusion.10), channel_id=1, source_target_pairs={{0,4},{2,6},{4,0},{6,2},{1,5},{3,7},{5,1},{7,3},{8,12},{10,14},{12... | collective-permute-start | bytes 663560 | tf_op jit(solution)/shard_map/ppermute | solution.py:553
  334.1 321.4 %reduce-scatter.4.cloned.1.call-start = ((), (), s32[]{:S(2)}) async-start(), calls=%async_computation.4 | async-start | bytes 2949120 | tf_op jit(solution)/shard_map/reduce_scatter | solution.py:893
  505.7 302.2 %reduce-scatter.6.cloned.1.call-start = ((), (), s32[]{:S(2)}) async-start(), calls=%async_computation.5 | async-start | bytes 2949120 | tf_op jit(solution)/shard_map/reduce_scatter | solution.py:893
  528.3 37.8 %collective-permute-start.54 = (bf16[264,1536]{1,0:T(8,128)(2,1)S(1)}, bf16[264,1536]{1,0:T(8,128)(2,1)S(1)}, u32[]{:S(2)}, u32[]{:S(2)}) collective-permute-start(bf16[264,1536]{1,0:T(8,128)(2,1)S(1)} %get-tuple-element.334.refs_0_), channel_id=1, source_target_pairs={{0,6},{2,0},{4,2},{6,4},{1,7},{3,1},{5,3},{7,5},{8,14},{10,8},{12,... | collective-permute-start | bytes 2433032 | tf_op jit(solution)/shard_map/ppermute | solution.py:553
  530.0 57.2 %collective-permute-start.56 = (bf16[264,1536]{1,0:T(8,128)(2,1)S(1)}, bf16[264,1536]{1,0:T(8,128)(2,1)S(1)}, u32[]{:S(2)}, u32[]{:S(2)}) collective-permute-start(bf16[264,1536]{1,0:T(8,128)(2,1)S(1)} %get-tuple-element.334.refs_0_), channel_id=1, source_target_pairs={{0,2},{2,4},{4,6},{6,0},{1,3},{3,5},{5,7},{7,1},{8,10},{10,12},{12... | collective-permute-start | bytes 2433032 | tf_op jit(solution)/shard_map/ppermute | solution.py:553
  606.1 203.8 %reduce-scatter.8.cloned.1.call-start = ((), (), s32[]{:S(2)}) async-start(), calls=%async_computation.6 | async-start | bytes 2949120 | tf_op jit(solution)/shard_map/reduce_scatter | solution.py:893
  675.2 65.1 %collective-permute-start.72 = (bf16[384,1536]{1,0:T(8,128)(2,1)}, bf16[384,1536]{1,0:T(8,128)(2,1)}, u32[]{:S(2)}, u32[]{:S(2)}) collective-permute-start(bf16[384,1536]{1,0:T(8,128)(2,1)} %pad_maximum_fusion.8), channel_id=1, source_target_pairs={{0,8},{8,0},{16,24},{24,16},{1,9},{9,1},{17,25},{25,17},{2,10},{10... | collective-permute-start | bytes 3538952 | tf_op jit(solution)/shard_map/ppermute | solution.py:558
  686.8 53.5 %collective-permute-start.75 = (bf16[288,192]{1,0:T(8,128)(2,1)S(1)}, bf16[288,192]{1,0:T(8,128)(2,1)S(1)}, u32[]{:S(2)}, u32[]{:S(2)}) collective-permute-start(bf16[288,192]{1,0:T(8,128)(2,1)S(1)} %get-tuple-element.428), channel_id=1, source_target_pairs={{0,2},{2,4},{4,6},{6,0},{1,3},{3,5},{5,7},{7,1},{8,10},{10,12},{12... | collective-permute-start | bytes 331784 | tf_op jit(solution)/shard_map/ppermute | solution.py:553
  726.7 46.2 %collective-permute-start.64 = (bf16[4,264,1536]{2,1,0:T(8,128)(2,1)}, bf16[4,264,1536]{2,1,0:T(8,128)(2,1)}, u32[]{:S(2)}, u32[]{:S(2)}) collective-permute-start(bf16[4,264,1536]{2,1,0:T(8,128)(2,1)} %bitcast.77), channel_id=1, source_target_pairs={{0,1},{1,0},{2,3},{3,2},{4,5},{5,4},{6,7},{7,6},{8,9},{9,8},{10,11... | collective-permute-start | bytes 9732104 | tf_op jit(solution)/shard_map/ppermute | solution.py:548
  740.1 39.8 %collective-permute-start.62 = (bf16[4,264,1536]{2,1,0:T(8,128)(2,1)}, bf16[4,264,1536]{2,1,0:T(8,128)(2,1)S(1)}, u32[]{:S(2)}, u32[]{:S(2)}) collective-permute-start(bf16[4,264,1536]{2,1,0:T(8,128)(2,1)} %get-tuple-element.137), channel_id=1, source_target_pairs={{0,1},{1,0},{2,3},{3,2},{4,5},{5,4},{6,7},{7,6},{8,9},{9,8},{10,11... | collective-permute-start | bytes 9732104 | tf_op jit(solution)/shard_map/ppermute | solution.py:548
  794.5 101.7 %collective-permute-start.70 = (bf16[264,1536]{1,0:T(8,128)(2,1)}, bf16[264,1536]{1,0:T(8,128)(2,1)}, u32[]{:S(2)}, u32[]{:S(2)}) collective-permute-start(bf16[264,1536]{1,0:T(8,128)(2,1)} %pad_maximum_fusion.25), channel_id=1, source_target_pairs={{0,2},{2,4},{4,6},{6,0},{1,3},{3,5},{5,7},{7,1},{8,10},{10,12},{12... | collective-permute-start | bytes 2433032 | tf_op jit(solution)/shard_map/ppermute | solution.py:553
  796.0 84.9 %collective-permute-start.65 = (bf16[264,1536]{1,0:T(8,128)(2,1)}, bf16[264,1536]{1,0:T(8,128)(2,1)}, u32[]{:S(2)}, u32[]{:S(2)}) collective-permute-start(bf16[264,1536]{1,0:T(8,128)(2,1)} %pad_maximum_fusion.23), channel_id=1, source_target_pairs={{0,8},{8,0},{16,24},{24,16},{1,9},{9,1},{17,25},{25,17},{2,10},{10... | collective-permute-start | bytes 2433032 | tf_op jit(solution)/shard_map/ppermute | solution.py:558
  801.3 87.6 %collective-permute-start.67 = (bf16[264,1536]{1,0:T(8,128)(2,1)}, bf16[264,1536]{1,0:T(8,128)(2,1)}, u32[]{:S(2)}, u32[]{:S(2)}) collective-permute-start(bf16[264,1536]{1,0:T(8,128)(2,1)} %pad_maximum_fusion.24), channel_id=1, source_target_pairs={{0,16},{8,24},{16,0},{24,8},{1,17},{9,25},{17,1},{25,9},{2,18},{10... | collective-permute-start | bytes 2433032 | tf_op jit(solution)/shard_map/ppermute | solution.py:558
  806.7 85.6 %collective-permute-start.82 = (bf16[384,1152]{0,1:T(8,128)(2,1)}, bf16[384,1152]{0,1:T(8,128)(2,1)}, u32[]{:S(2)}, u32[]{:S(2)}) collective-permute-start(bf16[384,1152]{0,1:T(8,128)(2,1)} %pad_maximum_fusion.15), channel_id=1, source_target_pairs={{0,16},{8,24},{16,0},{24,8},{1,17},{9,25},{17,1},{25,9},{2,18},{10... | collective-permute-start | bytes 2654216 | tf_op jit(solution)/shard_map/ppermute | solution.py:558
  892.3 59.1 %collective-permute-start.68 = (bf16[264,1536]{1,0:T(8,128)(2,1)}, bf16[264,1536]{1,0:T(8,128)(2,1)}, u32[]{:S(2)}, u32[]{:S(2)}) collective-permute-start(bf16[264,1536]{1,0:T(8,128)(2,1)} %add_convert_fusion.2), channel_id=1, source_target_pairs={{0,1},{1,0},{2,3},{3,2},{4,5},{5,4},{6,7},{7,6},{8,9},{9,8},{10,11... | collective-permute-start | bytes 2433032 | tf_op jit(solution)/shard_map/ppermute | solution.py:548
  934.3 58.6 %collective-permute-start.85 = (f32[264,1536]{1,0:T(8,128)}, f32[264,1536]{1,0:T(8,128)}, u32[]{:S(2)}, u32[]{:S(2)}) collective-permute-start(f32[264,1536]{1,0:T(8,128)} %fusion.23), channel_id=1, source_target_pairs={{0,1},{1,0},{2,3},{3,2},{4,5},{5,4},{6,7},{7,6},{8,9},{9,8},{10,11... | collective-permute-start | bytes 4866056 | tf_op jit(solution)/shard_map/ppermute | solution.py:548
  (182 other events, 2724.2 us)
Sparse Core Ops, SparseCore 0:
  40.0 68.0 all-gather.7
  116.8 50.8 all-gather.9
  169.9 70.5 all-gather.11
  334.2 49.6 all-gather.13
  505.9 64.9 reduce-scatter.3
  606.2 46.1 reduce-scatter.5
  655.6 49.6 reduce-scatter.7

commit v3 on v2

--- a/solution.py
+++ b/solution.py
@@ -4,6 +4,7 @@
 import jax.numpy as jnp
 from jax import lax
 from jax.experimental import pallas as pl
+from jax.experimental.layout import Layout, with_layout_constraint
 from jax.experimental.pallas import tpu as pltpu
 from jax.sharding import PartitionSpec as P
 
@@ -26,6 +27,7 @@
 bf = jnp.bfloat16
 fl = jnp.float32
 MIB = 1024 * 1024
+SHORT = pl.CostEstimate(flops=1000, bytes_accessed=1000, transcendentals=0)
 
 
 def params(mib):
@@ -137,11 +139,7 @@
         ],
         scratch_shapes=[pltpu.VMEM((rows, width), bf)],
         compiler_params=params(48),
-        cost_estimate=pl.CostEstimate(
-            flops=2 * count * rows * width * 4 * few,
-            bytes_accessed=count * rows * (4 * width + 6 * few),
-            transcendentals=0,
-        ),
+        cost_estimate=SHORT,
         name="project",
     )(*blocks, gain, weight, *(table.reshape(count, rows, LANES) for table in tables))
 
@@ -187,11 +185,7 @@
             jax.ShapeDtypeStruct((latents, spots_up, block), fl),
         ],
         compiler_params=params(48),
-        cost_estimate=pl.CostEstimate(
-            flops=latents * heads * total * total * 16 * HD,
-            bytes_accessed=rows * 4 * wide * 2,
-            transcendentals=latents * heads * total * total,
-        ),
+        cost_estimate=SHORT,
         name="attend",
     )(qkv, mask)
 
@@ -261,11 +255,7 @@
         out_shape=jax.ShapeDtypeStruct((rows, lanes), bf),
         scratch_shapes=[pltpu.VMEM((total, lanes), fl)],
         compiler_params=params(56),
-        cost_estimate=pl.CostEstimate(
-            flops=latents * heads * total * total * 40 * HD,
-            bytes_accessed=rows * 10 * wide * 2,
-            transcendentals=latents * heads * total * total,
-        ),
+        cost_estimate=SHORT,
         name="attend_back",
     )(qkv, grads, mixed, lse, mask, *tables)
 
@@ -305,11 +295,7 @@
             jax.ShapeDtypeStruct((latents, heads_up, rows), fl),
         ],
         compiler_params=params(32),
-        cost_estimate=pl.CostEstimate(
-            flops=latents * heads * rows * 256 * 16 * HD,
-            bytes_accessed=8 * latents * rows * wide,
-            transcendentals=latents * heads * rows * 144,
-        ),
+        cost_estimate=SHORT,
         name="cross",
     )(queries, pairs, mask)
 
@@ -371,11 +357,7 @@
             jax.ShapeDtypeStruct(pairs.shape, bf),
         ],
         compiler_params=params(32),
-        cost_estimate=pl.CostEstimate(
-            flops=latents * heads * rows * 256 * 40 * HD,
-            bytes_accessed=12 * latents * rows * wide,
-            transcendentals=latents * heads * rows * 144,
-        ),
+        cost_estimate=SHORT,
         name="cross_back",
     )(queries, pairs, grads, mixed, lse, mask)
 
@@ -416,11 +398,7 @@
         ],
         scratch_shapes=[pltpu.VMEM((rows, width), bf), pltpu.VMEM((few, width), fl)],
         compiler_params=params(48),
-        cost_estimate=pl.CostEstimate(
-            flops=4 * count * rows * width * 256,
-            bytes_accessed=2 * count * rows * (width + 2 * few) + 8 * width * few,
-            transcendentals=0,
-        ),
+        cost_estimate=SHORT,
         name="mix_back",
     )(*blocks, weight, mixed)
 
@@ -531,17 +509,13 @@
             pltpu.VMEM((rows, width), bf),
         ],
         compiler_params=params(60),
-        cost_estimate=pl.CostEstimate(
-            flops=12 * count * rows * width * units,
-            bytes_accessed=2 * count * rows * (6 * width + 3 * units) + 6 * width * units,
-            transcendentals=count * rows * units,
-        ),
+        cost_estimate=SHORT,
         name="mlp",
     )(*blocks, *grads, *weights)
 
 
 def after(value, *others):
-    return lax.optimization_barrier((value,) + others)[0]
+    return lax.optimization_barrier((value,) + others)[0] if others else value
 
 
 def swap(value):
@@ -556,6 +530,14 @@
 def cross_over(value, bits):
     size = lax.axis_size("shard")
     return lax.ppermute(value, "shard", [(i, i ^ bits) for i in range(size)])
+
+
+def together(values, *others):
+    return lax.optimization_barrier((tuple(values),) + others)[0]
+
+
+def nothing(token):
+    return ()
 
 
 def ring_gather(own, first=(), second=()):
@@ -563,40 +545,44 @@
     if size != 4:
         return [own] + [after(ring_shift(own, r), *second) for r in range(1, size)]
     half = own.shape[-1] // 2
-    following = after(ring_shift(own, 1), *first)
-    before = after(ring_shift(own, -1), *first)
-    far = jnp.concatenate(
-        [
-            after(ring_shift(following[:, :half], 1), *second),
-            after(ring_shift(before[:, half:], -1), *second),
-        ],
-        axis=-1,
-    )
-    return [own, following, far, before]
-
-
-def ring_scatter(parts, first=(), second=()):
+    following, before = together((ring_shift(own, 1), ring_shift(own, -1)), *first)
+    far = together(
+        (ring_shift(following[:, :half], 1), ring_shift(before[:, half:], -1)), *second
+    )
+    return [own, following, jnp.concatenate(far, axis=-1), before]
+
+
+def ring_scatter(parts, first=(), between=nothing):
     if lax.axis_size("ctx") != 4:
         total = parts[0].astype(fl)
         for r in range(1, len(parts)):
-            total = total + after(ring_shift(parts[r], -r), *second).astype(fl)
+            total = total + after(ring_shift(parts[r], -r), *between(parts[0])).astype(fl)
         return total
     half = parts[0].shape[-1] // 2
-    by_after = after(ring_shift(parts[2][:, :half], -1), *first)
-    by_before = after(ring_shift(parts[2][:, half:], 1), *first)
+    by_after, by_before = together(
+        (ring_shift(parts[2][:, :half], -1), ring_shift(parts[2][:, half:], 1)), *first
+    )
     to_after = jnp.concatenate([parts[1][:, :half] + by_after, parts[1][:, half:]], axis=-1)
     to_before = jnp.concatenate([parts[3][:, :half], parts[3][:, half:] + by_before], axis=-1)
-    from_before = after(ring_shift(to_after, -1), *second)
-    from_after = after(ring_shift(to_before, 1), *second)
+    from_before, from_after = together(
+        (ring_shift(to_after, -1), ring_shift(to_before, 1)), *between(by_after)
+    )
     return parts[0].astype(fl) + from_before.astype(fl) + from_after.astype(fl)
 
 
-def ring_exchange(parts):
-    return [parts[0]] + [ring_shift(part, -r) for r, part in enumerate(parts[1:], 1)]
-
-
-def square_exchange(parts):
-    return [parts[0]] + [cross_over(part, r) for r, part in enumerate(parts[1:], 1)]
+def ring_exchange(parts, before=()):
+    return [parts[0]] + [after(ring_shift(part, -r), *before) for r, part in enumerate(parts[1:], 1)]
+
+
+def square_exchange(parts, before=()):
+    return [parts[0]] + [after(cross_over(part, r), *before) for r, part in enumerate(parts[1:], 1)]
+
+
+def summed(parts):
+    total = parts[0].astype(fl)
+    for part in parts[1:]:
+        total = total + part.astype(fl)
+    return total
 
 
 def at(array, index):
@@ -619,32 +605,27 @@
     if size != 4:
         return [own] + [after(cross_over(own, r), *second) for r in range(1, size)]
     half = own.shape[-1] // 2
-    one = after(cross_over(own, 1), *first)
-    two = after(cross_over(own, 2), *first)
-    three = jnp.concatenate(
-        [
-            after(cross_over(two[:, :half], 1), *second),
-            after(cross_over(one[:, half:], 2), *second),
-        ],
-        axis=-1,
-    )
-    return [own, one, two, three]
-
-
-def square_scatter(parts, first=(), second=()):
+    one, two = together((cross_over(own, 1), cross_over(own, 2)), *first)
+    three = together((cross_over(two[:, :half], 1), cross_over(one[:, half:], 2)), *second)
+    return [own, one, two, jnp.concatenate(three, axis=-1)]
+
+
+def square_scatter(parts, first=(), between=nothing):
     size = lax.axis_size("shard")
     if size != 4:
         total = parts[0].astype(fl)
         for r in range(1, size):
-            total = total + after(cross_over(parts[r], r), *second).astype(fl)
+            total = total + after(cross_over(parts[r], r), *between(parts[0])).astype(fl)
         return total
     half = parts[0].shape[-1] // 2
-    by_one = after(cross_over(parts[3][:, :half], 1), *first)
-    by_two = after(cross_over(parts[3][:, half:], 2), *first)
+    by_one, by_two = together(
+        (cross_over(parts[3][:, :half], 1), cross_over(parts[3][:, half:], 2)), *first
+    )
     to_two = jnp.concatenate([parts[2][:, :half] + by_one, parts[2][:, half:]], axis=-1)
     to_one = jnp.concatenate([parts[1][:, :half], parts[1][:, half:] + by_two], axis=-1)
-    from_one = after(cross_over(to_one, 1), *second)
-    from_two = after(cross_over(to_two, 2), *second)
+    from_one, from_two = together(
+        (cross_over(to_one, 1), cross_over(to_two, 2)), *between(by_one)
+    )
     return parts[0].astype(fl) + from_one.astype(fl) + from_two.astype(fl)
 
 
@@ -744,6 +725,7 @@
     key_valid = (slot < lengths_here[:, :, None]).reshape(-1)
     key_mask = jnp.broadcast_to(key_valid.astype(fl)[:, None], (key_valid.shape[0], LANES))
     tables = lax.optimization_barrier(rotary_tables(positions))
+    other_valid = (slot < lengths_here[1, 0]).astype(fl)[:, None]
     own_valid = (slot < lengths_here[0, 0]).astype(fl)[:, None]
 
     tokens_mine = mine(tokens)
@@ -771,38 +753,35 @@
     ctx_after = [(ctx_index + r) % ctxs for r in range(ctxs)]
     ctx_before = [(ctx_index - r) % ctxs for r in range(ctxs)]
     shard_near = [shard_index ^ r for r in range(shards)]
-    attn_rows = place(
-        ring_exchange([at(sent_attn, index) for index in ctx_after]), ctx_before
+    sent_mlp = jnp.concatenate(
+        [
+            gate_up_weight.astype(bf),
+            down_weight.astype(bf)[:, None],
+        ],
+        axis=1,
+    )
+    sent_mlp = jnp.transpose(sent_mlp.reshape(owned, 3, shards, units), (2, 0, 1, 3)).reshape(
+        shards, owned, 3 * units
+    )
+    attn_rows = after(
+        lax.all_to_all(sent_attn, "ctx", 0, 0, tiled=True), sent_mlp, *tables
     ).reshape(ctxs * owned, -1)
     attn_full = lax.all_gather(attn_rows, "shard", axis=0, tiled=True)
     pair_full = attn_full[:, 4 * few : 6 * few]
     output_full = attn_full[:, 3 * few : 4 * few]
     gains = jnp.transpose(attn_full[:, n_kinds * few : n_kinds * few + 3].astype(fl))
 
-    sent_mlp = jnp.concatenate(
-        [gate_up_weight.astype(bf), down_weight.astype(bf)[:, None]], axis=1
-    )
-    sent_mlp = jnp.transpose(sent_mlp.reshape(owned, 3, shards, units), (2, 0, 1, 3)).reshape(
-        shards, owned, 3 * units
-    )
-    sent_mlp = place(
-        square_exchange([at(sent_mlp, index) for index in shard_near]), shard_near
-    )
-    token_blocks = ring_gather(tokens_mine)
-    sent_mlp = after(sent_mlp, token_blocks[2], attn_rows)
+    token_blocks = ring_gather(tokens_mine, (attn_rows,))
+    sent_mlp = lax.all_to_all(sent_mlp, "shard", 0, 0, tiled=True)
+    sent_gate, sent_up, sent_down = (
+        sent_mlp[:, :, k * units : (k + 1) * units] for k in range(3)
+    )
     over_ctx = lambda array: lax.all_gather(array, "ctx", axis=0, tiled=False)
-    gate_full = over_ctx(sent_mlp[:, :, :units])
-    up_full = over_ctx(sent_mlp[:, :, units : 2 * units])
-
     token_swapped = [tokens_other] + [swap(block) for block in token_blocks[1:]]
-    token_last = after(token_swapped[-1], sent_mlp)
+    token_last = after(token_swapped[-1], sent_gate, sent_up, sent_down)
 
     total = pieces * cap
     block = total // 3
-    sent_cross = jnp.concatenate(
-        [cross_query_weight.astype(bf), cross_out_weight.astype(bf)], axis=1
-    )
-    sent_cross = after(sent_cross, token_blocks[2])
     input1, qkv = project(
         token_blocks + token_swapped[:-1] + [token_last], gains[0:1], attn_full, tables, scale, few
     )
@@ -811,30 +790,35 @@
     cond_rows = jnp.pad(both(conditioning), ((0, 0), (0, cond_up - cond_len), (0, 0))).reshape(
         seqs * cond_up, width
     )
-    own_pairs = after(matmul(cond_rows, pair_full).astype(bf), qkv)
+    own_pairs = matmul(cond_rows, pair_full).astype(bf)
+    gate_full = over_ctx(after(sent_gate, token_last, attn_full))
+    sent_cross = jnp.concatenate(
+        [cross_query_weight.astype(bf), cross_out_weight.astype(bf)], axis=1
+    )
+    sent_cross = after(sent_cross, qkv)
+    cross_rows = [sent_cross] + [ring_shift(sent_cross, r) for r in range(1, ctxs)]
     mixed_low, lse = attend(qkv, key_mask, seqs, heads_few, block)
-    cross_blocks = ring_gather(sent_cross, (qkv,), (mixed_low,))
+    cross_rows = place(cross_rows, ctx_after).reshape(ctxs * owned, -1)
+    cross_full = lax.all_gather(after(cross_rows, gate_full), "shard", axis=0, tiled=True)
     partial = matmul_t(mixed_low, output_full).astype(bf).reshape(seqs, pieces, cap, width)
     from_other = swap(partial[1])
     mine_parts = [partial[0, r] + from_other[r] for r in range(pieces)]
-    pairs = place(
-        [own_pairs]
-        + [after(ring_shift(own_pairs, r), mine_parts[0]) for r in range(1, ctxs)],
-        ctx_after,
-    )
+    own_pairs = after(own_pairs, mixed_low)
+    pairs = [own_pairs] + [ring_shift(own_pairs, r) for r in range(1, ctxs)]
+    pairs = place(pairs, ctx_after)
     pairs = jnp.transpose(
         pairs.reshape(ctxs, seqs, cond_up, 2, few), (1, 2, 3, 0, 4)
     ).reshape(seqs, cond_up, 2 * local_width)
-    cross_rows = place(cross_blocks, ctx_after).reshape(ctxs * owned, -1)
-    cross_full = place(square_gather(cross_rows, (mine_parts[0],)), shard_near).reshape(width, -1)
     query_full = cross_full[:, :local_width]
     cross_out_full = cross_full[:, local_width:]
     x_rows = tokens_mine.astype(fl)
-    x_first = x_rows + ring_scatter(mine_parts, (), (pairs, cross_full))
-    dy_low = after(dy_low, cross_full)
-    dy_blocks = square_gather(dy_low, (x_first,), (x_first,))
-    dy_swapped = [swap(block_of) for block_of in dy_blocks]
-    down_full = over_ctx(after(sent_mlp[:, :, 2 * units :], x_first))
+    x_first = x_rows + ring_scatter(mine_parts, (cross_rows,), lambda token: (pairs,))
+    up_full = over_ctx(after(sent_up, x_first))
+    down_full = over_ctx(after(sent_down, x_first))
+    dy_low = after(dy_low, x_first)
+    dy_blocks = [dy_low] + [cross_over(dy_low, r) for r in range(1, shards)]
+    dy_other = (others(cotangent).astype(fl) * other_valid).astype(bf)
+    dy_swapped = [dy_other] + [swap(block_of) for block_of in dy_blocks[1:]]
 
     plain2, inverse2 = norm_parts(x_first)
     input2_mine = (plain2 * gains[1]).astype(bf)
@@ -851,7 +835,7 @@
 
     plain3, inverse3 = norm_parts(x_second)
     input3 = (plain3 * gains[2]).astype(bf)
-    input3_blocks = square_gather(input3)
+    input3_blocks = square_gather(input3, (), dy_swapped)
     (
         input3_all,
         dy_all,
@@ -875,8 +859,17 @@
         from_other = swap(other)
         return [own[r] + from_other[r] for r in range(own.shape[0])]
 
+    def by_owner(array):
+        return jnp.transpose(
+            array.reshape(shards, ctxs, owned, array.shape[1]), (1, 0, 2, 3)
+        ).reshape(ctxs * shards * owned, -1)
+
+    def sum_over_ctx(array):
+        return lax.psum_scatter(array, "ctx", scatter_dimension=0, tiled=True)
+
+    grad_down, grad_gate, grad_up = by_owner(grad_down), by_owner(grad_gate), by_owner(grad_up)
     back_sum = square_scatter(
-        add_cores(back_own, back_other), (grad_down,), (grad_gate, grad_up)
+        add_cores(back_own, back_other), (grad_down,), lambda token: (grad_gate, grad_up)
     )
     back3, grad_gain3 = norm_back(back_sum, plain3, inverse3, gains[2])
 
@@ -885,12 +878,6 @@
         return jnp.stack(
             [jnp.where(straight, first, second), jnp.where(straight, second, first)]
         )
-
-    def sum_over_ctx(array):
-        by_owner = jnp.transpose(
-            array.reshape(shards, ctxs, owned, array.shape[1]), (1, 0, 2, 3)
-        ).reshape(ctxs * shards * owned, -1)
-        return lax.psum_scatter(by_owner, "ctx", scatter_dimension=0, tiled=True)
 
     sum_down = sum_over_ctx(grad_down)
     sum_gate = sum_over_ctx(grad_gate)
@@ -919,17 +906,32 @@
 
     grad_first = grad_second + back2
     grad1_mine = grad_first.astype(bf)
-    grad1_blocks = ring_gather(grad1_mine)
-    grad_cross = after(grad_cross, grad1_mine)
-    cross_sum = square_scatter(
-        [rows_at(grad_cross, index, ctxs * owned) for index in shard_near]
-    ).astype(bf)
+    down_parts = add_cores(after(down_own, back_sum), after(down_other, back_sum))
+    down_sum = summed(square_exchange(down_parts, (grad1_mine,)))
+    block_mine = (x_second + down_sum).astype(bf)
+    block_out = natural(block_mine, swap(block_mine))
+    grad1_blocks = ring_gather(
+        grad1_mine, (grad_cross, grad_pairs, sum_down), (block_mine, sum_gate)
+    )
+    cross_sum = lax.psum_scatter(
+        after(grad_cross, grad1_mine), "shard", scatter_dimension=0, tiled=True
+    )
     grad_mixed, grad_output = mix_back(
         grad1_blocks + [swap(block_of) for block_of in grad1_blocks],
         output_full,
         mixed_low.reshape(seqs * pieces, cap, few),
     )
     sum_up = sum_over_ctx(after(grad_up, grad1_blocks[2]))
+    grad_pairs = after(grad_pairs, grad_mixed)
+    own_pair_grads = summed(
+        ring_exchange([at(grad_pairs, index) for index in ctx_after])
+    ).astype(bf)
+    grad_pair = contract_rows(cond_rows, own_pair_grads).astype(bf)
+    to_owner = lambda array: jnp.transpose(
+        lax.all_to_all(array.reshape(shards, owned, -1), "shard", 0, 0, tiled=True), (1, 0, 2)
+    ).reshape(owned, units_half)
+    own_gate = to_owner(after(sum_gate, grad_mixed))
+    own_down = to_owner(after(sum_down, grad_mixed))
     grad_projected = attend_back(
         qkv,
         grad_mixed.reshape(seqs * total, few),
@@ -942,35 +944,38 @@
         block,
         scale,
     )
-    first_partial = matmul_t(grad_projected, attn_full[:, : 3 * few]).astype(bf).reshape(
-        seqs, pieces, cap, width
-    )
+    grad_turned = after(grad_projected, own_gate, own_down, grad_pair, cross_sum)
+    grad_qkv = contract_rows(merged(input1), grad_turned).astype(bf)
+    grad_attn = jnp.concatenate([grad_qkv, grad_output, grad_pair], axis=1)
+    attn_sum = lax.psum_scatter(grad_attn, "shard", scatter_dimension=0, tiled=True)
+    first_partial = matmul_t(after(grad_turned, grad_attn, sum_up), attn_full[:, : 3 * few]).astype(
+        bf
+    ).reshape(seqs, pieces, cap, width)
     first_parts = add_cores(first_partial[0], first_partial[1])
-    grad_qkv = contract_rows(merged(input1), grad_projected).astype(bf)
-    grad_pairs = after(grad_pairs, grad_mixed)
-    own_pair_grads = ring_scatter(
-        [at(grad_pairs, index) for index in ctx_after], (grad_projected,), (first_parts[0],)
-    ).astype(bf)
-    grad_pair = contract_rows(cond_rows, own_pair_grads).astype(bf)
-    down_own, down_other = after(down_own, grad_mixed), after(down_other, grad_mixed)
-    down_parts = add_cores(down_own, after(down_other, grad_mixed))
-    down_sum = square_scatter(down_parts, (first_parts[0],), (grad_qkv,))
-    grad_attn = jnp.concatenate([grad_qkv, grad_output, grad_pair], axis=1)
-    attn_sum = square_scatter(
-        [rows_at(grad_attn, index, ctxs * owned) for index in shard_near]
-    ).astype(bf)
-    back1_sum = ring_scatter(first_parts, (grad_qkv,), (cross_sum, attn_sum, down_sum))
-    block_mine = (x_second + down_sum).astype(bf)
-    block_out = natural(block_mine, swap(block_mine))
+    arrived = []
+
+    def exchange(token):
+        arrived.extend(
+            [
+                to_owner(after(sum_up, token)),
+                summed(
+                    ring_exchange(
+                        [rows_at(after(cross_sum, token), index, owned) for index in ctx_after]
+                    )
+                ),
+            ]
+        )
+        return arrived
+
+    back1_sum = ring_scatter(first_parts, (), exchange)
+    own_up = arrived[0]
+    own_cross = arrived[1]
     plain1, inverse1 = norm_parts(x_rows)
     back1, grad_gain1 = norm_back(back1_sum, plain1, inverse1, gains[0])
     tokens_grad_mine = grad_first + back1
     tokens_grad = natural(tokens_grad_mine, swap(tokens_grad_mine))
 
-    own_cross = ring_scatter([rows_at(cross_sum, index, owned) for index in ctx_after])
-    own_kinds = place(
-        ring_exchange([rows_at(attn_sum, index, owned) for index in ctx_after]), ctx_before
-    )
+    own_kinds = lax.all_to_all(attn_sum.reshape(ctxs, owned, -1), "ctx", 0, 0, tiled=True)
     own_kinds = jnp.transpose(
         own_kinds.reshape(ctxs, owned, n_kinds, few), (1, 2, 0, 3)
     ).reshape(owned, n_kinds, local_width).astype(fl)
@@ -979,15 +984,10 @@
     own_pair = own_kinds[:, 4:]
     own_query = own_cross[:, :local_width]
     own_cross_out = own_cross[:, local_width:]
-    own_mlp = jnp.concatenate([sum_gate, sum_up, sum_down], axis=1)
-    own_mlp = place(
-        square_exchange([rows_at(own_mlp, index, owned) for index in shard_near]), shard_near
-    )
-    own_mlp = jnp.transpose(own_mlp.reshape(shards, owned, 3, units), (1, 2, 0, 3)).reshape(
-        owned, 3, units_half
-    )
-    own_gate_up = own_mlp[:, :2].astype(fl)
-    own_down = own_mlp[:, 2].astype(fl)
+    own_gate_up = with_layout_constraint(
+        jnp.stack([own_gate, own_up], axis=1), Layout((0, 1, 2))
+    ).astype(fl)
+    own_down = own_down.astype(fl)
 
     squares = jnp.sum(own_kinds * own_kinds) + jnp.sum(own_cross * own_cross)
     squares = squares + jnp.sum(own_gate_up * own_gate_up) + jnp.sum(own_down * own_down)

time: 1010 us -> 880 us (0.87)
  starting transfers between devices: 169 us -> 91.1 us
  waiting for transfers between devices: 362 us -> 335 us
  local copies, waits for them, and re-layouts: 142 us -> 116 us
    ppermute x34 -> x14, waiting for transfers between devices: 159 us -> 64.7 us  [cross_over(): return lax.ppermute(value, 'shard', [(i, i ^ bits) for i in range(size)])]
    ppermute x37 -> x28, starting transfers between devices: 110 us -> 36.5 us  [ring_shift(): lax.ppermute(value, 'ctx', [(i, (i - by) % size) for i in range(size)])]
    all_to_all x0 -> x6, starting transfers between devices: none -> 27.7 us  [the longest x3 12.2 us: local(): lax.all_to_all(array.reshape(shards, owned, -1), 'shard', 0, 0, tiled=True)]
    ppermute x34 -> x14, starting transfers between devices: 40.9 us -> 17 us  [cross_over(): return lax.ppermute(value, 'shard', [(i, i ^ bits) for i in range(size)])]
    all_to_all x0 -> x6, waiting for transfers between devices: none -> 21.5 us  [the longest x1 19.5 us: local(): lax.all_to_all(attn_sum.reshape(ctxs, owned, -1), 'ctx', 0, 0, tiled=True)]
    all_gather x1, waiting for transfers between devices: 0.02 us -> 21.3 us  [local(): attn_full = lax.all_gather(attn_rows, 'shard', axis=0, tiled=True)]
    dynamic_update_slice x25 -> x8, local copies, waits for them, and re-layouts: 12.8 us -> 0.25 us  [place(): out = lax.dynamic_update_index_in_dim(out, block, index, 0)]
    all_gather x3, waiting for transfers between devices: 0.01 us -> 12.1 us  [local(): over_ctx = lambda array: lax.all_gather(array, 'ctx', axis=0, tiled=False)]
  transfers between devices with their start and end apart: 108 -> 87, of which waited for: 52 -> 40; matrix products, arithmetic and copies ran while one was open for 28% -> 27% of each run, Pallas kernels for 8% -> 10%
where the time goes in v3:
time: 880 us; the launch traced here: 869 us
  waiting for transfers between devices  335 us (38%)
  Pallas kernels  134 us (15%)
  local copies, waits for them, and re-layouts  116 us (13%)
  other arithmetic  105 us (12%)
  starting transfers between devices  91.1 us (10%)
  matrix products  61.8 us (7%)
  between operations  25.3 us (3%)
    ppermute x28, waiting for transfers between devices, ring_shift(): lax.ppermute(value, 'ctx', [(i, (i - by) % size) for i in range(size)])  190 us
    ppermute x14, waiting for transfers between devices, cross_over(): return lax.ppermute(value, 'shard', [(i, i ^ bits) for i in range(size)])  64.7 us
    pallas_call x1, Pallas kernels, mlp(): pl.pallas_call(functools.partial(mlp_kernel, count, given), grid=(count,)...  50.2 us
    dot_general x7, matrix products, contract_rows(): lax.dot_general(left, right, (((0,), (0,)), ((), ())), preferred_element_...  39.5 us
    unnamed x195, local copies, waits for them, and re-layouts  37.4 us
    ppermute x28, starting transfers between devices, ring_shift(): lax.ppermute(value, 'ctx', [(i, (i - by) % size) for i in range(size)])  36.5 us
    pallas_call x1, Pallas kernels, attend_back(): pl.pallas_call(functools.partial(attend_back_kernel, heads, wide, block,...  28.4 us
    all_gather x1, waiting for transfers between devices, local(): attn_full = lax.all_gather(attn_rows, 'shard', axis=0, tiled=True)  21.3 us
  transfers between devices with their start and end apart: 87, of which 40 were waited for; matrix products, arithmetic and copies ran while one was open for 27% of the time, Pallas kernels for 10%

profile of v3, /device:TPU:0, one launch (start us, length us, event | category | flops | bytes accessed | tf_op | source)
XLA Modules:
  0.0 868.9 jit_solution(8213324364459884185)
XLA Ops:
  56.1 14.1 %collective-permute-done.refs_1_ = bf16[264,1536]{1,0:T(8,128)(2,1)S(1)} collective-permute-done((bf16[264,1536]{1,0:T(8,128)(2,1)S(1)}, bf16[264,1536]{1,0:T(8,128)(2,1)S(1)}, u32[]{:S(2)}, u32[]{:S(2)}) %collective-permute-start) | collective-permute-done | bytes 811040 | tf_op jit(solution)/shard_map/ppermute | solution.py:527
  70.1 16.6 %collective-permute-done.1.refs_3_ = bf16[264,1536]{1,0:T(8,128)(2,1)S(1)} collective-permute-done((bf16[264,1536]{1,0:T(8,128)(2,1)S(1)}, bf16[264,1536]{1,0:T(8,128)(2,1)S(1)}, u32[]{:S(2)}, u32[]{:S(2)}) %collective-permute-start.1) | collective-permute-done | bytes 811040 | tf_op jit(solution)/shard_map/ppermute | solution.py:527
  95.2 21.3 %all-gather.9.cloned.1.call-done.refs_9_ = bf16[1536,1280]{1,0:T(8,128)(2,1)} async-done(((bf16[384,1280]{1,0:T(8,128)(2,1)}), bf16[1536,1280]{1,0:T(8,128)(2,1)}) %all-gather.9.cloned.1.call-update) | async-done | bytes 3932176 | tf_op jit(solution)/shard_map/all_gather | solution.py:769
  129.1 14.6 %project.1 = (bf16[8,264,1536]{2,1,0:T(8,128)(2,1)}, bf16[8,264,576]{2,1,0:T(8,128)(2,1)}) custom-call(bf16[264,1536]{1,0:T(8,128)(2,1)S(1)} %get-tuple-element.369.refs_0_, bf16[264,1536]{1,0:T(8,128)(2,1)S(1)} %collective-permute-done.refs_1_, bf16[264,1536]{1,0:T(8,128)(2,1)} %constant_dynamic-update-slice_fusion.refs_2_, ...), custom_call_target="tpu_custom_call" | custom-call | flops 1000 | bytes 1000 | tf_op jit(solution)/shard_map/project/pallas_call | solution.py:124
  150.3 15.2 %attend.1 = (bf16[2112,192]{1,0:T(8,128)(2,1)S(1)}, f32[2,16,352]{2,1,0:T(8,128)S(1)}) custom-call(bf16[2112,576]{1,0:T(8,128)(2,1)S(1)} %bitcast.234, f32[2112,128]{1,0:T(8,128)S(1)} %broadcast_in_dim.101.mask_ref), custom_call_target="tpu_custom_call" | custom-call | flops 1000 | bytes 1000 | tf_op jit(solution)/shard_map/attend/pallas_call | solution.py:172
  166.2 27.7 %collective-permute-done.11 = bf16[96,1536]{1,0:T(8,128)(2,1)S(1)} collective-permute-done((bf16[96,1536]{1,0:T(8,128)(2,1)S(1)}, bf16[96,1536]{1,0:T(8,128)(2,1)S(1)}, u32[]{:S(2)}, u32[]{:S(2)}) %collective-permute-start.11) | collective-permute-done | bytes 294944 | tf_op jit(solution)/shard_map/ppermute | solution.py:527
  234.7 11.9 %collective-permute-done.16 = bf16[288,384]{1,0:T(8,128)(2,1)S(1)} collective-permute-done((bf16[288,384]{1,0:T(8,128)(2,1)S(1)}, bf16[288,384]{1,0:T(8,128)(2,1)S(1)}, u32[]{:S(2)}, u32[]{:S(2)}) %collective-permute-start.16) | collective-permute-done | bytes 221216 | tf_op jit(solution)/shard_map/ppermute | solution.py:527
  258.5 19.4 %collective-permute-done.13 = bf16[264,1536]{1,0:T(8,128)(2,1)} collective-permute-done((bf16[264,1536]{1,0:T(8,128)(2,1)}, bf16[264,1536]{1,0:T(8,128)(2,1)}, u32[]{:S(2)}, u32[]{:S(2)}) %collective-permute-start.13) | collective-permute-done | bytes 811040 | tf_op jit(solution)/shard_map/ppermute | solution.py:527
  310.9 10.9 %collective-permute-done.27.refs_13_ = bf16[264,1536]{1,0:T(8,128)(2,1)} collective-permute-done((bf16[264,1536]{1,0:T(8,128)(2,1)}, bf16[264,1536]{1,0:T(8,128)(2,1)}, u32[]{:S(2)}, u32[]{:S(2)}) %collective-permute-start.27) | collective-permute-done | bytes 811040 | tf_op jit(solution)/shard_map/ppermute | solution.py:532
  321.9 18.9 %collective-permute-done.29.refs_14_ = bf16[264,1536]{1,0:T(8,128)(2,1)} collective-permute-done((bf16[264,1536]{1,0:T(8,128)(2,1)}, bf16[264,1536]{1,0:T(8,128)(2,1)}, u32[]{:S(2)}, u32[]{:S(2)}) %collective-permute-start.29) | collective-permute-done | bytes 811040 | tf_op jit(solution)/shard_map/ppermute | solution.py:532
  341.3 14.9 %collective-permute-done.21.refs_5_ = bf16[264,1536]{1,0:T(8,128)(2,1)} collective-permute-done((bf16[264,1536]{1,0:T(8,128)(2,1)}, bf16[264,1536]{1,0:T(8,128)(2,1)}, u32[]{:S(2)}, u32[]{:S(2)}) %collective-permute-start.21) | collective-permute-done | bytes 811040 | tf_op jit(solution)/shard_map/ppermute | solution.py:532
  371.9 12.1 %all-gather.17.cloned.1.call-done = bf16[16,96,768]{2,1,0:T(8,128)(2,1)} async-done(((bf16[4,96,768]{2,1,0:T(8,128)(2,1)}), bf16[16,96,768]{2,1,0:T(8,128)(2,1)}) %all-gather.17.cloned.1.call-update) | async-done | bytes 2359312 | tf_op jit(solution)/shard_map/all_gather | solution.py:779
  384.0 50.2 %mlp.1 = (bf16[8,264,1536]{2,1,0:T(8,128)(2,1)}, bf16[8,264,1536]{2,1,0:T(8,128)(2,1)}, bf16[8,264,768]{2,1,0:T(8,128)(2,1)}, bf16[8,264,1536]{2,1,0:T(8,128)(2,...) custom-call(bf16[264,1536]{1,0:T(8,128)(2,1)} %collective-permute-do, ...), custom_call_target="tpu_custom_call" | custom-call | flops 1000 | bytes 1000 | tf_op jit(solution)/shard_map/mlp/pallas_call | solution.py:485
  434.3 8.9 %bitcast_convert_fusion = bf16[1536,768]{1,0:T(8,128)(2,1)S(1)} fusion(bf16[8,264,1536]{2,1,0:T(8,128)(2,1)} %get-tuple-element.127, bf16[8,264,768]{2,1,0:T(8,128)(2,1)} %get-tuple-element.128), kind=kOutput, calls=%fused_computation.5 | convolution fusion | flops 4984012800 | bytes 12091392 | tf_op jit(solution)/shard_map/dot_general | solution.py:52
  450.9 9.0 %convolution_convert_fusion.4 = bf16[1536,768]{1,0:T(8,128)(2,1)S(1)} fusion(bf16[2112,1536]{1,0:T(8,128)(2,1)} %bitcast.278, bf16[2112,1536]{1,0:T(8,128)(2,1)} %bitcast.282), kind=kOutput, calls=%fused_computation.10 | convolution fusion | flops 4984012800 | bytes 12091392 | tf_op jit(solution)/shard_map/dot_general | solution.py:52
  494.4 9.5 %cross_back.1 = (bf16[2,264,768]{2,1,0:T(8,128)(2,1)S(1)}, bf16[2,144,1536]{2,1,0:T(8,128)(2,1)S(1)}) custom-call(bf16[2,264,768]{2,1,0:T(8,128)(2,1)S(1)} %bitcast.236, bf16[2,144,1536]{2,1,0:T(8,128)(2,1)S(1)} %reshape.446.kv_ref, bf16[2,264,768]{2,1,0:T(8,128)(2,1)S(1)} %bitcast.239, bf16[2,264,768]{2,1,0:T(8,128)(2,1)S(1)} %get-tuple-element.116.o_ref, ...), custom_call_target="tpu_custom_call" | custom-call | flops 1000 | bytes 1000 | tf_op jit(solution)/shard_map/cross_back/pallas_call | solution.py:343
  548.6 9.0 %collective-permute-done.46.refs_1_ = bf16[264,1536]{1,0:T(8,128)(2,1)S(1)} collective-permute-done((bf16[264,1536]{1,0:T(8,128)(2,1)S(1)}, bf16[264,1536]{1,0:T(8,128)(2,1)S(1)}, u32[]{:S(2)}, u32[]{:S(2)}) %collective-permute-start.46) | collective-permute-done | bytes 811040 | tf_op jit(solution)/shard_map/ppermute | solution.py:527
  557.6 19.5 %collective-permute-done.47.refs_3_ = bf16[264,1536]{1,0:T(8,128)(2,1)S(1)} collective-permute-done((bf16[264,1536]{1,0:T(8,128)(2,1)S(1)}, bf16[264,1536]{1,0:T(8,128)(2,1)S(1)}, u32[]{:S(2)}, u32[]{:S(2)}) %collective-permute-start.47) | collective-permute-done | bytes 811040 | tf_op jit(solution)/shard_map/ppermute | solution.py:527
  585.1 13.0 %collective-permute-done.48 = bf16[264,768]{1,0:T(8,128)(2,1)} collective-permute-done((bf16[264,768]{1,0:T(8,128)(2,1)}, bf16[264,768]{1,0:T(8,128)(2,1)}, u32[]{:S(2)}, u32[]{:S(2)}) %collective-permute-start.48) | collective-permute-done | bytes 405536 | tf_op jit(solution)/shard_map/ppermute | solution.py:527
  608.8 10.4 %mix_back.1 = (bf16[8,264,192]{2,1,0:T(8,128)(2,1)}, bf16[1536,192]{1,0:T(8,128)(2,1)S(1)}) custom-call(bf16[264,1536]{1,0:T(8,128)(2,1)S(1)} %get-tuple-element.370.refs_0_, bf16[264,1536]{1,0:T(8,128)(2,1)S(1)} %collective-permute-done.46.refs_1_, bf16[264,1536]{1,0:T(8,128)(2,1)} %constant_dynamic-update-slice_fusion.4.refs_2_, ...), custom_call_target="tpu_custom_call" | custom-call | flops 1000 | bytes 1000 | tf_op jit(solution)/shard_map/mix_back/pallas_call | solution.py:389
  627.9 28.4 %attend_back.1 = bf16[2112,576]{1,0:T(8,128)(2,1)} custom-call(bf16[2112,576]{1,0:T(8,128)(2,1)} %bitcast.233, bf16[2112,192]{1,0:T(8,128)(2,1)} %bitcast.270, bf16[2112,192]{1,0:T(8,128)(2,1)} %copy-done, f32[2,16,352]{2,1,0:T(8,128)} %copy-done.6, f32[2112,128]{1,0:T(8,128)} %copy-done.2, f32[2112,128]{1,0:T(8,128)} %get-tuple-element.97.cos_ref, ...), custom_call_target="tpu_custom_call" | custom-call | flops 1000 | bytes 1000 | tf_op jit(solution)/shard_map/attend_back/pallas_call | solution.py:241
  761.6 18.7 %collective-permute-done.60 = bf16[264,1536]{1,0:T(8,128)(2,1)} collective-permute-done((bf16[264,1536]{1,0:T(8,128)(2,1)}, bf16[264,1536]{1,0:T(8,128)(2,1)}, u32[]{:S(2)}, u32[]{:S(2)}) %collective-permute-start.60) | collective-permute-done | bytes 811040 | tf_op jit(solution)/shard_map/ppermute | solution.py:527
  784.3 19.5 %all-to-all-done.3 = bf16[4,96,1152]{2,1,0:T(8,128)(2,1)S(1)} async-done(((bf16[4,96,1152]{2,1,0:T(8,128)(2,1)}), bf16[4,96,1152]{2,1,0:T(8,128)(2,1)S(1)}, u32[]{:S(2)}, u32[]{:S(2)}) %all-to-all-start.3) | async-done | bytes 884768 | tf_op jit(solution)/shard_map/all_to_all | solution.py:978
  848.1 10.1 %multiply_subtract_fusion = (f32[96,2,3072]{2,1,0:T(2,128)}, f32[96,2,3072]{2,1,0:T(2,128)}, f32[96,2,3072]{2,1,0:T(2,128)}) fusion(f32[96,2,3072]{2,1,0:T(2,128)S(1)} %copy-done.13, f32[]{:T(128)S(6)} %div.161, bf16[96,2,3072]{2,1,0:T(2,128)(2,1)S(1)} %copy-done.17, f32[96,2,3072]{2,1,0:T(2,128)S(1)} %copy-done.39, f32[96,2,3072]{2,1,0:T(2,128)S(1)} %copy-done.40), kind=kLoop, calls=%fused_computation.29 | loop fusion | flops 10027008 | bytes 15335428 | tf_op jit(solution)/shard_map/sub | solution.py:648
  (562 shorter events, 440.0 us)
Async XLA Ops:
  23.8 92.7 %all-gather.9.cloned.1.call-start = ((), (), s32[]{:S(2)}) async-start(), calls=%async_computation.11 | async-start | bytes 4915200 | tf_op jit(solution)/shard_map/all_gather | solution.py:769
  56.0 137.9 %all-gather.13.cloned.1.call-start = ((), (), s32[]{:S(2)}) async-start(), calls=%async_computation.16 | async-start | bytes 2949120 | tf_op jit(solution)/shard_map/all_gather | solution.py:779
  116.5 168.3 %all-gather.11.cloned.1.call-start = ((), (), s32[]{:S(2)}) async-start(), calls=%async_computation.12 | async-start | bytes 5898240 | tf_op jit(solution)/shard_map/all_gather | solution.py:802
  147.0 46.8 %collective-permute-start.11 = (bf16[96,1536]{1,0:T(8,128)(2,1)S(1)}, bf16[96,1536]{1,0:T(8,128)(2,1)S(1)}, u32[]{:S(2)}, u32[]{:S(2)}) collective-permute-start(bf16[96,1536]{1,0:T(8,128)(2,1)S(1)} %pad_maximum_fusion.19), channel_id=1, source_target_pairs={{0,4},{2,6},{4,0},{6,2},{1,5},{3,7},{5,1},{7,3},{8,12},{10,14},{12... | collective-permute-start | bytes 884744 | tf_op jit(solution)/shard_map/ppermute | solution.py:527
  147.0 46.8 %collective-permute-start.12 = (bf16[96,1536]{1,0:T(8,128)(2,1)S(1)}, bf16[96,1536]{1,0:T(8,128)(2,1)S(1)}, u32[]{:S(2)}, u32[]{:S(2)}) collective-permute-start(bf16[96,1536]{1,0:T(8,128)(2,1)S(1)} %pad_maximum_fusion.19), channel_id=1, source_target_pairs={{0,2},{2,4},{4,6},{6,0},{1,3},{3,5},{5,7},{7,1},{8,10},{10,12},{12... | collective-permute-start | bytes 884744 | tf_op jit(solution)/shard_map/ppermute | solution.py:527
  195.0 177.0 %all-gather.15.cloned.1.call-start = ((), (), s32[]{:S(2)}) async-start(), calls=%async_computation.17 | async-start | bytes 2949120 | tf_op jit(solution)/shard_map/all_gather | solution.py:779
  231.6 46.3 %collective-permute-start.13 = (bf16[264,1536]{1,0:T(8,128)(2,1)}, bf16[264,1536]{1,0:T(8,128)(2,1)}, u32[]{:S(2)}, u32[]{:S(2)}) collective-permute-start(bf16[264,1536]{1,0:T(8,128)(2,1)} %pad_maximum_fusion.13), channel_id=1, source_target_pairs={{0,2},{2,4},{4,6},{6,0},{1,3},{3,5},{5,7},{7,1},{8,10},{10,12},{12... | collective-permute-start | bytes 2433032 | tf_op jit(solution)/shard_map/ppermute | solution.py:527
  281.2 102.8 %all-gather.17.cloned.1.call-start = ((), (), s32[]{:S(2)}) async-start(), calls=%async_computation.18 | async-start | bytes 2949120 | tf_op jit(solution)/shard_map/all_gather | solution.py:779
  302.1 38.6 %collective-permute-start.29 = (bf16[264,1536]{1,0:T(8,128)(2,1)}, bf16[264,1536]{1,0:T(8,128)(2,1)}, u32[]{:S(2)}, u32[]{:S(2)}) collective-permute-start(bf16[264,1536]{1,0:T(8,128)(2,1)} %get-tuple-element.119.refs_12_), channel_id=1, source_target_pairs={{0,16},{8,24},{16,0},{24,8},{1,17},{9,25},{17,1},{25,9},{2,18},{10... | collective-permute-start | bytes 2433032 | tf_op jit(solution)/shard_map/ppermute | solution.py:532
  304.2 244.4 %reduce-scatter.10.cloned.1.call-start = ((), (), s32[]{:S(2)}) async-start(), calls=%async_computation.13 | async-start | bytes 2949120 | tf_op jit(solution)/shard_map/reduce_scatter | solution.py:868
  308.0 48.1 %collective-permute-start.21 = (bf16[264,1536]{1,0:T(8,128)(2,1)}, bf16[264,1536]{1,0:T(8,128)(2,1)}, u32[]{:S(2)}, u32[]{:S(2)}) collective-permute-start(bf16[264,1536]{1,0:T(8,128)(2,1)} %multiply_convert_fusion.refs_4_), channel_id=1, source_target_pairs={{0,8},{8,0},{16,24},{24,16},{1,9},{9,1},{17,25},{25,17},{2,10},{10... | collective-permute-start | bytes 2433032 | tf_op jit(solution)/shard_map/ppermute | solution.py:532
  309.5 47.8 %collective-permute-start.22 = (bf16[264,1536]{1,0:T(8,128)(2,1)}, bf16[264,1536]{1,0:T(8,128)(2,1)}, u32[]{:S(2)}, u32[]{:S(2)}) collective-permute-start(bf16[264,1536]{1,0:T(8,128)(2,1)} %multiply_convert_fusion.refs_4_), channel_id=1, source_target_pairs={{0,16},{8,24},{16,0},{24,8},{1,17},{9,25},{17,1},{25,9},{2,18},{10... | collective-permute-start | bytes 2433032 | tf_op jit(solution)/shard_map/ppermute | solution.py:532
  321.9 39.6 %collective-permute-start.28 = (bf16[264,1536]{1,0:T(8,128)(2,1)}, bf16[264,1536]{1,0:T(8,128)(2,1)}, u32[]{:S(2)}, u32[]{:S(2)}) collective-permute-start(bf16[264,1536]{1,0:T(8,128)(2,1)} %collective-permute-done.27.refs_13_), channel_id=1, source_target_pairs={{0,1},{1,0},{2,3},{3,2},{4,5},{5,4},{6,7},{7,6},{8,9},{9,8},{10,11... | collective-permute-start | bytes 2433032 | tf_op jit(solution)/shard_map/ppermute | solution.py:522
  444.8 140.3 %reduce-scatter.12.cloned.1.call-start = ((), (), s32[]{:S(2)}) async-start(), calls=%async_computation.14 | async-start | bytes 2949120 | tf_op jit(solution)/shard_map/reduce_scatter | solution.py:868
  474.3 187.7 %reduce-scatter.16.cloned.1.call-start = ((), (), s32[]{:S(2)}) async-start(), calls=%async_computation.19 | async-start | bytes 5898240
  523.6 156.6 %reduce-scatter.14.cloned.1.call-start = ((), (), s32[]{:S(2)}) async-start(), calls=%async_computation.15 | async-start | bytes 2949120 | tf_op jit(solution)/shard_map/reduce_scatter | solution.py:868
  524.9 52.2 %collective-permute-start.47 = (bf16[264,1536]{1,0:T(8,128)(2,1)S(1)}, bf16[264,1536]{1,0:T(8,128)(2,1)S(1)}, u32[]{:S(2)}, u32[]{:S(2)}) collective-permute-start(bf16[264,1536]{1,0:T(8,128)(2,1)S(1)} %get-tuple-element.370.refs_0_), channel_id=1, source_target_pairs={{0,2},{2,4},{4,6},{6,0},{1,3},{3,5},{5,7},{7,1},{8,10},{10,12},{12... | collective-permute-start | bytes 2433032 | tf_op jit(solution)/shard_map/ppermute | solution.py:527
  534.1 46.6 %collective-permute-start.40 = (bf16[264,1536]{1,0:T(8,128)(2,1)}, bf16[264,1536]{1,0:T(8,128)(2,1)}, u32[]{:S(2)}, u32[]{:S(2)}) collective-permute-start(bf16[264,1536]{1,0:T(8,128)(2,1)} %get-tuple-element.385), channel_id=1, source_target_pairs={{0,8},{8,0},{16,24},{24,16},{1,9},{9,1},{17,25},{25,17},{2,10},{10... | collective-permute-start | bytes 2433032 | tf_op jit(solution)/shard_map/ppermute | solution.py:532
  534.7 46.0 %collective-permute-start.43 = (bf16[264,1536]{1,0:T(8,128)(2,1)}, bf16[264,1536]{1,0:T(8,128)(2,1)}, u32[]{:S(2)}, u32[]{:S(2)}) collective-permute-start(bf16[264,1536]{1,0:T(8,128)(2,1)} %get-tuple-element.387), channel_id=1, source_target_pairs={{0,16},{8,24},{16,0},{24,8},{1,17},{9,25},{17,1},{25,9},{2,18},{10... | collective-permute-start | bytes 2433032 | tf_op jit(solution)/shard_map/ppermute | solution.py:532
  535.5 45.2 %collective-permute-start.44 = (bf16[264,1536]{1,0:T(8,128)(2,1)}, bf16[264,1536]{1,0:T(8,128)(2,1)}, u32[]{:S(2)}, u32[]{:S(2)}) collective-permute-start(bf16[264,1536]{1,0:T(8,128)(2,1)} %get-tuple-element.386), channel_id=1, source_target_pairs={{0,24},{8,16},{16,8},{24,0},{1,25},{9,17},{17,9},{25,1},{2,26},{10... | collective-permute-start | bytes 2433032 | tf_op jit(solution)/shard_map/ppermute | solution.py:532
  627.9 113.9 %reduce-scatter.18.cloned.1.call-start = ((), (), s32[]{:S(2)}) async-start(), calls=%async_computation.20 | async-start | bytes 4423680 | tf_op jit(solution)/shard_map/reduce_scatter | solution.py:950
  735.2 45.1 %collective-permute-start.60 = (bf16[264,1536]{1,0:T(8,128)(2,1)}, bf16[264,1536]{1,0:T(8,128)(2,1)}, u32[]{:S(2)}, u32[]{:S(2)}) collective-permute-start(bf16[264,1536]{1,0:T(8,128)(2,1)} %pad_maximum_fusion.17), channel_id=1, source_target_pairs={{0,2},{2,4},{4,6},{6,0},{1,3},{3,5},{5,7},{7,1},{8,10},{10,12},{12... | collective-permute-start | bytes 2433032 | tf_op jit(solution)/shard_map/ppermute | solution.py:527
  740.4 71.9 %collective-permute-start.45 = (bf16[264,1536]{1,0:T(8,128)(2,1)}, bf16[264,1536]{1,0:T(8,128)(2,1)}, u32[]{:S(2)}, u32[]{:S(2)}) collective-permute-start(bf16[264,1536]{1,0:T(8,128)(2,1)} %fusion.29), channel_id=1, source_target_pairs={{0,1},{1,0},{2,3},{3,2},{4,5},{5,4},{6,7},{7,6},{8,9},{9,8},{10,11... | collective-permute-start | bytes 2433032 | tf_op jit(solution)/shard_map/ppermute | solution.py:522
  741.8 61.9 %all-to-all-start.3 = ((bf16[4,96,1152]{2,1,0:T(8,128)(2,1)}), bf16[4,96,1152]{2,1,0:T(8,128)(2,1)S(1)}, u32[]{:S(2)}, u32[]{:S(2)}) async-start(bf16[4,96,1152]{2,1,0:T(8,128)(2,1)} %bitcast.271), calls=%async_computation.6 | async-start | bytes 1769472 | tf_op jit(solution)/shard_map/all_to_all | solution.py:978
  (155 other events, 1785.4 us)
Sparse Core Ops, SparseCore 0:
  48.4 68.0 all-gather.8
  118.6 73.5 all-gather.12
  195.1 55.1 all-gather.10
  281.4 51.2 all-gather.14
  334.7 49.2 all-gather.16
  444.9 46.9 reduce-scatter.9
  494.8 60.5 reduce-scatter.11
  558.3 67.1 reduce-scatter.15
  628.4 50.2 reduce-scatter.13
  681.7 55.4 reduce-scatter.17

commit v4 on v3

--- a/solution.py
+++ b/solution.py
@@ -81,12 +81,27 @@
     )
 
 
-def pick(step, refs, held):
-    for k, ref in enumerate(refs):
+def stream(step, refs, held, sems):
+    count = len(refs)
+    copy = lambda k: pltpu.make_async_copy(refs[k], held.at[k % 2], sems.at[k % 2])
+
+    @pl.when(step == 0)
+    def _():
+        copy(0).start()
+
+    for k in range(1, count):
+
+        @pl.when(step == k - 1)
+        def _(k=k):
+            copy(k).start()
+
+    for k in range(count):
 
         @pl.when(step == k)
-        def _(ref=ref):
-            held[...] = ref[...]
+        def _(k=k):
+            copy(k).wait()
+
+    return held[lax.rem(step, 2)]
 
 
 def one_buffer(shape):
@@ -101,9 +116,8 @@
 
 def project_kernel(count, few, scale, *refs):
     x_refs = refs[:count]
-    gain_ref, w_ref, cos_ref, up_ref, down_ref, a_ref, qkv_ref, held = refs[count:]
-    pick(pl.program_id(0), x_refs, held)
-    plain, _ = norm_parts(held[...].astype(fl))
+    gain_ref, w_ref, cos_ref, up_ref, down_ref, a_ref, qkv_ref, held, sems = refs[count:]
+    plain, _ = norm_parts(stream(pl.program_id(0), x_refs, held, sems).astype(fl))
     rows = (plain * gain_ref[...]).astype(bf)
     a_ref[0] = rows
     projected = matmul(rows, w_ref[:, : 3 * few])
@@ -124,7 +138,7 @@
     return pl.pallas_call(
         functools.partial(project_kernel, count, few, scale),
         grid=(count,),
-        in_specs=[one_buffer((rows, width))] * count
+        in_specs=[pl.BlockSpec(memory_space=pl.ANY)] * count
         + [
             whole((1, width)),
             one_buffer((width, used)),
@@ -137,23 +151,29 @@
             jax.ShapeDtypeStruct((count, rows, width), bf),
             jax.ShapeDtypeStruct((count, rows, 3 * few), bf),
         ],
-        scratch_shapes=[pltpu.VMEM((rows, width), bf)],
+        scratch_shapes=[pltpu.VMEM((2, rows, width), bf), pltpu.SemaphoreType.DMA((2,))],
         compiler_params=params(48),
         cost_estimate=SHORT,
         name="project",
     )(*blocks, gain, weight, *(table.reshape(count, rows, LANES) for table in tables))
 
 
+def marked(rows, mark):
+    lane = lax.broadcasted_iota(jnp.int32, (rows.shape[0], LANES - HD), 1)
+    more = jnp.where(lane == 0, mark, 0.0)
+    return jnp.concatenate([rows.astype(fl), more], axis=1).astype(bf)
+
+
 def attend_kernel(heads, wide, block, qkv_ref, mask_ref, o_ref, lse_ref):
-    mask = mask_ref[:, 0:1] > 0.5
+    bias = jnp.where(mask_ref[:, 0:1] > 0.5, 0.0, masked_score)
     total = qkv_ref.shape[0]
     for h in range(heads):
         low, high = h * HD, (h + 1) * HD
-        keys = qkv_ref[:, wide + low : wide + high]
+        keys = marked(qkv_ref[:, wide + low : wide + high], bias)
         values_t = flip(qkv_ref[:, 2 * wide + low : 2 * wide + high]).astype(bf)
         for b in range(total // block):
-            queries = qkv_ref[b * block : (b + 1) * block, low:high]
-            scores = jnp.where(mask, matmul_t(keys, queries), masked_score)
+            queries = marked(qkv_ref[b * block : (b + 1) * block, low:high], 1.0)
+            scores = matmul_t(keys, queries)
             peak = jnp.max(scores, axis=0, keepdims=True)
             weights = jnp.exp(scores - peak)
             sums = jnp.sum(weights, axis=0, keepdims=True)
@@ -194,13 +214,14 @@
     heads, wide, block, scale, qkv_ref, do_ref, o_ref, lse_ref, mask_ref, cos_ref, up_ref, down_ref,
     out_ref, work_ref,
 ):
-    mask = mask_ref[:, 0:1] > 0.5
+    bias = jnp.where(mask_ref[:, 0:1] > 0.5, 0.0, masked_score)
     total = qkv_ref.shape[0]
     ones = jnp.ones((8, HD), fl)
     for h in range(heads):
         low, high = h * HD, (h + 1) * HD
         keys = qkv_ref[:, wide + low : wide + high]
         keys_t = flip(keys).astype(bf)
+        keys = marked(keys, bias)
         values = qkv_ref[:, 2 * wide + low : 2 * wide + high]
         grad_keys = jnp.zeros((total, HD), fl)
         grad_values = jnp.zeros((total, HD), fl)
@@ -209,7 +230,7 @@
             grads = do_ref[b * block : (b + 1) * block, low:high]
             mixed = o_ref[b * block : (b + 1) * block, low:high]
             spot = h * (total // block) + b
-            scores = jnp.where(mask, matmul_t(keys, queries), masked_score)
+            scores = matmul_t(keys, marked(queries, 1.0))
             probs = jnp.exp(scores - lse_ref[0, spot : spot + 1, :])
             delta = lax.dot_general(
                 ones,
@@ -364,7 +385,7 @@
 
 def mix_back_kernel(count, *refs):
     g_refs = refs[:count]
-    w_ref, o_ref, do_ref, grad_ref, held, total = refs[count:]
+    w_ref, o_ref, do_ref, grad_ref, held, total, sems = refs[count:]
     step = pl.program_id(0)
     few = o_ref.shape[2]
 
@@ -372,8 +393,7 @@
     def _():
         total[...] = jnp.zeros_like(total)
 
-    pick(step, g_refs, held)
-    rows = held[...]
+    rows = stream(step, g_refs, held, sems)
     do_ref[0] = matmul(rows, w_ref[:, :few]).astype(bf)
     total[...] += matmul(flip(o_ref[0]).astype(bf), rows)
 
@@ -389,18 +409,26 @@
     return pl.pallas_call(
         functools.partial(mix_back_kernel, count),
         grid=(count,),
-        in_specs=[one_buffer((rows, width))] * count
+        in_specs=[pl.BlockSpec(memory_space=pl.ANY)] * count
         + [one_buffer(weight.shape), stacked((rows, few))],
         out_specs=[stacked((rows, few)), whole((width, few))],
         out_shape=[
             jax.ShapeDtypeStruct((count, rows, few), bf),
             jax.ShapeDtypeStruct((width, few), bf),
         ],
-        scratch_shapes=[pltpu.VMEM((rows, width), bf), pltpu.VMEM((few, width), fl)],
+        scratch_shapes=[
+            pltpu.VMEM((2, rows, width), bf),
+            pltpu.VMEM((few, width), fl),
+            pltpu.SemaphoreType.DMA((2,)),
+        ],
         compiler_params=params(48),
         cost_estimate=SHORT,
         name="mix_back",
     )(*blocks, weight, mixed)
+
+
+def fetched(shape):
+    return shape[2] % 16 == 0 and shape[3] % LANES == 0
 
 
 def mlp_kernel(count, given, *refs):
@@ -420,26 +448,65 @@
         weight,
         a_held,
         dy_held,
+        weight_sems,
+        block_sems,
     ) = refs[2 * given :]
     step = pl.program_id(0)
     ctxs, shards, owned, units = gate_ref.shape
 
+    def weight_copies():
+        for k, kind in enumerate((gate_ref, up_ref, down_ref)):
+            for c in range(ctxs):
+                for s in range(shards):
+                    row = (s * ctxs + c) * owned
+                    yield pltpu.make_async_copy(
+                        kind.at[c, s],
+                        weight.at[pl.ds(row, owned), pl.ds(k * units, units)],
+                        weight_sems.at[k, c * shards + s],
+                    )
+
+    def block_copies(k):
+        for side, (sources, held) in enumerate(((a_refs, a_held), (dy_refs, dy_held))):
+            source = sources[k] if given == count else sources[0].at[k]
+            yield pltpu.make_async_copy(source, held.at[k % 2], block_sems.at[side, k % 2])
+
     @pl.when(step == 0)
     def _():
-        for s in range(shards):
-            for c in range(ctxs):
-                row = (s * ctxs + c) * owned
-                for k, kind in enumerate((gate_ref, up_ref, down_ref)):
-                    weight[row : row + owned, k * units : (k + 1) * units] = kind[c, s]
-
-    if given == count:
-        pick(step, a_refs, a_held)
-        pick(step, dy_refs, dy_held)
-    else:
-        a_held[...] = a_refs[0][0]
-        dy_held[...] = dy_refs[0][0]
-    rows = a_held[...]
-    grads = dy_held[...]
+        for copy in block_copies(0):
+            copy.start()
+        if fetched(gate_ref.shape):
+            for copy in weight_copies():
+                copy.start()
+
+    for k in range(1, count):
+
+        @pl.when(step == k - 1)
+        def _(k=k):
+            for copy in block_copies(k):
+                copy.start()
+
+    for k in range(count):
+
+        @pl.when(step == k)
+        def _(k=k):
+            for copy in block_copies(k):
+                copy.wait()
+
+    @pl.when(step == 0)
+    def _():
+        if fetched(gate_ref.shape):
+            for copy in weight_copies():
+                copy.wait()
+        else:
+            for s in range(shards):
+                for c in range(ctxs):
+                    row = (s * ctxs + c) * owned
+                    for k, kind in enumerate((gate_ref, up_ref, down_ref)):
+                        weight[row : row + owned, k * units : (k + 1) * units] = kind[c, s]
+
+    slot = lax.rem(step, 2)
+    rows = a_held[slot]
+    grads = dy_held[slot]
     a_ref[0] = rows
     dy_ref[0] = grads
     gate = matmul(rows, weight[:, :units])
@@ -474,18 +541,22 @@
     half = count // 2
     rows, width = blocks[0].shape
     units = weights[0].shape[3]
-    if count <= MOST_BLOCKS:
-        feeds = one_buffer((rows, width))
-    else:
-        feeds = stacked((rows, width))
+    if count > MOST_BLOCKS:
         blocks, grads = [jnp.stack(blocks)], [jnp.stack(grads)]
     given = len(blocks)
+    ctxs, shards = weights[0].shape[:2]
     first = pl.BlockSpec((1, rows, width), lambda i: (jnp.minimum(i, half - 1), 0, 0))
     second = pl.BlockSpec((1, rows, width), lambda i: (jnp.maximum(i - half, 0), 0, 0))
     return pl.pallas_call(
         functools.partial(mlp_kernel, count, given),
         grid=(count,),
-        in_specs=[feeds] * (2 * given) + [one_buffer(weights[0].shape)] * 3,
+        in_specs=[pl.BlockSpec(memory_space=pl.ANY)] * (2 * given)
+        + [
+            pl.BlockSpec(memory_space=pl.ANY)
+            if fetched(weights[0].shape)
+            else one_buffer(weights[0].shape)
+        ]
+        * 3,
         out_specs=[
             stacked((rows, width)),
             stacked((rows, width)),
@@ -505,10 +576,12 @@
         + [jax.ShapeDtypeStruct((half, rows, width), bf)] * 4,
         scratch_shapes=[
             pltpu.VMEM((width, 3 * units), bf),
-            pltpu.VMEM((rows, width), bf),
-            pltpu.VMEM((rows, width), bf),
-        ],
-        compiler_params=params(60),
+            pltpu.VMEM((2, rows, width), bf),
+            pltpu.VMEM((2, rows, width), bf),
+            pltpu.SemaphoreType.DMA((3, ctxs * shards)),
+            pltpu.SemaphoreType.DMA((2, 2)),
+        ],
+        compiler_params=params(48),
         cost_estimate=SHORT,
         name="mlp",
     )(*blocks, *grads, *weights)

time: 880 us -> 875 us (level)
  starting transfers between devices: 91.1 us -> 105 us
  waiting for transfers between devices: 335 us -> 323 us
    all_to_all x1, starting transfers between devices: 4.81 us -> 20.2 us  [local(): lax.all_to_all(attn_sum.reshape(ctxs, owned, -1), 'ctx', 0, 0, tiled=True)]
    ppermute x28, waiting for transfers between devices: 190 us -> 177 us  [ring_shift(): lax.ppermute(value, 'ctx', [(i, (i - by) % size) for i in range(size)])]
    unnamed x195 -> x199, local copies, waits for them, and re-layouts: 37.4 us -> 38 us
  transfers between devices with their start and end apart: 87 -> 87, of which waited for: 40 -> 40; matrix products, arithmetic and copies ran while one was open for 27% -> 27% of each run, Pallas kernels for 10% -> 9%
where the time goes in v4:
time: 875 us; the launch traced here: 864 us
  waiting for transfers between devices  323 us (37%)
  Pallas kernels  127 us (15%)
  local copies, waits for them, and re-layouts  116 us (13%)
  starting transfers between devices  105 us (12%)
  other arithmetic  104 us (12%)
  matrix products  61.9 us (7%)
  between operations  25.4 us (3%)
    ppermute x28, waiting for transfers between devices, ring_shift(): lax.ppermute(value, 'ctx', [(i, (i - by) % size) for i in range(size)])  177 us
    ppermute x14, waiting for transfers between devices, cross_over(): return lax.ppermute(value, 'shard', [(i, i ^ bits) for i in range(size)])  64.4 us
    pallas_call x1, Pallas kernels, mlp(): pl.pallas_call(functools.partial(mlp_kernel, count, given), grid=(count,)...  45.8 us
    dot_general x7, matrix products, contract_rows(): lax.dot_general(left, right, (((0,), (0,)), ((), ())), preferred_element_...  39.5 us
    unnamed x199, local copies, waits for them, and re-layouts  38 us
    ppermute x28, starting transfers between devices, ring_shift(): lax.ppermute(value, 'ctx', [(i, (i - by) % size) for i in range(size)])  36.8 us
    pallas_call x1, Pallas kernels, attend_back(): pl.pallas_call(functools.partial(attend_back_kernel, heads, wide, block,...  28.1 us
    all_gather x1, waiting for transfers between devices, local(): attn_full = lax.all_gather(attn_rows, 'shard', axis=0, tiled=True)  21.3 us
  transfers between devices with their start and end apart: 87, of which 40 were waited for; matrix products, arithmetic and copies ran while one was open for 27% of the time, Pallas kernels for 9%

profile of v4, /device:TPU:0, one launch (start us, length us, event | category | flops | bytes accessed | tf_op | source)
XLA Modules:
  0.0 863.8 jit_solution(17915942475070954368)
XLA Ops:
  56.1 14.1 %collective-permute-done.refs_1_ = bf16[264,1536]{1,0:T(8,128)(2,1)S(1)} collective-permute-done((bf16[264,1536]{1,0:T(8,128)(2,1)S(1)}, bf16[264,1536]{1,0:T(8,128)(2,1)S(1)}, u32[]{:S(2)}, u32[]{:S(2)}) %collective-permute-start) | collective-permute-done | bytes 811040 | tf_op jit(solution)/shard_map/ppermute | solution.py:600
  70.1 16.6 %collective-permute-done.1.refs_3_ = bf16[264,1536]{1,0:T(8,128)(2,1)S(1)} collective-permute-done((bf16[264,1536]{1,0:T(8,128)(2,1)S(1)}, bf16[264,1536]{1,0:T(8,128)(2,1)S(1)}, u32[]{:S(2)}, u32[]{:S(2)}) %collective-permute-start.1) | collective-permute-done | bytes 811040 | tf_op jit(solution)/shard_map/ppermute | solution.py:600
  95.2 21.3 %all-gather.9.cloned.1.call-done.refs_9_ = bf16[1536,1280]{1,0:T(8,128)(2,1)} async-done(((bf16[384,1280]{1,0:T(8,128)(2,1)}), bf16[1536,1280]{1,0:T(8,128)(2,1)}) %all-gather.9.cloned.1.call-update) | async-done | bytes 3932176 | tf_op jit(solution)/shard_map/all_gather | solution.py:842
  129.1 13.6 %project.1 = (bf16[8,264,1536]{2,1,0:T(8,128)(2,1)}, bf16[8,264,576]{2,1,0:T(8,128)(2,1)}) custom-call(bf16[264,1536]{1,0:T(8,128)(2,1)S(1)} %get-tuple-element.369.refs_0_, bf16[264,1536]{1,0:T(8,128)(2,1)S(1)} %collective-permute-done.refs_1_, bf16[264,1536]{1,0:T(8,128)(2,1)} %constant_dynamic-update-slice_fusion.refs_2_, ...), custom_call_target="tpu_custom_call" | custom-call | flops 1000 | bytes 1000 | tf_op jit(solution)/shard_map/project/pallas_call | solution.py:138
  149.4 14.4 %attend.1 = (bf16[2112,192]{1,0:T(8,128)(2,1)S(1)}, f32[2,16,352]{2,1,0:T(8,128)S(1)}) custom-call(bf16[2112,576]{1,0:T(8,128)(2,1)S(1)} %bitcast.234, f32[2112,128]{1,0:T(8,128)S(1)} %broadcast_in_dim.101.mask_ref), custom_call_target="tpu_custom_call" | custom-call | flops 1000 | bytes 1000 | tf_op jit(solution)/shard_map/attend/pallas_call | solution.py:192
  164.9 28.9 %collective-permute-done.11 = bf16[96,1536]{1,0:T(8,128)(2,1)S(1)} collective-permute-done((bf16[96,1536]{1,0:T(8,128)(2,1)S(1)}, bf16[96,1536]{1,0:T(8,128)(2,1)S(1)}, u32[]{:S(2)}, u32[]{:S(2)}) %collective-permute-start.11) | collective-permute-done | bytes 294944 | tf_op jit(solution)/shard_map/ppermute | solution.py:600
  234.5 11.9 %collective-permute-done.16 = bf16[288,384]{1,0:T(8,128)(2,1)S(1)} collective-permute-done((bf16[288,384]{1,0:T(8,128)(2,1)S(1)}, bf16[288,384]{1,0:T(8,128)(2,1)S(1)}, u32[]{:S(2)}, u32[]{:S(2)}) %collective-permute-start.16) | collective-permute-done | bytes 221216 | tf_op jit(solution)/shard_map/ppermute | solution.py:600
  258.4 19.4 %collective-permute-done.13 = bf16[264,1536]{1,0:T(8,128)(2,1)} collective-permute-done((bf16[264,1536]{1,0:T(8,128)(2,1)}, bf16[264,1536]{1,0:T(8,128)(2,1)}, u32[]{:S(2)}, u32[]{:S(2)}) %collective-permute-start.13) | collective-permute-done | bytes 811040 | tf_op jit(solution)/shard_map/ppermute | solution.py:600
  310.1 11.1 %collective-permute-done.27.refs_13_ = bf16[264,1536]{1,0:T(8,128)(2,1)} collective-permute-done((bf16[264,1536]{1,0:T(8,128)(2,1)}, bf16[264,1536]{1,0:T(8,128)(2,1)}, u32[]{:S(2)}, u32[]{:S(2)}) %collective-permute-start.27) | collective-permute-done | bytes 811040 | tf_op jit(solution)/shard_map/ppermute | solution.py:605
  321.2 18.9 %collective-permute-done.29.refs_14_ = bf16[264,1536]{1,0:T(8,128)(2,1)} collective-permute-done((bf16[264,1536]{1,0:T(8,128)(2,1)}, bf16[264,1536]{1,0:T(8,128)(2,1)}, u32[]{:S(2)}, u32[]{:S(2)}) %collective-permute-start.29) | collective-permute-done | bytes 811040 | tf_op jit(solution)/shard_map/ppermute | solution.py:605
  340.6 14.6 %collective-permute-done.21.refs_5_ = bf16[264,1536]{1,0:T(8,128)(2,1)} collective-permute-done((bf16[264,1536]{1,0:T(8,128)(2,1)S(1)}, bf16[264,1536]{1,0:T(8,128)(2,1)}, u32[]{:S(2)}, u32[]{:S(2)}) %collective-permute-start.21) | collective-permute-done | bytes 811040 | tf_op jit(solution)/shard_map/ppermute | solution.py:605
  370.8 13.1 %all-gather.17.cloned.1.call-done = bf16[16,96,768]{2,1,0:T(8,128)(2,1)} async-done(((bf16[4,96,768]{2,1,0:T(8,128)(2,1)}), bf16[16,96,768]{2,1,0:T(8,128)(2,1)}) %all-gather.17.cloned.1.call-update) | async-done | bytes 2359312 | tf_op jit(solution)/shard_map/all_gather | solution.py:852
  384.0 45.8 %mlp.1 = (bf16[8,264,1536]{2,1,0:T(8,128)(2,1)}, bf16[8,264,1536]{2,1,0:T(8,128)(2,1)}, bf16[8,264,768]{2,1,0:T(8,128)(2,1)}, bf16[8,264,1536]{2,1,0:T(8,128)(2,...) custom-call(bf16[264,1536]{1,0:T(8,128)(2,1)} %collective-permute-do, ...), custom_call_target="tpu_custom_call" | custom-call | flops 1000 | bytes 1000 | tf_op jit(solution)/shard_map/mlp/pallas_call | solution.py:550
  429.8 8.9 %bitcast_convert_fusion = bf16[1536,768]{1,0:T(8,128)(2,1)S(1)} fusion(bf16[8,264,1536]{2,1,0:T(8,128)(2,1)} %get-tuple-element.127, bf16[8,264,768]{2,1,0:T(8,128)(2,1)} %get-tuple-element.128), kind=kOutput, calls=%fused_computation.5 | convolution fusion | flops 4984012800 | bytes 12091392 | tf_op jit(solution)/shard_map/dot_general | solution.py:52
  446.5 9.0 %convolution_convert_fusion.4 = bf16[1536,768]{1,0:T(8,128)(2,1)S(1)} fusion(bf16[2112,1536]{1,0:T(8,128)(2,1)} %bitcast.278, bf16[2112,1536]{1,0:T(8,128)(2,1)} %bitcast.282), kind=kOutput, calls=%fused_computation.10 | convolution fusion | flops 4984012800 | bytes 12091392 | tf_op jit(solution)/shard_map/dot_general | solution.py:52
  489.8 9.5 %cross_back.1 = (bf16[2,264,768]{2,1,0:T(8,128)(2,1)S(1)}, bf16[2,144,1536]{2,1,0:T(8,128)(2,1)S(1)}) custom-call(bf16[2,264,768]{2,1,0:T(8,128)(2,1)S(1)} %bitcast.236, bf16[2,144,1536]{2,1,0:T(8,128)(2,1)S(1)} %reshape.446.kv_ref, bf16[2,264,768]{2,1,0:T(8,128)(2,1)S(1)} %bitcast.239, bf16[2,264,768]{2,1,0:T(8,128)(2,1)S(1)} %copy-done.5, ...), custom_call_target="tpu_custom_call" | custom-call | flops 1000 | bytes 1000 | tf_op jit(solution)/shard_map/cross_back/pallas_call | solution.py:364
  544.0 9.2 %collective-permute-done.46.refs_1_ = bf16[264,1536]{1,0:T(8,128)(2,1)S(1)} collective-permute-done((bf16[264,1536]{1,0:T(8,128)(2,1)S(1)}, bf16[264,1536]{1,0:T(8,128)(2,1)S(1)}, u32[]{:S(2)}, u32[]{:S(2)}) %collective-permute-start.46) | collective-permute-done | bytes 811040 | tf_op jit(solution)/shard_map/ppermute | solution.py:600
  553.1 19.5 %collective-permute-done.47.refs_3_ = bf16[264,1536]{1,0:T(8,128)(2,1)S(1)} collective-permute-done((bf16[264,1536]{1,0:T(8,128)(2,1)S(1)}, bf16[264,1536]{1,0:T(8,128)(2,1)S(1)}, u32[]{:S(2)}, u32[]{:S(2)}) %collective-permute-start.47) | collective-permute-done | bytes 811040 | tf_op jit(solution)/shard_map/ppermute | solution.py:600
  580.7 13.0 %collective-permute-done.48 = bf16[264,768]{1,0:T(8,128)(2,1)} collective-permute-done((bf16[264,768]{1,0:T(8,128)(2,1)}, bf16[264,768]{1,0:T(8,128)(2,1)}, u32[]{:S(2)}, u32[]{:S(2)}) %collective-permute-start.48) | collective-permute-done | bytes 405536 | tf_op jit(solution)/shard_map/ppermute | solution.py:600
  604.3 9.9 %mix_back.1 = (bf16[8,264,192]{2,1,0:T(8,128)(2,1)}, bf16[1536,192]{1,0:T(8,128)(2,1)S(1)}) custom-call(bf16[264,1536]{1,0:T(8,128)(2,1)S(1)} %get-tuple-element.370.refs_0_, bf16[264,1536]{1,0:T(8,128)(2,1)S(1)} %collective-permute-done.46.refs_1_, bf16[264,1536]{1,0:T(8,128)(2,1)} %constant_dynamic-update-slice_fusion.4.refs_2_, ...), custom_call_target="tpu_custom_call" | custom-call | flops 1000 | bytes 1000 | tf_op jit(solution)/shard_map/mix_back/pallas_call | solution.py:409
  623.1 28.1 %attend_back.1 = bf16[2112,576]{1,0:T(8,128)(2,1)} custom-call(bf16[2112,576]{1,0:T(8,128)(2,1)} %bitcast.233, bf16[2112,192]{1,0:T(8,128)(2,1)} %bitcast.270, bf16[2112,192]{1,0:T(8,128)(2,1)} %copy-done, f32[2,16,352]{2,1,0:T(8,128)} %copy-done.8, f32[2112,128]{1,0:T(8,128)} %copy-done.2, f32[2112,128]{1,0:T(8,128)} %get-tuple-element.97.cos_ref, ...), custom_call_target="tpu_custom_call" | custom-call | flops 1000 | bytes 1000 | tf_op jit(solution)/shard_map/attend_back/pallas_call | solution.py:262
  736.9 20.2 %all-to-all-start.3 = ((bf16[4,96,1152]{2,1,0:T(8,128)(2,1)}), bf16[4,96,1152]{2,1,0:T(8,128)(2,1)S(1)}, u32[]{:S(2)}, u32[]{:S(2)}) async-start(bf16[4,96,1152]{2,1,0:T(8,128)(2,1)} %bitcast.271), calls=%async_computation.6 | async-start | bytes 1769472 | tf_op jit(solution)/shard_map/all_to_all | solution.py:1051
  779.3 19.4 %all-to-all-done.3 = bf16[4,96,1152]{2,1,0:T(8,128)(2,1)S(1)} async-done(((bf16[4,96,1152]{2,1,0:T(8,128)(2,1)}), bf16[4,96,1152]{2,1,0:T(8,128)(2,1)S(1)}, u32[]{:S(2)}, u32[]{:S(2)}) %all-to-all-start.3) | async-done | bytes 884768 | tf_op jit(solution)/shard_map/all_to_all | solution.py:1051
  843.0 10.1 %multiply_subtract_fusion = (f32[96,2,3072]{2,1,0:T(2,128)}, f32[96,2,3072]{2,1,0:T(2,128)}, f32[96,2,3072]{2,1,0:T(2,128)}) fusion(f32[96,2,3072]{2,1,0:T(2,128)S(1)} %copy-done.15, f32[]{:T(128)S(6)} %div.161, bf16[96,2,3072]{2,1,0:T(2,128)(2,1)S(1)} %copy-done.19, f32[96,2,3072]{2,1,0:T(2,128)S(1)} %copy-done.41, f32[96,2,3072]{2,1,0:T(2,128)S(1)} %copy-done.42), kind=kLoop, calls=%fused_computation.29 | loop fusion | flops 10027008 | bytes 15335428 | tf_op jit(solution)/shard_map/sub | solution.py:721
  (566 shorter events, 437.8 us)
Async XLA Ops:
  23.8 92.7 %all-gather.9.cloned.1.call-start = ((), (), s32[]{:S(2)}) async-start(), calls=%async_computation.11 | async-start | bytes 4915200 | tf_op jit(solution)/shard_map/all_gather | solution.py:842
  56.0 137.9 %all-gather.13.cloned.1.call-start = ((), (), s32[]{:S(2)}) async-start(), calls=%async_computation.16 | async-start | bytes 2949120 | tf_op jit(solution)/shard_map/all_gather | solution.py:852
  116.5 168.2 %all-gather.11.cloned.1.call-start = ((), (), s32[]{:S(2)}) async-start(), calls=%async_computation.12 | async-start | bytes 5898240 | tf_op jit(solution)/shard_map/all_gather | solution.py:875
  146.2 47.6 %collective-permute-start.11 = (bf16[96,1536]{1,0:T(8,128)(2,1)S(1)}, bf16[96,1536]{1,0:T(8,128)(2,1)S(1)}, u32[]{:S(2)}, u32[]{:S(2)}) collective-permute-start(bf16[96,1536]{1,0:T(8,128)(2,1)S(1)} %pad_maximum_fusion.19), channel_id=1, source_target_pairs={{0,4},{2,6},{4,0},{6,2},{1,5},{3,7},{5,1},{7,3},{8,12},{10,14},{12... | collective-permute-start | bytes 884744 | tf_op jit(solution)/shard_map/ppermute | solution.py:600
  146.2 47.6 %collective-permute-start.12 = (bf16[96,1536]{1,0:T(8,128)(2,1)S(1)}, bf16[96,1536]{1,0:T(8,128)(2,1)S(1)}, u32[]{:S(2)}, u32[]{:S(2)}) collective-permute-start(bf16[96,1536]{1,0:T(8,128)(2,1)S(1)} %pad_maximum_fusion.19), channel_id=1, source_target_pairs={{0,2},{2,4},{4,6},{6,0},{1,3},{3,5},{5,7},{7,1},{8,10},{10,12},{12... | collective-permute-start | bytes 884744 | tf_op jit(solution)/shard_map/ppermute | solution.py:600
  194.9 175.9 %all-gather.15.cloned.1.call-start = ((), (), s32[]{:S(2)}) async-start(), calls=%async_computation.17 | async-start | bytes 2949120 | tf_op jit(solution)/shard_map/all_gather | solution.py:852
  231.4 46.3 %collective-permute-start.13 = (bf16[264,1536]{1,0:T(8,128)(2,1)}, bf16[264,1536]{1,0:T(8,128)(2,1)}, u32[]{:S(2)}, u32[]{:S(2)}) collective-permute-start(bf16[264,1536]{1,0:T(8,128)(2,1)} %pad_maximum_fusion.13), channel_id=1, source_target_pairs={{0,2},{2,4},{4,6},{6,0},{1,3},{3,5},{5,7},{7,1},{8,10},{10,12},{12... | collective-permute-start | bytes 2433032 | tf_op jit(solution)/shard_map/ppermute | solution.py:600
  281.1 102.8 %all-gather.17.cloned.1.call-start = ((), (), s32[]{:S(2)}) async-start(), calls=%async_computation.18 | async-start | bytes 2949120 | tf_op jit(solution)/shard_map/all_gather | solution.py:852
  303.5 240.5 %reduce-scatter.10.cloned.1.call-start = ((), (), s32[]{:S(2)}) async-start(), calls=%async_computation.13 | async-start | bytes 2949120 | tf_op jit(solution)/shard_map/reduce_scatter | solution.py:941
  307.2 48.1 %collective-permute-start.21 = (bf16[264,1536]{1,0:T(8,128)(2,1)S(1)}, bf16[264,1536]{1,0:T(8,128)(2,1)}, u32[]{:S(2)}, u32[]{:S(2)}) collective-permute-start(bf16[264,1536]{1,0:T(8,128)(2,1)S(1)} %multiply_convert_fusion.refs_4_), channel_id=1, source_target_pairs={{0,8},{8,0},{16,24},{24,16},{1,9},{9,1},{17,25},{25,17},{2,10},{10... | collective-permute-start | bytes 2433032 | tf_op jit(solution)/shard_map/ppermute | solution.py:605
  308.6 47.7 %collective-permute-start.22 = (bf16[264,1536]{1,0:T(8,128)(2,1)S(1)}, bf16[264,1536]{1,0:T(8,128)(2,1)}, u32[]{:S(2)}, u32[]{:S(2)}) collective-permute-start(bf16[264,1536]{1,0:T(8,128)(2,1)S(1)} %multiply_convert_fusion.refs_4_), channel_id=1, source_target_pairs={{0,16},{8,24},{16,0},{24,8},{1,17},{9,25},{17,1},{25,9},{2,18},{10... | collective-permute-start | bytes 2433032 | tf_op jit(solution)/shard_map/ppermute | solution.py:605
  440.3 140.4 %reduce-scatter.12.cloned.1.call-start = ((), (), s32[]{:S(2)}) async-start(), calls=%async_computation.14 | async-start | bytes 2949120 | tf_op jit(solution)/shard_map/reduce_scatter | solution.py:941
  469.8 187.1 %reduce-scatter.16.cloned.1.call-start = ((), (), s32[]{:S(2)}) async-start(), calls=%async_computation.19 | async-start | bytes 5898240
  519.0 156.2 %reduce-scatter.14.cloned.1.call-start = ((), (), s32[]{:S(2)}) async-start(), calls=%async_computation.15 | async-start | bytes 2949120 | tf_op jit(solution)/shard_map/reduce_scatter | solution.py:941
  520.2 52.4 %collective-permute-start.47 = (bf16[264,1536]{1,0:T(8,128)(2,1)S(1)}, bf16[264,1536]{1,0:T(8,128)(2,1)S(1)}, u32[]{:S(2)}, u32[]{:S(2)}) collective-permute-start(bf16[264,1536]{1,0:T(8,128)(2,1)S(1)} %get-tuple-element.370.refs_0_), channel_id=1, source_target_pairs={{0,2},{2,4},{4,6},{6,0},{1,3},{3,5},{5,7},{7,1},{8,10},{10,12},{12... | collective-permute-start | bytes 2433032 | tf_op jit(solution)/shard_map/ppermute | solution.py:600
  529.5 46.8 %collective-permute-start.40 = (bf16[264,1536]{1,0:T(8,128)(2,1)}, bf16[264,1536]{1,0:T(8,128)(2,1)}, u32[]{:S(2)}, u32[]{:S(2)}) collective-permute-start(bf16[264,1536]{1,0:T(8,128)(2,1)} %get-tuple-element.385), channel_id=1, source_target_pairs={{0,8},{8,0},{16,24},{24,16},{1,9},{9,1},{17,25},{25,17},{2,10},{10... | collective-permute-start | bytes 2433032 | tf_op jit(solution)/shard_map/ppermute | solution.py:605
  530.0 46.3 %collective-permute-start.43 = (bf16[264,1536]{1,0:T(8,128)(2,1)}, bf16[264,1536]{1,0:T(8,128)(2,1)}, u32[]{:S(2)}, u32[]{:S(2)}) collective-permute-start(bf16[264,1536]{1,0:T(8,128)(2,1)} %get-tuple-element.387), channel_id=1, source_target_pairs={{0,16},{8,24},{16,0},{24,8},{1,17},{9,25},{17,1},{25,9},{2,18},{10... | collective-permute-start | bytes 2433032 | tf_op jit(solution)/shard_map/ppermute | solution.py:605
  530.8 45.5 %collective-permute-start.44 = (bf16[264,1536]{1,0:T(8,128)(2,1)}, bf16[264,1536]{1,0:T(8,128)(2,1)}, u32[]{:S(2)}, u32[]{:S(2)}) collective-permute-start(bf16[264,1536]{1,0:T(8,128)(2,1)} %get-tuple-element.386), channel_id=1, source_target_pairs={{0,24},{8,16},{16,8},{24,0},{1,25},{9,17},{17,9},{25,1},{2,26},{10... | collective-permute-start | bytes 2433032 | tf_op jit(solution)/shard_map/ppermute | solution.py:605
  623.1 113.8 %reduce-scatter.18.cloned.1.call-start = ((), (), s32[]{:S(2)}) async-start(), calls=%async_computation.20 | async-start | bytes 4423680 | tf_op jit(solution)/shard_map/reduce_scatter | solution.py:1023
  716.2 41.0 %collective-permute-start.63 = (bf16[96,1536]{1,0:T(8,128)(2,1)}, bf16[96,1536]{1,0:T(8,128)(2,1)}, u32[]{:S(2)}, u32[]{:S(2)}) collective-permute-start(bf16[96,1536]{1,0:T(8,128)(2,1)} %get-tuple-element.402), channel_id=1, source_target_pairs={{0,4},{2,6},{4,0},{6,2},{1,5},{3,7},{5,1},{7,3},{8,12},{10,14},{12... | collective-permute-start | bytes 884744 | tf_op jit(solution)/shard_map/ppermute | solution.py:600
  721.8 47.3 %collective-permute-start.61 = (bf16[264,1536]{1,0:T(8,128)(2,1)}, bf16[264,1536]{1,0:T(8,128)(2,1)}, u32[]{:S(2)}, u32[]{:S(2)}) collective-permute-start(bf16[264,1536]{1,0:T(8,128)(2,1)} %pad_maximum_fusion.18), channel_id=1, source_target_pairs={{0,6},{2,0},{4,2},{6,4},{1,7},{3,1},{5,3},{7,5},{8,14},{10,8},{12,... | collective-permute-start | bytes 2433032 | tf_op jit(solution)/shard_map/ppermute | solution.py:600
  730.1 45.1 %collective-permute-start.60 = (bf16[264,1536]{1,0:T(8,128)(2,1)}, bf16[264,1536]{1,0:T(8,128)(2,1)}, u32[]{:S(2)}, u32[]{:S(2)}) collective-permute-start(bf16[264,1536]{1,0:T(8,128)(2,1)} %pad_maximum_fusion.17), channel_id=1, source_target_pairs={{0,2},{2,4},{4,6},{6,0},{1,3},{3,5},{5,7},{7,1},{8,10},{10,12},{12... | collective-permute-start | bytes 2433032 | tf_op jit(solution)/shard_map/ppermute | solution.py:600
  735.2 71.4 %collective-permute-start.45 = (bf16[264,1536]{1,0:T(8,128)(2,1)}, bf16[264,1536]{1,0:T(8,128)(2,1)}, u32[]{:S(2)}, u32[]{:S(2)}) collective-permute-start(bf16[264,1536]{1,0:T(8,128)(2,1)} %fusion.29), channel_id=1, source_target_pairs={{0,1},{1,0},{2,3},{3,2},{4,5},{5,4},{6,7},{7,6},{8,9},{9,8},{10,11... | collective-permute-start | bytes 2433032 | tf_op jit(solution)/shard_map/ppermute | solution.py:595
  736.9 61.7 %all-to-all-start.3 = ((bf16[4,96,1152]{2,1,0:T(8,128)(2,1)}), bf16[4,96,1152]{2,1,0:T(8,128)(2,1)S(1)}, u32[]{:S(2)}, u32[]{:S(2)}) async-start(bf16[4,96,1152]{2,1,0:T(8,128)(2,1)} %bitcast.271), calls=%async_computation.6 | async-start | bytes 1769472 | tf_op jit(solution)/shard_map/all_to_all | solution.py:1051
  (157 other events, 1807.4 us)
Sparse Core Ops, SparseCore 0:
  48.4 68.0 all-gather.8
  118.6 73.8 all-gather.12
  195.0 55.9 all-gather.10
  281.3 51.2 all-gather.14
  334.6 49.2 all-gather.16
  440.4 46.9 reduce-scatter.9
  490.3 60.7 reduce-scatter.11
  554.1 67.0 reduce-scatter.15
  624.1 49.5 reduce-scatter.13
  676.6 55.9 reduce-scatter.17
